TPU v7x, 256 devices: a whole 4x4x8 slice. The times are simulated.
256 devices in a mesh: seq: 64 (over x, y_lo, z), ch: 4 (over y_hi, core).
Axes of the slice: x: 4, y: 4 (y_hi: 2, y_lo: 2; y = y_hi * 2 + y_lo), z: 8, core: 2. Of those that a mesh axis runs over, the one named last changes fastest.
Arguments:
- latents: bfloat16 [128, 1280, 16, 32], P('seq', 'ch'), may hold values from -16 to 16
- spatial_weight: bfloat16 [3, 3, 1280, 1280], P(None, None, 'ch'), may hold values from -0.078125 to 0.078125
- temporal_weight: bfloat16 [3, 1280, 1280], P(None, 'ch'), may hold values from -0.125 to 0.125
- mix_factor: float32 [1], replicated, may hold values from -1.5 to 1.5
Outputs:
- mixed_out: bfloat16 [128, 1280, 16, 32], P('seq', 'ch')
All inputs are finite; a program needn't handle non-finite values.
Results may differ from a plain program's by a relative error of at most 0.012.
Values may be sent and summed in bfloat16 or wider, within the bound.
No kernel may reach another device: no remote copies, remote signals or barrier semaphores. Data moves between devices by JAX's collectives and lax.ppermute only.
A program may use at most 128 MiB of HBM per device.

v0:
```python
import jax
import jax.numpy as jnp
from jax import lax
from jax.sharding import PartitionSpec as P

CH = 1280
GROUPS = 32


norm_eps = 1e-05


def silu_norm(values, group_mean, group_var):
    return jax.nn.silu((values - group_mean) * lax.rsqrt(group_var + norm_eps))


def spatial_taps(weight_block, padded, height, columns):
    running = None
    for row_tap in range(3):
        for col_tap in range(3):
            shifted = padded[:, :, row_tap : row_tap + height, col_tap : col_tap + columns]
            term = lax.dot_general(
                weight_block[row_tap, col_tap],
                shifted,
                (((0,), (1,)), ((), ())),
                preferred_element_type=jnp.float32,
            )
            running = term if running is None else running + term
    return running


def per_device(latents, spatial_weight, temporal_weight, mix_factor):
    latents_f = latents.astype(jnp.float32)
    frame_count, chan_local, height, columns = latents_f.shape
    pixels = height * columns
    group_size = CH // GROUPS
    local_groups = chan_local // group_size
    grouped = latents_f.reshape(frame_count, local_groups, group_size, pixels)
    group_mean = jnp.mean(grouped, axis=(2, 3), keepdims=True)
    squares = jnp.mean(grouped * grouped, axis=(2, 3), keepdims=True)
    act_spatial = silu_norm(grouped, group_mean, squares - group_mean * group_mean)
    act_spatial = act_spatial.reshape(frame_count, chan_local, height, columns).astype(jnp.bfloat16)
    padded = jnp.pad(act_spatial, ((0, 0), (0, 0), (1, 1), (1, 1)))
    weight_cols = spatial_weight
    spatial = lax.psum_scatter(
        spatial_taps(weight_cols, padded, height, columns), "ch", scatter_dimension=0, tiled=True
    )
    hidden = spatial.reshape(chan_local, frame_count, pixels) + latents_f.transpose(
        1, 0, 2, 3
    ).reshape(chan_local, frame_count, pixels)
    grouped = hidden.reshape(local_groups, group_size, frame_count, pixels)
    group_sums = jnp.sum(grouped, axis=(1, 2, 3))
    square_sums = jnp.sum(grouped * grouped, axis=(1, 2, 3))
    group_sums, square_sums = lax.psum((group_sums, square_sums), "seq")
    entries = group_size * frame_count * pixels * lax.axis_size("seq")
    group_mean = (group_sums / entries).reshape(local_groups, 1, 1, 1)
    group_var = (square_sums / entries).reshape(local_groups, 1, 1, 1) - group_mean * group_mean
    act_temporal = (
        silu_norm(grouped, group_mean, group_var)
        .reshape(chan_local, frame_count, pixels)
        .astype(jnp.bfloat16)
    )
    regrouped = lax.all_to_all(act_temporal, "seq", split_axis=2, concat_axis=1, tiled=True)
    all_frames = regrouped.shape[1]
    slice_px = regrouped.shape[2]
    flattened = regrouped.reshape(chan_local, all_frames * slice_px)
    extended = jnp.pad(flattened, ((0, 0), (slice_px, slice_px)))
    weight_cols = temporal_weight
    running = jnp.zeros((chan_local * lax.axis_size("ch"), all_frames * slice_px), jnp.float32)
    for time_tap in range(3):
        window = extended[:, time_tap * slice_px : time_tap * slice_px + all_frames * slice_px]
        running = running + lax.dot_general(
            weight_cols[time_tap],
            window,
            (((0,), (0,)), ((), ())),
            preferred_element_type=jnp.float32,
        )
    reduced = lax.psum_scatter(running.astype(jnp.bfloat16), "ch", scatter_dimension=0, tiled=True)
    reduced = reduced.reshape(chan_local, all_frames, slice_px)
    branch = lax.all_to_all(reduced, "seq", split_axis=1, concat_axis=2, tiled=True)
    blend_weight = jax.nn.sigmoid(mix_factor[0])
    mixed_out = hidden + (1.0 - blend_weight) * branch.astype(jnp.float32)
    return (
        mixed_out.reshape(chan_local, frame_count, height, columns)
        .transpose(1, 0, 2, 3)
        .astype(jnp.bfloat16)
    )


def solution(mesh):
    placed = (P("seq", "ch", None, None), P(None, None, "ch", None), P(None, "ch", None), P())
    return jax.shard_map(
        per_device,
        mesh=mesh,
        in_specs=placed,
        out_specs=P("seq", "ch", None, None),
        check_vma=False,
    )
```

profile of v0, /device:TPU:1, one launch (start us, length us, event | category | flops | bytes accessed | tf_op | source)
XLA Modules:
  0.0 411.2 jit_solution(8611858980453452202)
XLA Ops:
  6.5 1.4 convert_reduce_fusion
  8.6 1.8 fusion.7
  10.4 3.1 fusion.12
  13.5 3.8 fusion.14
  17.3 3.8 fusion.16
  21.1 3.9 fusion.18
  25.0 3.9 fusion.20
  28.8 3.8 fusion.22
  32.6 3.9 fusion.24
  36.5 3.8 fusion.26
  40.4 15.6 %add_add_fusion = f32[2,16,32,1280]{3,2,1,0:T(8,128)} fusion(f32[2,16,32,1280]{3,2,1,0:T(8,128)S(1)} %fusion.12, f32[2,16,32,1280]{3,2,1,0:T(8,128)} %fusion.14, f32[2,16,32,1280]{3,2,1,0:T(8,128)} %fusion.16, f32[2,16,32,1280]{3,2,1,0:T(8,128)} %fusion.18, f32[2,16,32,1280]{3,2,1,0:T(8,128)} %fusion.20, f32[2,16,32,1280]{3,2,1,0:T(8,128)} %fusion.22, ...), kind=kOutput, calls=%fused_computation | convolution fusion | flops 849346560 | bytes 48660480 | tf_op jit(solution)/shard_map/dot_general | solution.py:22
  56.0 5.9 %copy.39 = f32[1280,1024]{1,0:T(8,128)} copy(f32[1280,1024]{0,1:T(8,128)} %bitcast.109) | data formatting | bytes 10485760
  62.0 67.4 %reduce-scatter.7.cloned.1.call-done = f32[320,1024]{1,0:T(8,128)} async-done(((f32[1280,1024]{1,0:T(8,128)}), f32[320,1024]{1,0:T(8,128)}) %reduce-scatter.7.cloned.1.call-update) | async-done | bytes 1310736
  129.3 2.9 copy.40
  132.3 1.7 fusion.60
  134.1 0.1 reduce_sum.72
  134.3 0.1 reduce_sum.75
  134.4 130.2 %all-reduce.2 = (f32[8]{0:T(128)S(1)}, f32[8]{0:T(128)S(1)}) all-reduce(f32[8]{0:T(128)S(1)} %reduce_sum.75, f32[8]{0:T(128)S(1)} %reduce_sum.72), channel_id=1, replica_groups=mesh['seq'=64,'ch'=4] {'seq'}, use_global_device_ids=true, to_apply=%region_10.11 | all-reduce | flops 16 | bytes 128 | tf_op jit(solution)/shard_map/psum | solution.py:54
  264.9 0.5 copy.21
  265.4 0.5 multiply_convert_fusion
  265.9 1.2 copy.22
  267.1 19.6 %all_to_all.24 = bf16[320,2,512]{0,1,2:T(2,128)(2,1)S(1)} all-to-all(bf16[320,2,512]{0,1,2:T(2,128)(2,1)S(1)} %copy.22), channel_id=1, replica_groups=mesh['seq'=64,'ch'=4] {'seq'}, dimensions={2} | all-to-all | bytes 1310720 | tf_op jit(solution)/shard_map/all_to_all | solution.py:63
  287.0 1.5 fusion.29
  288.5 1.5 fusion.31
  290.0 3.1 fusion
  293.1 4.5 %copy.37 = bf16[1280,1024]{1,0:T(8,128)(2,1)} copy(bf16[1280,1024]{0,1:T(8,128)(2,1)} %fusion) | data formatting | bytes 5242880
  297.6 71.8 %reduce-scatter.9.cloned.1.call-done = bf16[320,1024]{1,0:T(8,128)(2,1)} async-done(((bf16[1280,1024]{1,0:T(8,128)(2,1)}), bf16[320,1024]{1,0:T(8,128)(2,1)}) %reduce-scatter.9.cloned.1.call-update) | async-done | bytes 655376
  369.4 2.2 copy.38
  371.7 10.2 %all-to-all-start.1 = ((bf16[320,128,8]{0,2,1:T(8,128)(2,1)}), bf16[320,128,8]{0,2,1:T(8,128)(2,1)S(1)}, u32[]{:S(2)}, u32[]{:S(2)}) async-start(bf16[320,128,8]{0,2,1:T(8,128)(2,1)} %bitcast.38), calls=%async_computation.1 | async-start | bytes 1572864 | tf_op jit(solution)/shard_map/all_to_all | solution.py:80
  382.6 20.4 %all-to-all-done.1 = bf16[320,128,8]{0,2,1:T(8,128)(2,1)S(1)} async-done(((bf16[320,128,8]{0,2,1:T(8,128)(2,1)}), bf16[320,128,8]{0,2,1:T(8,128)(2,1)S(1)}, u32[]{:S(2)}, u32[]{:S(2)}) %all-to-all-start.1) | async-done | bytes 655392 | tf_op jit(solution)/shard_map/all_to_all | solution.py:80
  403.0 0.1 convert_multiply_fusion.1
  403.2 1.1 fusion.45
  (29 shorter events, 1.5 us)
Async XLA Ops:
  6.5 122.8 %reduce-scatter.7.cloned.1.call-start = ((), (), s32[]{:S(2)}) async-start(), calls=%async_computation.4 | async-start | bytes 6553600
  8.6 4.8 %copy-start = (bf16[3,3,320,1280]{3,2,1,0:T(8,128)(2,1)S(1)}, bf16[3,3,320,1280]{3,2,1,0:T(8,128)(2,1)}, u32[]{:S(2)}) copy-start(bf16[3,3,320,1280]{3,2,1,0:T(8,128)(2,1)} %param.5) | copy-start | bytes 22118404
  61.9 70.4 %copy-start.1 = (bf16[2,320,16,32]{1,3,2,0:T(8,128)(2,1)S(1)}, bf16[2,320,16,32]{1,3,2,0:T(8,128)(2,1)}, u32[]{:S(2)}) copy-start(bf16[2,320,16,32]{1,3,2,0:T(8,128)(2,1)} %param.4) | copy-start | bytes 1966084
  61.9 307.5 %reduce-scatter.9.cloned.1.call-start = ((), (), s32[]{:S(2)}) async-start(), calls=%async_computation.5 | async-start | bytes 3276800
  267.1 19.8 %copy-start.2 = (bf16[3,320,1280]{2,1,0:T(8,128)(2,1)S(1)}, bf16[3,320,1280]{2,1,0:T(8,128)(2,1)}, u32[]{:S(2)}) copy-start(bf16[3,320,1280]{2,1,0:T(8,128)(2,1)} %param.6) | copy-start | bytes 7372804
  371.7 31.3 %all-to-all-start.1 = ((bf16[320,128,8]{0,2,1:T(8,128)(2,1)}), bf16[320,128,8]{0,2,1:T(8,128)(2,1)S(1)}, u32[]{:S(2)}, u32[]{:S(2)}) async-start(bf16[320,128,8]{0,2,1:T(8,128)(2,1)} %bitcast.38), calls=%async_computation.1 | async-start | bytes 1572864 | tf_op jit(solution)/shard_map/all_to_all | solution.py:80
Sparse Core Ops, SparseCore 0:
  62.0 67.2 reduce-scatter.6
  297.7 71.6 reduce-scatter.8
where the time goes:
time: 413 us; the launch traced here: 411 us
  waiting for transfers between devices  160 us (39%)
  blocking collectives  150 us (36%)
  matrix products  51.7 us (13%)
  local copies, waits for them, and re-layouts  18.5 us (4%)
  between operations  14.3 us (3%)
  starting transfers between devices  10.2 us (2%)
  other arithmetic  7.09 us (2%)
    unnamed x4, waiting for transfers between devices  139 us
    psum x1, blocking collectives, per_device(): group_sums, square_sums = lax.psum((group_sums, square_sums), 'seq')  130 us
    dot_general x9, matrix products, spatial_taps(): lax.dot_general(weight_block[row_tap, col_tap], shifted, (((0,), (1,)), (...  45.6 us
    all_to_all x1, waiting for transfers between devices, per_device(): lax.all_to_all(reduced, 'seq', split_axis=1, concat_axis=2, tiled=True)  20.4 us
    all_to_all x1, blocking collectives, per_device(): lax.all_to_all(act_temporal, 'seq', split_axis=2, concat_axis=1, tiled=True)  19.6 us
    unnamed x10, local copies, waits for them, and re-layouts  15.7 us
    all_to_all x1, starting transfers between devices, per_device(): lax.all_to_all(reduced, 'seq', split_axis=1, concat_axis=2, tiled=True)  10.2 us
  transfers between devices with their start and end apart: 3, of which 3 were waited for; matrix products, arithmetic and copies ran while one was open for 0% of the time, Pallas kernels for 0%

commit v1 on v0

v1 whole, which is shorter than its diff:
```python
import functools

import jax
import jax.numpy as jnp
from jax import lax
from jax.experimental import pallas as pl
from jax.experimental.pallas import tpu as pltpu
from jax.sharding import PartitionSpec as P

CH = 1280
GROUPS = 32
GROUP = CH // GROUPS
ROWS = 16
COLS = 32
PX = ROWS * COLS
LOCAL = CH // 4
LOCAL_GROUPS = LOCAL // GROUP
TAPS = 3
WIDE = TAPS * LOCAL
TILE = 256
EPS = 1e-05

CORE_SWAP = [(0, 1), (1, 0), (2, 3), (3, 2)]
HALF_SWAP = [(0, 2), (2, 0), (1, 3), (3, 1)]
VMEM_LIMIT = 40 * 1024 * 1024
BF16 = jnp.bfloat16
F32 = jnp.float32
HIGHEST = lax.Precision.HIGHEST


def params():
    return pltpu.CompilerParams(vmem_limit_bytes=VMEM_LIMIT)


def silu(v):
    half = 0.5 * v
    return half + half * jnp.tanh(half)


def group_block():
    row = lax.broadcasted_iota(jnp.int32, (LOCAL, LOCAL), 0)
    col = lax.broadcasted_iota(jnp.int32, (LOCAL, LOCAL), 1)
    out = jnp.zeros((LOCAL, LOCAL), F32)
    for g in range(LOCAL_GROUPS):
        lo, hi = g * GROUP, (g + 1) * GROUP
        same = (row >= lo) & (row < hi) & (col >= lo) & (col < hi)
        out = jnp.where(same, 1.0, out)
    return out


def group_to_lane(shift):
    row = lax.broadcasted_iota(jnp.int32, (LOCAL, 128), 0)
    lane = lax.broadcasted_iota(jnp.int32, (LOCAL, 128), 1) - shift
    return jnp.where((row >= lane * GROUP) & (row < (lane + 1) * GROUP), 1.0, 0.0)


def lane_to_group(shift):
    lane = lax.broadcasted_iota(jnp.int32, (128, LOCAL), 0) - shift
    col = lax.broadcasted_iota(jnp.int32, (128, LOCAL), 1)
    return jnp.where((col >= lane * GROUP) & (col < (lane + 1) * GROUP), 1.0, 0.0)


def exact_dot(a, b):
    return jnp.dot(a, b, precision=HIGHEST, preferred_element_type=F32)


def pack(block):
    return jnp.concatenate([block[: PX // 2], block[PX // 2 :]], axis=1)


def unpack(ref):
    return jnp.concatenate([ref[:, :LOCAL], ref[:, LOCAL:]], axis=0)


def split_cores(total_ref, send_ref, own_ref):
    core = lax.axis_index("ch") % 2

    def copy(ref, first):
        ref[:, :LOCAL] = total_ref[:, first : first + LOCAL]
        ref[:, LOCAL:] = total_ref[:, first + 2 * LOCAL : first + 3 * LOCAL]

    @pl.when(core == 0)
    def _():
        copy(own_ref, 0)
        copy(send_ref, LOCAL)

    @pl.when(core == 1)
    def _():
        copy(own_ref, LOCAL)
        copy(send_ref, 0)


def spatial_kernel(lat_ref, weight_ref, send_ref, own_ref, taps_ref, total_ref):
    tile = pl.program_id(0)

    @pl.when(tile == 0)
    def _():
        lat = lat_ref[...].astype(F32)
        sums = jnp.sum(lat, axis=0, keepdims=True)
        squares = jnp.sum(lat * lat, axis=0, keepdims=True)
        both = jnp.concatenate([sums, squares, jnp.zeros((6, LOCAL), F32)], axis=0)
        both = exact_dot(both, group_block()) * (1.0 / (GROUP * PX))
        mean = both[0:1]
        var = both[1:2] - mean * mean
        act = silu((lat - mean) * lax.rsqrt(var + EPS))
        col = lax.broadcasted_iota(jnp.int32, (PX, LOCAL), 0) % COLS
        left = jnp.where(col == 0, 0.0, pltpu.roll(act, 1, 0))
        right = jnp.where(col == COLS - 1, 0.0, pltpu.roll(act, PX - 1, 0))
        taps_ref[:COLS, :] = jnp.zeros((COLS, WIDE), BF16)
        taps_ref[COLS + PX :, :] = jnp.zeros((COLS, WIDE), BF16)
        taps_ref[COLS : COLS + PX, :] = jnp.concatenate([left, act, right], axis=1).astype(BF16)

    total = None
    for row_tap in range(TAPS):
        term = jnp.dot(
            taps_ref[row_tap * COLS : row_tap * COLS + PX, :],
            weight_ref[row_tap],
            preferred_element_type=F32,
        )
        total = term if total is None else total + term
    total_ref[:, pl.ds(pl.multiple_of(tile * TILE, TILE), TILE)] = total.astype(BF16)

    @pl.when(tile == CH // TILE - 1)
    def _():
        split_cores(total_ref, send_ref, own_ref)


def spatial_call(lat, weight, frame):
    shape = jax.ShapeDtypeStruct((PX, 2 * LOCAL), BF16)
    return pl.pallas_call(
        spatial_kernel,
        grid=(CH // TILE,),
        in_specs=[
            pl.BlockSpec((PX, LOCAL), lambda n: (frame, 0)),
            pl.BlockSpec((TAPS, WIDE, TILE), lambda n: (0, 0, n)),
        ],
        out_specs=[pl.BlockSpec((PX, 2 * LOCAL), lambda n: (0, 0))] * 2,
        out_shape=[shape, shape],
        scratch_shapes=[
            pltpu.VMEM((PX + 2 * COLS, WIDE), BF16),
            pltpu.VMEM((PX, CH), BF16),
        ],
        compiler_params=params(),
        cost_estimate=pl.CostEstimate(
            flops=2 * PX * TAPS * WIDE * CH,
            bytes_accessed=2 * TAPS * WIDE * CH,
            transcendentals=PX * LOCAL,
        ),
        name="spatial",
    )(lat, weight)


def temporal_kernel(last, hidden_ref, halo_ref, stats_ref, weight_ref, send_ref, own_ref, taps_ref, total_ref):
    tile = pl.program_id(0)

    @pl.when(tile == 0)
    def _():
        seq, size = lax.axis_index("seq"), lax.axis_size("seq")
        sums = jnp.sum(stats_ref[...], axis=0, keepdims=True) * (1.0 / (GROUP * 2 * PX * size))
        sums = jnp.broadcast_to(sums, (8, 128))
        mean = exact_dot(sums, lane_to_group(0))[0:1]
        var = exact_dot(sums, lane_to_group(LOCAL_GROUPS))[0:1] - mean * mean
        scale = lax.rsqrt(var + EPS)

        def act(values):
            return silu((values - mean) * scale)

        edge = (seq == size - 1) if last else (seq == 0)
        halo = act(unpack(halo_ref).astype(F32)) * jnp.where(edge, 0.0, 1.0)
        first, second = act(hidden_ref[:PX]), act(hidden_ref[PX:])
        frames = [first, second, halo] if last else [halo, first, second]
        taps_ref[...] = jnp.concatenate(frames, axis=1).astype(BF16)

    total = jnp.dot(taps_ref[...], weight_ref[...], preferred_element_type=F32)
    total_ref[:, pl.ds(pl.multiple_of(tile * TILE, TILE), TILE)] = total.astype(BF16)

    @pl.when(tile == CH // TILE - 1)
    def _():
        split_cores(total_ref, send_ref, own_ref)


def temporal_call(hidden, halo, stats, weight, last):
    shape = jax.ShapeDtypeStruct((PX, 2 * LOCAL), BF16)
    return pl.pallas_call(
        functools.partial(temporal_kernel, last),
        grid=(CH // TILE,),
        in_specs=[
            pl.BlockSpec(hidden.shape, lambda n: (0, 0)),
            pl.BlockSpec(halo.shape, lambda n: (0, 0)),
            pl.BlockSpec(stats.shape, lambda n: (0, 0)),
            pl.BlockSpec((WIDE, TILE), lambda n: (0, n)),
        ],
        out_specs=[pl.BlockSpec((PX, 2 * LOCAL), lambda n: (0, 0))] * 2,
        out_shape=[shape, shape],
        scratch_shapes=[
            pltpu.VMEM((PX, WIDE), BF16),
            pltpu.VMEM((PX, CH), BF16),
        ],
        compiler_params=params(),
        cost_estimate=pl.CostEstimate(
            flops=2 * PX * WIDE * CH,
            bytes_accessed=2 * WIDE * CH,
            transcendentals=3 * PX * LOCAL,
        ),
        name="temporal",
    )(hidden, halo, stats, weight)


def chip_sum_kernel(own_ref, got_ref, send_ref, keep_ref):
    half = lax.axis_index("ch") // 2

    def block(first):
        cols = slice(first, first + LOCAL)
        return own_ref[:, cols].astype(F32) + got_ref[:, cols].astype(F32)

    @pl.when(half == 0)
    def _():
        keep_ref[...] = block(0)
        send_ref[...] = pack(block(LOCAL)).astype(BF16)

    @pl.when(half == 1)
    def _():
        keep_ref[...] = block(LOCAL)
        send_ref[...] = pack(block(0)).astype(BF16)


def chip_sum(own, got):
    return pl.pallas_call(
        chip_sum_kernel,
        out_shape=[
            jax.ShapeDtypeStruct((PX // 2, 2 * LOCAL), BF16),
            jax.ShapeDtypeStruct((PX, LOCAL), F32),
        ],
        compiler_params=params(),
        cost_estimate=pl.CostEstimate(flops=PX * 2 * LOCAL, bytes_accessed=8 * PX * LOCAL, transcendentals=0),
        name="chip_sum",
    )(own, got)


def hidden_kernel(lat_ref, keep0, keep1, got0, got1, hidden_ref, first_ref, last_ref, stats_ref):
    sums, squares = 0.0, 0.0
    for frame, (keep, got, edge) in enumerate(((keep0, got0, first_ref), (keep1, got1, last_ref))):
        cells = slice(frame * PX, (frame + 1) * PX)
        hidden = lat_ref[cells].astype(F32) + keep[...] + unpack(got).astype(F32)
        hidden_ref[cells] = hidden
        edge[...] = pack(hidden).astype(BF16)
        sums += jnp.sum(hidden, axis=0, keepdims=True)
        squares += jnp.sum(hidden * hidden, axis=0, keepdims=True)
    row = exact_dot(jnp.broadcast_to(sums, (8, LOCAL)), group_to_lane(0))
    row += exact_dot(jnp.broadcast_to(squares, (8, LOCAL)), group_to_lane(LOCAL_GROUPS))
    stats_ref[...] = jnp.broadcast_to(row[0:1], stats_ref.shape)


def hidden_call(lat, keeps, gots, size):
    edge = jax.ShapeDtypeStruct((PX // 2, 2 * LOCAL), BF16)
    return pl.pallas_call(
        hidden_kernel,
        out_shape=[
            jax.ShapeDtypeStruct((2 * PX, LOCAL), F32),
            edge,
            edge,
            jax.ShapeDtypeStruct((size, 128), F32),
        ],
        compiler_params=params(),
        cost_estimate=pl.CostEstimate(flops=10 * PX * LOCAL, bytes_accessed=20 * PX * LOCAL, transcendentals=0),
        name="hidden",
    )(lat, *keeps, *gots)


def blend_kernel(mix_ref, hidden_ref, keep0, keep1, got0, got1, out_ref):
    mix = jnp.full((1, LOCAL), mix_ref[0], F32)
    weight = 1.0 - jax.nn.sigmoid(mix)
    for frame, (keep, got) in enumerate(((keep0, got0), (keep1, got1))):
        cells = slice(frame * PX, (frame + 1) * PX)
        branch = (keep[...] + unpack(got).astype(F32)).astype(BF16).astype(F32)
        out_ref[cells] = (hidden_ref[cells] + weight * branch).astype(BF16)


def blend_call(mix, hidden, keeps, gots):
    whole = pl.BlockSpec(memory_space=pltpu.VMEM)
    return pl.pallas_call(
        blend_kernel,
        in_specs=[pl.BlockSpec(memory_space=pltpu.SMEM)] + [whole] * 5,
        out_specs=whole,
        out_shape=jax.ShapeDtypeStruct((2 * PX, LOCAL), BF16),
        compiler_params=params(),
        cost_estimate=pl.CostEstimate(flops=6 * PX * LOCAL, bytes_accessed=16 * PX * LOCAL, transcendentals=0),
        name="blend",
    )(mix, hidden, *keeps, *gots)


def reduce_channels(parts):
    keeps, gots = [], []
    for send, own in parts:
        got = lax.ppermute(send, "ch", CORE_SWAP)
        send, keep = chip_sum(own, got)
        keeps.append(keep)
        gots.append(lax.ppermute(send, "ch", HALF_SWAP))
    return keeps, gots


def per_device(latents, spatial_weight, temporal_weight, mix_factor):
    size = lax.axis_size("seq")
    lat = latents.transpose(0, 2, 3, 1).reshape(2 * PX, LOCAL)
    weight_s = spatial_weight.reshape(TAPS, WIDE, CH)
    weight_t = temporal_weight.reshape(WIDE, CH)
    keeps, gots = reduce_channels([spatial_call(lat, weight_s, frame) for frame in range(2)])
    hidden, first, last, stats = hidden_call(lat, keeps, gots, size)
    after = lax.ppermute(first, "seq", [(i + 1, i) for i in range(size - 1)])
    before = lax.ppermute(last, "seq", [(i, i + 1) for i in range(size - 1)])
    stats = lax.all_to_all(stats, "seq", 0, 0, tiled=True)
    keeps, gots = reduce_channels(
        [
            temporal_call(hidden, before, stats, weight_t, False),
            temporal_call(hidden, after, stats, weight_t, True),
        ]
    )
    out = blend_call(mix_factor, hidden, keeps, gots)
    return out.reshape(2, ROWS, COLS, LOCAL).transpose(0, 3, 1, 2)


def solution(mesh):
    placed = (P("seq", "ch", None, None), P(None, None, "ch", None), P(None, "ch", None), P())
    return jax.shard_map(
        per_device,
        mesh=mesh,
        in_specs=placed,
        out_specs=P("seq", "ch", None, None),
        check_vma=False,
    )
```

time: 413 us -> 97.4 us (0.24)
  waiting for transfers between devices: 160 us -> 26.2 us
  blocking collectives: 150 us -> 21.6 us
  matrix products: 51.7 us -> 0 us
  Pallas kernels: 0 us -> 24.5 us
  local copies, waits for them, and re-layouts: 18.5 us -> 4.24 us
  between operations: 14.3 us -> 0.76 us
  starting transfers between devices: 10.2 us -> 19.8 us
  other arithmetic: 7.09 us -> 0 us
    unnamed x4 -> x0, waiting for transfers between devices: 139 us -> none
    psum x1 -> x0, blocking collectives: 130 us -> none  [per_device(): group_sums, square_sums = lax.psum((group_sums, square_sums), 'seq')]
    dot_general x12 -> x0, matrix products: 51.7 us -> none  [the longest x9 45.6 us: spatial_taps(): lax.dot_general(weight_block[row_tap, col_tap], shifted, (((0,), (1,)), (...]
    ppermute x0 -> x10, waiting for transfers between devices: none -> 26.2 us  [the longest x4 25.7 us: reduce_channels(): gots.append(lax.ppermute(send, 'ch', HALF_SWAP))]
    pallas_call x0 -> x10, Pallas kernels: none -> 24.5 us  [the longest x2 13.4 us: spatial_call(): pl.pallas_call(spatial_kernel, grid=(CH // TILE,), in_specs=[pl.BlockSpec...]
    all_to_all x1 -> x0, waiting for transfers between devices: 20.4 us -> none  [per_device(): lax.all_to_all(reduced, 'seq', split_axis=1, concat_axis=2, tiled=True)]
    ppermute x0 -> x10, starting transfers between devices: none -> 19.8 us  [the longest x4 7.53 us: reduce_channels(): gots.append(lax.ppermute(send, 'ch', HALF_SWAP))]
    unnamed x10 -> x8, local copies, waits for them, and re-layouts: 15.7 us -> 4.24 us
  transfers between devices with their start and end apart: 3 -> 10, of which waited for: 3 -> 5; matrix products, arithmetic and copies ran while one was open for 0% -> 0% of each run, Pallas kernels for 0% -> 16%
where the time goes in v1:
time: 97.4 us; the launch traced here: 97.2 us
  waiting for transfers between devices  26.2 us (27%)
  Pallas kernels  24.5 us (25%)
  blocking collectives  21.6 us (22%)
  starting transfers between devices  19.8 us (20%)
  local copies, waits for them, and re-layouts  4.24 us (4%)
    ppermute x4, waiting for transfers between devices, reduce_channels(): gots.append(lax.ppermute(send, 'ch', HALF_SWAP))  25.7 us
    all_to_all x1, blocking collectives, per_device(): stats = lax.all_to_all(stats, 'seq', 0, 0, tiled=True)  21.6 us
    pallas_call x2, Pallas kernels, spatial_call(): pl.pallas_call(spatial_kernel, grid=(CH // TILE,), in_specs=[pl.BlockSpec...  13.4 us
    pallas_call x2, Pallas kernels, temporal_call(): pl.pallas_call(functools.partial(temporal_kernel, last), grid=(CH // TILE...  7.86 us
    ppermute x4, starting transfers between devices, reduce_channels(): gots.append(lax.ppermute(send, 'ch', HALF_SWAP))  7.53 us
    ppermute x4, starting transfers between devices, reduce_channels(): got = lax.ppermute(send, 'ch', CORE_SWAP)  6.98 us
    unnamed x8, local copies, waits for them, and re-layouts  4.24 us
    ppermute x1, starting transfers between devices, per_device(): before = lax.ppermute(last, 'seq', [(i, i + 1) for i in range(size - 1)])  4.01 us
  transfers between devices with their start and end apart: 10, of which 5 were waited for; matrix products, arithmetic and copies ran while one was open for 0% of the time, Pallas kernels for 16%

profile of v1, /device:TPU:1, one launch (start us, length us, event | category | flops | bytes accessed | tf_op | source)
XLA Modules:
  0.0 97.2 jit_solution(765906585627658972)
XLA Ops:
  0.0 1.1 %copy-done = bf16[2,320,16,32]{1,3,2,0:T(8,128)(2,1)S(1)} copy-done((bf16[2,320,16,32]{1,3,2,0:T(8,128)(2,1)S(1)}, bf16[2,320,16,32]{1,3,2,0:T(8,128)(2,1)}, u32[]{:S(2)}) %copy-start) | copy-done | bytes 655384
  1.1 3.1 %copy-done.2 = bf16[3,3,320,1280]{3,2,1,0:T(8,128)(2,1)S(1)} copy-done((bf16[3,3,320,1280]{3,2,1,0:T(8,128)(2,1)S(1)}, bf16[3,3,320,1280]{3,2,1,0:T(8,128)(2,1)}, u32[]{:S(2)}) %copy-start.2) | copy-done | bytes 7372824
  4.2 6.7 %spatial.3 = (bf16[512,640]{1,0:T(8,128)(2,1)S(1)}, bf16[512,640]{1,0:T(8,128)(2,1)S(1)}) custom-call(bf16[1024,320]{1,0:T(8,128)(2,1)S(1)} %bitcast.12, bf16[3,960,1280]{2,1,0:T(8,128)(2,1)S(1)} %bitcast.18), custom_call_target="tpu_custom_call" | custom-call | flops 3774873600 | bytes 7372800 | tf_op jit(solution)/shard_map/spatial/pallas_call | solution.py:130
  11.0 3.3 %collective-permute-start.1 = (bf16[512,640]{1,0:T(8,128)(2,1)S(1)}, bf16[512,640]{1,0:T(8,128)(2,1)S(1)}, u32[]{:S(2)}, u32[]{:S(2)}) collective-permute-start(bf16[512,640]{1,0:T(8,128)(2,1)S(1)} %get-tuple-element.29), channel_id=1, source_target_pairs={{0,1},{1,0},{2,3},{3,2},{4,5},{5,4},{6,7},{7,6},{8,9},{9,8},{10,11... | collective-permute-start | bytes 1966088 | tf_op jit(solution)/shard_map/ppermute | solution.py:295
  14.3 6.7 %spatial.2 = (bf16[512,640]{1,0:T(8,128)(2,1)S(1)}, bf16[512,640]{1,0:T(8,128)(2,1)S(1)}) custom-call(bf16[1024,320]{1,0:T(8,128)(2,1)S(1)} %bitcast.13, bf16[3,960,1280]{2,1,0:T(8,128)(2,1)S(1)} %bitcast.19), custom_call_target="tpu_custom_call" | custom-call | flops 3774873600 | bytes 7372800 | tf_op jit(solution)/shard_map/spatial/pallas_call | solution.py:130
  21.0 0.0 copy-start.1
  21.0 0.1 collective-permute-start
  21.1 0.0 collective-permute-done.1.got_ref
  21.1 0.2 chip_sum.5
  21.4 0.0 copy-start.3
  21.4 1.4 %collective-permute-start.3 = (bf16[256,640]{1,0:T(8,128)(2,1)S(1)}, bf16[256,640]{1,0:T(8,128)(2,1)S(1)}, u32[]{:S(2)}, u32[]{:S(2)}) collective-permute-start(bf16[256,640]{1,0:T(8,128)(2,1)S(1)} %get-tuple-element.32), channel_id=1, source_target_pairs={{0,2},{2,0},{1,3},{3,1},{4,6},{6,4},{5,7},{7,5},{8,10},{10,8},{9,1... | collective-permute-start | bytes 983048 | tf_op jit(solution)/shard_map/ppermute | solution.py:298
  22.8 0.4 collective-permute-done.got_ref
  23.2 0.2 chip_sum.4
  23.5 1.4 %collective-permute-start.2 = (bf16[256,640]{1,0:T(8,128)(2,1)S(1)}, bf16[256,640]{1,0:T(8,128)(2,1)S(1)}, u32[]{:S(2)}, u32[]{:S(2)}) collective-permute-start(bf16[256,640]{1,0:T(8,128)(2,1)S(1)} %get-tuple-element.31), channel_id=1, source_target_pairs={{0,2},{2,0},{1,3},{3,1},{4,6},{6,4},{5,7},{7,5},{8,10},{10,8},{9,1... | collective-permute-start | bytes 983048 | tf_op jit(solution)/shard_map/ppermute | solution.py:298
  24.9 6.9 %collective-permute-done.3.got1 = bf16[256,640]{1,0:T(8,128)(2,1)S(1)} collective-permute-done((bf16[256,640]{1,0:T(8,128)(2,1)S(1)}, bf16[256,640]{1,0:T(8,128)(2,1)S(1)}, u32[]{:S(2)}, u32[]{:S(2)}) %collective-permute-start.3) | collective-permute-done | bytes 327712 | tf_op jit(solution)/shard_map/ppermute | solution.py:298
  31.8 7.0 %collective-permute-done.2.got0 = bf16[256,640]{1,0:T(8,128)(2,1)S(1)} collective-permute-done((bf16[256,640]{1,0:T(8,128)(2,1)S(1)}, bf16[256,640]{1,0:T(8,128)(2,1)S(1)}, u32[]{:S(2)}, u32[]{:S(2)}) %collective-permute-start.2) | collective-permute-done | bytes 327712 | tf_op jit(solution)/shard_map/ppermute | solution.py:298
  38.8 0.9 hidden.1
  39.8 1.3 %collective-permute-start.6 = (bf16[256,640]{1,0:T(8,128)(2,1)S(1)}, bf16[256,640]{1,0:T(8,128)(2,1)S(1)}, u32[]{:S(2)}, u32[]{:S(2)}) collective-permute-start(bf16[256,640]{1,0:T(8,128)(2,1)S(1)} %get-tuple-element.39), channel_id=1, source_target_pairs={{4,0},{8,4},{12,8},{16,12},{20,16},{24,20},{28,24},{32,28},{36,32}... | collective-permute-start | bytes 983048 | tf_op jit(solution)/shard_map/ppermute | solution.py:309
  41.1 4.0 %collective-permute-start.4 = (bf16[256,640]{1,0:T(8,128)(2,1)S(1)}, bf16[256,640]{1,0:T(8,128)(2,1)S(1)}, u32[]{:S(2)}, u32[]{:S(2)}) collective-permute-start(bf16[256,640]{1,0:T(8,128)(2,1)S(1)} %get-tuple-element.34), channel_id=1, source_target_pairs={{0,4},{4,8},{8,12},{12,16},{16,20},{20,24},{24,28},{28,32},{32,36}... | collective-permute-start | bytes 983048 | tf_op jit(solution)/shard_map/ppermute | solution.py:310
  45.1 21.6 %all_to_all.11 = f32[64,1,128]{2,1,0:T(1,128)S(1)} all-to-all(f32[64,1,128]{2,1,0:T(1,128)S(1)} %bitcast.17), channel_id=1, replica_groups=mesh['seq'=64,'ch'=4] {'seq'}, dimensions={0} | all-to-all | bytes 65536 | tf_op jit(solution)/shard_map/all_to_all | solution.py:311
  66.7 0.0 collective-permute-done.6.halo_ref
  66.7 3.9 %temporal.3 = (bf16[512,640]{1,0:T(8,128)(2,1)S(1)}, bf16[512,640]{1,0:T(8,128)(2,1)S(1)}) custom-call(f32[1024,320]{1,0:T(8,128)S(1)} %get-tuple-element.33.hidden_ref, bf16[256,640]{1,0:T(8,128)(2,1)S(1)} %collective-permute-done.6.halo_ref, f32[64,128]{1,0:T(8,128)S(1)} %bitcast.15, bf16[960,1280]{1,0:T(8,128)(2,1)S(1)} %bitcast.20), custom_call_target="tpu_custom_call" | custom-call | flops 1258291200 | bytes 2457600 | tf_op jit(solution)/shard_map/temporal/pallas_call | solution.py:184
  70.7 3.4 %collective-permute-start.7 = (bf16[512,640]{1,0:T(8,128)(2,1)S(1)}, bf16[512,640]{1,0:T(8,128)(2,1)S(1)}, u32[]{:S(2)}, u32[]{:S(2)}) collective-permute-start(bf16[512,640]{1,0:T(8,128)(2,1)S(1)} %get-tuple-element.41), channel_id=1, source_target_pairs={{0,1},{1,0},{2,3},{3,2},{4,5},{5,4},{6,7},{7,6},{8,9},{9,8},{10,11... | collective-permute-start | bytes 1966088 | tf_op jit(solution)/shard_map/ppermute | solution.py:295
  74.1 3.9 %temporal.2 = (bf16[512,640]{1,0:T(8,128)(2,1)S(1)}, bf16[512,640]{1,0:T(8,128)(2,1)S(1)}) custom-call(f32[1024,320]{1,0:T(8,128)S(1)} %get-tuple-element.33.hidden_ref, bf16[256,640]{1,0:T(8,128)(2,1)S(1)} %collective-permute-done.4.halo_ref, f32[64,128]{1,0:T(8,128)S(1)} %bitcast.16, bf16[960,1280]{1,0:T(8,128)(2,1)S(1)} %bitcast.21), custom_call_target="tpu_custom_call" | custom-call | flops 1258291200 | bytes 2457600 | tf_op jit(solution)/shard_map/temporal/pallas_call | solution.py:184
  78.0 0.1 collective-permute-start.5
  78.1 0.2 chip_sum.7
  78.4 2.9 %collective-permute-start.9 = (bf16[256,640]{1,0:T(8,128)(2,1)S(1)}, bf16[256,640]{1,0:T(8,128)(2,1)S(1)}, u32[]{:S(2)}, u32[]{:S(2)}) collective-permute-start(bf16[256,640]{1,0:T(8,128)(2,1)S(1)} %get-tuple-element.44), channel_id=1, source_target_pairs={{0,2},{2,0},{1,3},{3,1},{4,6},{6,4},{5,7},{7,5},{8,10},{10,8},{9,1... | collective-permute-start | bytes 983048 | tf_op jit(solution)/shard_map/ppermute | solution.py:298
  81.3 0.2 chip_sum.6
  81.5 1.8 %collective-permute-start.8 = (bf16[256,640]{1,0:T(8,128)(2,1)S(1)}, bf16[256,640]{1,0:T(8,128)(2,1)S(1)}, u32[]{:S(2)}, u32[]{:S(2)}) collective-permute-start(bf16[256,640]{1,0:T(8,128)(2,1)S(1)} %get-tuple-element.43), channel_id=1, source_target_pairs={{0,2},{2,0},{1,3},{3,1},{4,6},{6,4},{5,7},{7,5},{8,10},{10,8},{9,1... | collective-permute-start | bytes 983048 | tf_op jit(solution)/shard_map/ppermute | solution.py:298
  84.0 4.8 %collective-permute-done.9.got1 = bf16[256,640]{1,0:T(8,128)(2,1)S(1)} collective-permute-done((bf16[256,640]{1,0:T(8,128)(2,1)S(1)}, bf16[256,640]{1,0:T(8,128)(2,1)S(1)}, u32[]{:S(2)}, u32[]{:S(2)}) %collective-permute-start.9) | collective-permute-done | bytes 327712 | tf_op jit(solution)/shard_map/ppermute | solution.py:298
  88.8 7.0 %collective-permute-done.8.got0 = bf16[256,640]{1,0:T(8,128)(2,1)S(1)} collective-permute-done((bf16[256,640]{1,0:T(8,128)(2,1)S(1)}, bf16[256,640]{1,0:T(8,128)(2,1)S(1)}, u32[]{:S(2)}, u32[]{:S(2)}) %collective-permute-start.8) | collective-permute-done | bytes 327712 | tf_op jit(solution)/shard_map/ppermute | solution.py:298
  95.8 1.4 %blend.1 = bf16[1024,320]{1,0:T(8,128)(2,1)} custom-call(f32[1]{0:T(128)S(6)} %copy.6.mix_ref, f32[1024,320]{1,0:T(8,128)S(1)} %get-tuple-element.33.hidden_ref, f32[512,320]{1,0:T(8,128)S(1)} %get-tuple-element.38.keep0, f32[512,320]{1,0:T(8,128)S(1)} %get-tuple-element.42.keep1, bf16[256,640]{1,0:T(8,128)(2,1)S(1)} %collective-permute-done.8.got0, ...), custom_call_target="tpu_custom_call" | custom-call | flops 983040 | bytes 2621440 | tf_op jit(solution)/shard_map/blend/pallas_call | solution.py:281
  (7 shorter events, 0.0 us)
Async XLA Ops:
  0.0 1.1 %copy-start = (bf16[2,320,16,32]{1,3,2,0:T(8,128)(2,1)S(1)}, bf16[2,320,16,32]{1,3,2,0:T(8,128)(2,1)}, u32[]{:S(2)}) copy-start(bf16[2,320,16,32]{1,3,2,0:T(8,128)(2,1)} %param.4) | copy-start | bytes 1966084
  1.1 3.1 %copy-start.2 = (bf16[3,3,320,1280]{3,2,1,0:T(8,128)(2,1)S(1)}, bf16[3,3,320,1280]{3,2,1,0:T(8,128)(2,1)}, u32[]{:S(2)}) copy-start(bf16[3,3,320,1280]{3,2,1,0:T(8,128)(2,1)} %param.5) | copy-start | bytes 22118404
  11.0 10.2 %collective-permute-start.1 = (bf16[512,640]{1,0:T(8,128)(2,1)S(1)}, bf16[512,640]{1,0:T(8,128)(2,1)S(1)}, u32[]{:S(2)}, u32[]{:S(2)}) collective-permute-start(bf16[512,640]{1,0:T(8,128)(2,1)S(1)} %get-tuple-element.29), channel_id=1, source_target_pairs={{0,1},{1,0},{2,3},{3,2},{4,5},{5,4},{6,7},{7,6},{8,9},{9,8},{10,11... | collective-permute-start | bytes 1966088 | tf_op jit(solution)/shard_map/ppermute | solution.py:295
  21.0 17.8 %copy-start.1 = (bf16[2,320,16,32]{1,3,2,0:T(8,128)(2,1)S(1)}, bf16[2,320,16,32]{1,3,2,0:T(8,128)(2,1)}, u32[]{:S(2)}) copy-start(bf16[2,320,16,32]{1,3,2,0:T(8,128)(2,1)} %param.4) | copy-start | bytes 1966084
  21.0 2.2 %collective-permute-start = (bf16[512,640]{1,0:T(8,128)(2,1)S(1)}, bf16[512,640]{1,0:T(8,128)(2,1)S(1)}, u32[]{:S(2)}, u32[]{:S(2)}) collective-permute-start(bf16[512,640]{1,0:T(8,128)(2,1)S(1)} %get-tuple-element.26), channel_id=1, source_target_pairs={{0,1},{1,0},{2,3},{3,2},{4,5},{5,4},{6,7},{7,6},{8,9},{9,8},{10,11... | collective-permute-start | bytes 1966088 | tf_op jit(solution)/shard_map/ppermute | solution.py:295
  21.4 45.3 %copy-start.3 = (bf16[3,320,1280]{2,1,0:T(8,128)(2,1)S(1)}, bf16[3,320,1280]{2,1,0:T(8,128)(2,1)}, u32[]{:S(2)}) copy-start(bf16[3,320,1280]{2,1,0:T(8,128)(2,1)} %param.6) | copy-start | bytes 7372804
  21.4 10.4 %collective-permute-start.3 = (bf16[256,640]{1,0:T(8,128)(2,1)S(1)}, bf16[256,640]{1,0:T(8,128)(2,1)S(1)}, u32[]{:S(2)}, u32[]{:S(2)}) collective-permute-start(bf16[256,640]{1,0:T(8,128)(2,1)S(1)} %get-tuple-element.32), channel_id=1, source_target_pairs={{0,2},{2,0},{1,3},{3,1},{4,6},{6,4},{5,7},{7,5},{8,10},{10,8},{9,1... | collective-permute-start | bytes 983048 | tf_op jit(solution)/shard_map/ppermute | solution.py:298
  23.5 15.4 %collective-permute-start.2 = (bf16[256,640]{1,0:T(8,128)(2,1)S(1)}, bf16[256,640]{1,0:T(8,128)(2,1)S(1)}, u32[]{:S(2)}, u32[]{:S(2)}) collective-permute-start(bf16[256,640]{1,0:T(8,128)(2,1)S(1)} %get-tuple-element.31), channel_id=1, source_target_pairs={{0,2},{2,0},{1,3},{3,1},{4,6},{6,4},{5,7},{7,5},{8,10},{10,8},{9,1... | collective-permute-start | bytes 983048 | tf_op jit(solution)/shard_map/ppermute | solution.py:298
  39.8 27.0 %collective-permute-start.6 = (bf16[256,640]{1,0:T(8,128)(2,1)S(1)}, bf16[256,640]{1,0:T(8,128)(2,1)S(1)}, u32[]{:S(2)}, u32[]{:S(2)}) collective-permute-start(bf16[256,640]{1,0:T(8,128)(2,1)S(1)} %get-tuple-element.39), channel_id=1, source_target_pairs={{4,0},{8,4},{12,8},{16,12},{20,16},{24,20},{28,24},{32,28},{36,32}... | collective-permute-start | bytes 983048 | tf_op jit(solution)/shard_map/ppermute | solution.py:309
  41.1 33.0 %collective-permute-start.4 = (bf16[256,640]{1,0:T(8,128)(2,1)S(1)}, bf16[256,640]{1,0:T(8,128)(2,1)S(1)}, u32[]{:S(2)}, u32[]{:S(2)}) collective-permute-start(bf16[256,640]{1,0:T(8,128)(2,1)S(1)} %get-tuple-element.34), channel_id=1, source_target_pairs={{0,4},{4,8},{8,12},{12,16},{16,20},{20,24},{24,28},{28,32},{32,36}... | collective-permute-start | bytes 983048 | tf_op jit(solution)/shard_map/ppermute | solution.py:310
  70.7 7.5 %collective-permute-start.7 = (bf16[512,640]{1,0:T(8,128)(2,1)S(1)}, bf16[512,640]{1,0:T(8,128)(2,1)S(1)}, u32[]{:S(2)}, u32[]{:S(2)}) collective-permute-start(bf16[512,640]{1,0:T(8,128)(2,1)S(1)} %get-tuple-element.41), channel_id=1, source_target_pairs={{0,1},{1,0},{2,3},{3,2},{4,5},{5,4},{6,7},{7,6},{8,9},{9,8},{10,11... | collective-permute-start | bytes 1966088 | tf_op jit(solution)/shard_map/ppermute | solution.py:295
  78.0 3.3 %collective-permute-start.5 = (bf16[512,640]{1,0:T(8,128)(2,1)S(1)}, bf16[512,640]{1,0:T(8,128)(2,1)S(1)}, u32[]{:S(2)}, u32[]{:S(2)}) collective-permute-start(bf16[512,640]{1,0:T(8,128)(2,1)S(1)} %get-tuple-element.37), channel_id=1, source_target_pairs={{0,1},{1,0},{2,3},{3,2},{4,5},{5,4},{6,7},{7,6},{8,9},{9,8},{10,11... | collective-permute-start | bytes 1966088 | tf_op jit(solution)/shard_map/ppermute | solution.py:295
  78.4 10.4 %collective-permute-start.9 = (bf16[256,640]{1,0:T(8,128)(2,1)S(1)}, bf16[256,640]{1,0:T(8,128)(2,1)S(1)}, u32[]{:S(2)}, u32[]{:S(2)}) collective-permute-start(bf16[256,640]{1,0:T(8,128)(2,1)S(1)} %get-tuple-element.44), channel_id=1, source_target_pairs={{0,2},{2,0},{1,3},{3,1},{4,6},{6,4},{5,7},{7,5},{8,10},{10,8},{9,1... | collective-permute-start | bytes 983048 | tf_op jit(solution)/shard_map/ppermute | solution.py:298
  81.5 14.3 %collective-permute-start.8 = (bf16[256,640]{1,0:T(8,128)(2,1)S(1)}, bf16[256,640]{1,0:T(8,128)(2,1)S(1)}, u32[]{:S(2)}, u32[]{:S(2)}) collective-permute-start(bf16[256,640]{1,0:T(8,128)(2,1)S(1)} %get-tuple-element.43), channel_id=1, source_target_pairs={{0,2},{2,0},{1,3},{3,1},{4,6},{6,4},{5,7},{7,5},{8,10},{10,8},{9,1... | collective-permute-start | bytes 983048 | tf_op jit(solution)/shard_map/ppermute | solution.py:298

commit v2 on v1

v2 whole, which is shorter than its diff:
```python
import functools

import jax
import jax.numpy as jnp
from jax import lax
from jax.experimental import pallas as pl
from jax.experimental.pallas import tpu as pltpu
from jax.sharding import PartitionSpec as P

CH = 1280
GROUPS = 32
GROUP = CH // GROUPS
ROWS = 16
COLS = 32
PX = ROWS * COLS
LOCAL = CH // 4
LOCAL_GROUPS = LOCAL // GROUP
TAPS = 3
WIDE = TAPS * LOCAL
HALF = CH // 2
EPS = 1e-05

CORE_SWAP = [(0, 1), (1, 0), (2, 3), (3, 2)]
HALF_SWAP = [(0, 2), (2, 0), (1, 3), (3, 1)]
CORE_PIECES = 2
HALF_PIECES = 1
VMEM_LIMIT = 40 * 1024 * 1024
BF16 = jnp.bfloat16
F32 = jnp.float32
HIGHEST = lax.Precision.HIGHEST


def params():
    return pltpu.CompilerParams(vmem_limit_bytes=VMEM_LIMIT)


def silu(v):
    half = 0.5 * v
    return half + half * jnp.tanh(half)


def group_of(channel):
    return (channel * 205) >> 13


def group_block():
    row = lax.broadcasted_iota(jnp.int32, (LOCAL, LOCAL), 0)
    col = lax.broadcasted_iota(jnp.int32, (LOCAL, LOCAL), 1)
    return jnp.where(group_of(row) == group_of(col), 1.0, 0.0)


def group_to_lane(shift):
    row = lax.broadcasted_iota(jnp.int32, (LOCAL, 128), 0)
    lane = lax.broadcasted_iota(jnp.int32, (LOCAL, 128), 1)
    return jnp.where(group_of(row) == lane - shift, 1.0, 0.0)


def lane_to_group(shift):
    lane = lax.broadcasted_iota(jnp.int32, (128, LOCAL), 0)
    col = lax.broadcasted_iota(jnp.int32, (128, LOCAL), 1)
    return jnp.where(group_of(col) == lane - shift, 1.0, 0.0)


def exact_dot(a, b):
    return jnp.dot(a, b, precision=HIGHEST, preferred_element_type=F32)


def pack(block):
    return jnp.concatenate([block[: PX // 2], block[PX // 2 :]], axis=1)


def unpack(ref):
    return jnp.concatenate([ref[:, :LOCAL], ref[:, LOCAL:]], axis=0)


def split_cores(total_ref, send_ref, own_ref):
    core = lax.axis_index("ch") % 2

    def copy(ref, first):
        for frame in range(2):
            ref[:, frame * LOCAL : (frame + 1) * LOCAL] = total_ref[frame, :, first : first + LOCAL]

    @pl.when(core == 0)
    def _():
        copy(own_ref, 0)
        copy(send_ref, LOCAL)

    @pl.when(core == 1)
    def _():
        copy(own_ref, LOCAL)
        copy(send_ref, 0)


def half_columns(other):
    half = lax.axis_index("ch") // 2
    half = 1 - half if other else half
    return pl.ds(pl.multiple_of(half * HALF, HALF), HALF)


def spatial_kernel(other, lat_hbm, weight_hbm, after_ref, send_ref, own_ref, lat_ref, weight_ref, taps_ref, total_ref, sems):
    copies = [pltpu.make_async_copy(lat_hbm, lat_ref, sems.at[TAPS])]
    for row_tap in range(TAPS):
        source = weight_hbm.at[row_tap, :, half_columns(other)]
        copies.append(pltpu.make_async_copy(source, weight_ref.at[row_tap], sems.at[row_tap]))
    for copy in copies:
        copy.start()
    copies[0].wait()

    rows = []
    for frame in range(2):
        lat = lat_ref[frame * PX : (frame + 1) * PX].astype(F32)
        rows.append(jnp.sum(lat, axis=0, keepdims=True))
        rows.append(jnp.sum(lat * lat, axis=0, keepdims=True))
    means = jnp.concatenate(rows + [jnp.zeros((4, LOCAL), F32)], axis=0)
    means = exact_dot(means, group_block()) * (1.0 / (GROUP * PX))
    col = lax.broadcasted_iota(jnp.int32, (COLS, LOCAL), 0)
    for frame in range(2):
        mean = means[2 * frame : 2 * frame + 1]
        var = means[2 * frame + 1 : 2 * frame + 2] - mean * mean
        lat = lat_ref[frame * PX : (frame + 1) * PX].astype(F32)
        act = silu((lat - mean) * lax.rsqrt(var + EPS))
        left, right = [], []
        for row in range(ROWS):
            cells = act[row * COLS : (row + 1) * COLS]
            left.append(jnp.where(col == 0, 0.0, pltpu.roll(cells, 1, 0)))
            right.append(jnp.where(col == COLS - 1, 0.0, pltpu.roll(cells, COLS - 1, 0)))
        taps_ref[frame, :COLS] = jnp.zeros((COLS, WIDE), BF16)
        taps_ref[frame, COLS + PX :] = jnp.zeros((COLS, WIDE), BF16)
        inside = slice(COLS, COLS + PX)
        taps_ref[frame, inside, :LOCAL] = jnp.concatenate(left, axis=0).astype(BF16)
        taps_ref[frame, inside, LOCAL : 2 * LOCAL] = act.astype(BF16)
        taps_ref[frame, inside, 2 * LOCAL :] = jnp.concatenate(right, axis=0).astype(BF16)

    for copy in copies[1:]:
        copy.wait()
    for frame in range(2):
        total = None
        for row_tap in range(TAPS):
            cells = slice(row_tap * COLS, row_tap * COLS + PX)
            term = jnp.dot(taps_ref[frame, cells], weight_ref[row_tap], preferred_element_type=F32)
            total = term if total is None else total + term
        total_ref[frame] = total.astype(BF16)
    split_cores(total_ref, send_ref, own_ref)


def spatial_call(lat, weight, after, other):
    shape = jax.ShapeDtypeStruct((PX, 2 * LOCAL), BF16)
    vmem, hbm = pl.BlockSpec(memory_space=pltpu.VMEM), pl.BlockSpec(memory_space=pltpu.HBM)
    return pl.pallas_call(
        functools.partial(spatial_kernel, other),
        in_specs=[hbm, hbm, pl.BlockSpec(memory_space=pl.ANY)],
        out_specs=[vmem, vmem],
        out_shape=[shape, shape],
        scratch_shapes=[
            pltpu.VMEM((2 * PX, LOCAL), BF16),
            pltpu.VMEM((TAPS, WIDE, HALF), BF16),
            pltpu.VMEM((2, PX + 2 * COLS, WIDE), BF16),
            pltpu.VMEM((2, PX, HALF), BF16),
            pltpu.SemaphoreType.DMA((TAPS + 1,)),
        ],
        compiler_params=params(),
        cost_estimate=pl.CostEstimate(
            flops=4 * PX * TAPS * WIDE * HALF,
            bytes_accessed=2 * TAPS * WIDE * HALF,
            transcendentals=2 * PX * LOCAL,
        ),
        name="spatial",
    )(lat, weight, after)


def temporal_kernel(
    other, hidden_ref, before_ref, next_ref, stats_ref, weight_hbm, after_ref, send_ref, own_ref, weight_ref, taps_ref, total_ref, sem
):
    copy = pltpu.make_async_copy(weight_hbm.at[:, half_columns(other)], weight_ref, sem)
    copy.start()
    seq, size = lax.axis_index("seq"), lax.axis_size("seq")
    sums = jnp.sum(stats_ref[...], axis=0, keepdims=True) * (1.0 / (GROUP * 2 * PX * size))
    sums = jnp.broadcast_to(sums, (8, 128))
    mean = exact_dot(sums, lane_to_group(0))[0:1]
    var = exact_dot(sums, lane_to_group(LOCAL_GROUPS))[0:1] - mean * mean
    scale = lax.rsqrt(var + EPS)

    def act(values):
        return silu((values - mean) * scale)

    before = act(unpack(before_ref).astype(F32)) * jnp.where(seq == 0, 0.0, 1.0)
    after = act(unpack(next_ref).astype(F32)) * jnp.where(seq == size - 1, 0.0, 1.0)
    frames = [before, act(hidden_ref[:PX]), act(hidden_ref[PX:]), after]
    for frame in range(2):
        for tap in range(TAPS):
            taps_ref[frame, :, tap * LOCAL : (tap + 1) * LOCAL] = frames[frame + tap].astype(BF16)
    copy.wait()
    for frame in range(2):
        total_ref[frame] = jnp.dot(taps_ref[frame], weight_ref[...], preferred_element_type=F32).astype(BF16)
    split_cores(total_ref, send_ref, own_ref)


def temporal_call(hidden, before, next_, stats, weight, after, other):
    shape = jax.ShapeDtypeStruct((PX, 2 * LOCAL), BF16)
    vmem = pl.BlockSpec(memory_space=pltpu.VMEM)
    return pl.pallas_call(
        functools.partial(temporal_kernel, other),
        in_specs=[vmem] * 4 + [pl.BlockSpec(memory_space=pl.ANY)] * 2,
        out_specs=[vmem, vmem],
        out_shape=[shape, shape],
        scratch_shapes=[
            pltpu.VMEM((WIDE, HALF), BF16),
            pltpu.VMEM((2, PX, WIDE), BF16),
            pltpu.VMEM((2, PX, HALF), BF16),
            pltpu.SemaphoreType.DMA,
        ],
        compiler_params=params(),
        cost_estimate=pl.CostEstimate(
            flops=4 * PX * WIDE * HALF,
            bytes_accessed=2 * WIDE * HALF,
            transcendentals=4 * PX * LOCAL,
        ),
        name="temporal",
    )(hidden, before, next_, stats, weight, after)


def chip_sum_kernel(own_ref, got_ref, out_ref):
    out_ref[...] = (own_ref[...].astype(F32) + got_ref[...].astype(F32)).astype(BF16)


def chip_sum(own, got):
    return pl.pallas_call(
        chip_sum_kernel,
        out_shape=jax.ShapeDtypeStruct((PX, 2 * LOCAL), BF16),
        compiler_params=params(),
        cost_estimate=pl.CostEstimate(flops=2 * PX * LOCAL, bytes_accessed=12 * PX * LOCAL, transcendentals=0),
        name="chip_sum",
    )(own, got)


def three_sums(own_ref, core_refs, half_refs, frame):
    cols = slice(frame * LOCAL, (frame + 1) * LOCAL)
    core = jnp.concatenate([ref[:, cols] for ref in core_refs], axis=0)
    half = jnp.concatenate([ref[:, cols] for ref in half_refs], axis=0)
    return own_ref[:, cols].astype(F32) + core.astype(F32) + half.astype(F32)


def hidden_kernel(lat_ref, own_ref, *refs):
    cores, halves = refs[:CORE_PIECES], refs[CORE_PIECES : CORE_PIECES + HALF_PIECES]
    hidden_ref, first_ref, last_ref, stats_ref = refs[CORE_PIECES + HALF_PIECES :]
    sums, squares = 0.0, 0.0
    for frame, edge in enumerate((first_ref, last_ref)):
        cells = slice(frame * PX, (frame + 1) * PX)
        hidden = lat_ref[cells].astype(F32) + three_sums(own_ref, cores, halves, frame)
        hidden_ref[cells] = hidden
        edge[...] = pack(hidden).astype(BF16)
        sums += jnp.sum(hidden, axis=0, keepdims=True)
        squares += jnp.sum(hidden * hidden, axis=0, keepdims=True)
    row = exact_dot(jnp.broadcast_to(sums, (8, LOCAL)), group_to_lane(0))
    row += exact_dot(jnp.broadcast_to(squares, (8, LOCAL)), group_to_lane(LOCAL_GROUPS))
    stats_ref[...] = jnp.broadcast_to(row[0:1], stats_ref.shape)


def hidden_call(lat, shares, size):
    edge = jax.ShapeDtypeStruct((PX // 2, 2 * LOCAL), BF16)
    return pl.pallas_call(
        hidden_kernel,
        out_shape=[
            jax.ShapeDtypeStruct((2 * PX, LOCAL), F32),
            edge,
            edge,
            jax.ShapeDtypeStruct((size, 128), F32),
        ],
        compiler_params=params(),
        cost_estimate=pl.CostEstimate(flops=10 * PX * LOCAL, bytes_accessed=20 * PX * LOCAL, transcendentals=0),
        name="hidden",
    )(lat, *shares)


def blend_kernel(mix_ref, hidden_ref, own_ref, *refs):
    cores, halves, out_ref = refs[:CORE_PIECES], refs[CORE_PIECES:-1], refs[-1]
    mix = jnp.full((1, LOCAL), mix_ref[0], F32)
    weight = 1.0 - jax.nn.sigmoid(mix)
    for frame in range(2):
        cells = slice(frame * PX, (frame + 1) * PX)
        branch = three_sums(own_ref, cores, halves, frame).astype(BF16).astype(F32)
        out_ref[cells] = (hidden_ref[cells] + weight * branch).astype(BF16)


def blend_call(mix, hidden, shares):
    whole = pl.BlockSpec(memory_space=pltpu.VMEM)
    return pl.pallas_call(
        blend_kernel,
        in_specs=[pl.BlockSpec(memory_space=pltpu.SMEM)] + [whole] * (2 + CORE_PIECES + HALF_PIECES),
        out_specs=whole,
        out_shape=jax.ShapeDtypeStruct((2 * PX, LOCAL), BF16),
        compiler_params=params(),
        cost_estimate=pl.CostEstimate(flops=6 * PX * LOCAL, bytes_accessed=16 * PX * LOCAL, transcendentals=0),
        name="blend",
    )(mix, hidden, *shares)


def permute(array, perm, pieces):
    rows = array.shape[0] // pieces
    return [lax.ppermute(array[i * rows : (i + 1) * rows], "ch", perm) for i in range(pieces)]


def reduce_channels(conv, after):
    send, own = conv(after, True)
    chip = chip_sum(own, permute(send, CORE_SWAP, 1)[0])
    halves = permute(chip, HALF_SWAP, HALF_PIECES)
    send, own = conv(chip, False)
    return own, *permute(send, CORE_SWAP, CORE_PIECES), *halves


def per_device(latents, spatial_weight, temporal_weight, mix_factor):
    size = lax.axis_size("seq")
    lat = latents.transpose(0, 2, 3, 1).reshape(2 * PX, LOCAL)
    lat_hbm = pltpu.with_memory_space_constraint(lat, pltpu.HBM)
    weight_s = pltpu.with_memory_space_constraint(spatial_weight.reshape(TAPS, WIDE, CH), pltpu.HBM)
    weight_t = temporal_weight.reshape(WIDE, CH)
    shares = reduce_channels(functools.partial(spatial_call, lat_hbm, weight_s), lat_hbm)
    hidden, first, last, stats = hidden_call(lat, shares, size)
    next_ = lax.ppermute(first, "seq", [(i + 1, i) for i in range(size - 1)])
    before = lax.ppermute(last, "seq", [(i, i + 1) for i in range(size - 1)])
    stats = lax.all_to_all(stats, "seq", 0, 0, tiled=True)
    shares = reduce_channels(functools.partial(temporal_call, hidden, before, next_, stats, weight_t), hidden)
    out = blend_call(mix_factor, hidden, shares)
    return out.reshape(2, ROWS, COLS, LOCAL).transpose(0, 3, 1, 2)


def solution(mesh):
    placed = (P("seq", "ch", None, None), P(None, None, "ch", None), P(None, "ch", None), P())
    return jax.shard_map(
        per_device,
        mesh=mesh,
        in_specs=placed,
        out_specs=P("seq", "ch", None, None),
        check_vma=False,
    )
```

time: 97.4 us -> 86.8 us (0.89)
  waiting for transfers between devices: 26.2 us -> 20.4 us
  starting transfers between devices: 19.8 us -> 15.5 us
  local copies, waits for them, and re-layouts: 4.24 us -> 0.13 us
  Pallas kernels: 24.5 us -> 26.5 us
  blocking collectives: 21.6 us -> 23.4 us
    ppermute x9, waiting for transfers between devices: 26.2 us -> 20.4 us  [the longest x8 20.4 us: permute(): lax.ppermute(array[i * rows:(i + 1) * rows], 'ch', perm)]
    unnamed x8 -> x4, local copies, waits for them, and re-layouts: 4.24 us -> 0.01 us
    ppermute x1, starting transfers between devices: 4.01 us -> 1.83 us  [per_device(): before = lax.ppermute(last, 'seq', [(i, i + 1) for i in range(size - 1)])]
    ppermute x9, starting transfers between devices: 15.8 us -> 13.7 us  [the longest x8 12.4 us: permute(): lax.ppermute(array[i * rows:(i + 1) * rows], 'ch', perm)]
    all_to_all x1, blocking collectives: 21.6 us -> 23.4 us  [per_device(): stats = lax.all_to_all(stats, 'seq', 0, 0, tiled=True)]
    pallas_call x8 -> x6, Pallas kernels: 22.3 us -> 24 us  [the longest x2 16.2 us: spatial_call(): pl.pallas_call(functools.partial(spatial_kernel, other), in_specs=[hbm, h...]
  transfers between devices with their start and end apart: 10 -> 10, of which waited for: 5 -> 8; matrix products, arithmetic and copies ran while one was open for 0% -> 0% of each run, Pallas kernels for 16% -> 14%
where the time goes in v2:
time: 86.8 us; the launch traced here: 86.6 us
  Pallas kernels  26.5 us (31%)
  blocking collectives  23.4 us (27%)
  waiting for transfers between devices  20.4 us (24%)
  starting transfers between devices  15.5 us (18%)
    all_to_all x1, blocking collectives, per_device(): stats = lax.all_to_all(stats, 'seq', 0, 0, tiled=True)  23.4 us
    ppermute x8, waiting for transfers between devices, permute(): lax.ppermute(array[i * rows:(i + 1) * rows], 'ch', perm)  20.4 us
    pallas_call x2, Pallas kernels, spatial_call(): pl.pallas_call(functools.partial(spatial_kernel, other), in_specs=[hbm, h...  16.2 us
    ppermute x8, starting transfers between devices, permute(): lax.ppermute(array[i * rows:(i + 1) * rows], 'ch', perm)  12.4 us
    pallas_call x2, Pallas kernels, temporal_call(): pl.pallas_call(functools.partial(temporal_kernel, other), in_specs=[vmem]...  7.48 us
    ppermute x1, starting transfers between devices, per_device(): before = lax.ppermute(last, 'seq', [(i, i + 1) for i in range(size - 1)])  1.83 us
  transfers between devices with their start and end apart: 10, of which 8 were waited for; matrix products, arithmetic and copies ran while one was open for 0% of the time, Pallas kernels for 14%

profile of v2, /device:TPU:1, one launch (start us, length us, event | category | flops | bytes accessed | tf_op | source)
XLA Modules:
  0.0 86.6 jit_solution(2155997850696760219)
XLA Ops:
  0.0 8.1 %spatial.2 = (bf16[512,640]{1,0:T(8,128)(2,1)S(1)}, bf16[512,640]{1,0:T(8,128)(2,1)S(1)}) custom-call(bf16[1024,320]{1,0:T(8,128)(2,1)} %bitcast.14, bf16[3,960,1280]{2,1,0:T(8,128)(2,1)} %bitcast.21, bf16[1024,320]{1,0:T(8,128)(2,1)} %bitcast.15), custom_call_target="tpu_custom_call" | custom-call | flops 3774873600 | bytes 3686400 | tf_op jit(solution)/shard_map/spatial/pallas_call | solution.py:149
  8.1 3.3 %collective-permute-start = (bf16[512,640]{1,0:T(8,128)(2,1)S(1)}, bf16[512,640]{1,0:T(8,128)(2,1)S(1)}, u32[]{:S(2)}, u32[]{:S(2)}) collective-permute-start(bf16[512,640]{1,0:T(8,128)(2,1)S(1)} %get-tuple-element.18), channel_id=1, source_target_pairs={{0,1},{1,0},{2,3},{3,2},{4,5},{5,4},{6,7},{7,6},{8,9},{9,8},{10,11... | collective-permute-start | bytes 1966088 | tf_op jit(solution)/shard_map/ppermute | solution.py:300
  11.4 1.7 %collective-permute-done.got_ref = bf16[512,640]{1,0:T(8,128)(2,1)S(1)} collective-permute-done((bf16[512,640]{1,0:T(8,128)(2,1)S(1)}, bf16[512,640]{1,0:T(8,128)(2,1)S(1)}, u32[]{:S(2)}, u32[]{:S(2)}) %collective-permute-start) | collective-permute-done | bytes 655392 | tf_op jit(solution)/shard_map/ppermute | solution.py:300
  13.1 0.2 chip_sum.2.after_ref
  13.3 0.0 copy-start.1
  13.3 1.4 %collective-permute-start.3 = (bf16[512,640]{1,0:T(8,128)(2,1)S(1)}, bf16[512,640]{1,0:T(8,128)(2,1)S(1)}, u32[]{:S(2)}, u32[]{:S(2)}) collective-permute-start(bf16[512,640]{1,0:T(8,128)(2,1)S(1)} %chip_sum.2.after_ref), channel_id=1, source_target_pairs={{0,2},{2,0},{1,3},{3,1},{4,6},{6,4},{5,7},{7,5},{8,10},{10,8},{9,1... | collective-permute-start | bytes 1966088 | tf_op jit(solution)/shard_map/ppermute | solution.py:300
  14.8 8.1 %spatial.3 = (bf16[512,640]{1,0:T(8,128)(2,1)S(1)}, bf16[512,640]{1,0:T(8,128)(2,1)S(1)}) custom-call(bf16[1024,320]{1,0:T(8,128)(2,1)} %bitcast.16, bf16[3,960,1280]{2,1,0:T(8,128)(2,1)} %bitcast.22, bf16[512,640]{1,0:T(8,128)(2,1)S(1)} %chip_sum.2.after_ref), custom_call_target="tpu_custom_call" | custom-call | flops 3774873600 | bytes 3686400 | tf_op jit(solution)/shard_map/spatial/pallas_call | solution.py:149
  22.9 0.0 copy-start
  22.9 0.1 fusion.1
  22.9 0.7 collective-permute-start.2
  23.7 0.1 collective-permute-start.1
  23.8 1.2 %collective-permute-done.2.refs_1_ = bf16[256,640]{1,0:T(8,128)(2,1)S(1)} collective-permute-done((bf16[256,640]{1,0:T(8,128)(2,1)S(1)}, bf16[256,640]{1,0:T(8,128)(2,1)S(1)}, u32[]{:S(2)}, u32[]{:S(2)}) %collective-permute-start.2) | collective-permute-done | bytes 327712 | tf_op jit(solution)/shard_map/ppermute | solution.py:300
  24.9 0.5 collective-permute-done.1.refs_0_
  25.4 5.6 %collective-permute-done.3.refs_2_ = bf16[512,640]{1,0:T(8,128)(2,1)S(1)} collective-permute-done((bf16[512,640]{1,0:T(8,128)(2,1)S(1)}, bf16[512,640]{1,0:T(8,128)(2,1)S(1)}, u32[]{:S(2)}, u32[]{:S(2)}) %collective-permute-start.3) | collective-permute-done | bytes 655392 | tf_op jit(solution)/shard_map/ppermute | solution.py:300
  31.0 1.0 %hidden.1 = (f32[1024,320]{1,0:T(8,128)S(1)}, bf16[256,640]{1,0:T(8,128)(2,1)S(1)}, bf16[256,640]{1,0:T(8,128)(2,1)S(1)}, f32[64,128]{1,0:T(8,128)S(1)}) custom-call(bf16[1024,320]{1,0:T(8,128)(2,1)S(1)} %bitcast.17, bf16[512,640]{1,0:T(8,128)(2,1)S(1)} %get-tuple-element.19.own_ref, bf16[256,640]{1,0:T(8,128)(2,1)S(1)} %collective-permute-done.1.refs_0_, ...), custom_call_target="tpu_custom_call" | custom-call | flops 1638400 | bytes 3276800 | tf_op jit(solution)/shard_map/hidden/pallas_call | solution.py:261
  32.0 1.8 %collective-permute-start.4 = (bf16[256,640]{1,0:T(8,128)(2,1)S(1)}, bf16[256,640]{1,0:T(8,128)(2,1)S(1)}, u32[]{:S(2)}, u32[]{:S(2)}) collective-permute-start(bf16[256,640]{1,0:T(8,128)(2,1)S(1)} %get-tuple-element.22), channel_id=1, source_target_pairs={{0,4},{4,8},{8,12},{12,16},{16,20},{20,24},{24,28},{28,32},{32,36}... | collective-permute-start | bytes 983048 | tf_op jit(solution)/shard_map/ppermute | solution.py:320
  33.9 1.3 %collective-permute-start.5 = (bf16[256,640]{1,0:T(8,128)(2,1)S(1)}, bf16[256,640]{1,0:T(8,128)(2,1)S(1)}, u32[]{:S(2)}, u32[]{:S(2)}) collective-permute-start(bf16[256,640]{1,0:T(8,128)(2,1)S(1)} %get-tuple-element.23), channel_id=1, source_target_pairs={{4,0},{8,4},{12,8},{16,12},{20,16},{24,20},{28,24},{32,28},{36,32}... | collective-permute-start | bytes 983048 | tf_op jit(solution)/shard_map/ppermute | solution.py:319
  35.2 23.4 %all_to_all.11 = f32[64,1,128]{2,1,0:T(1,128)S(1)} all-to-all(f32[64,1,128]{2,1,0:T(1,128)S(1)} %bitcast.20), channel_id=1, replica_groups=mesh['seq'=64,'ch'=4] {'seq'}, dimensions={0} | all-to-all | bytes 65536 | tf_op jit(solution)/shard_map/all_to_all | solution.py:321
  58.5 0.0 collective-permute-done.4.before_ref
  58.5 3.9 %temporal.2 = (bf16[512,640]{1,0:T(8,128)(2,1)S(1)}, bf16[512,640]{1,0:T(8,128)(2,1)S(1)}) custom-call(f32[1024,320]{1,0:T(8,128)S(1)} %get-tuple-element.21.hidden_ref.after_ref, bf16[256,640]{1,0:T(8,128)(2,1)S(1)} %collective-permute-done.4.before_ref, bf16[256,640]{1,0:T(8,128)(2,1)S(1)} %collective-permute-done.5.next_ref, f32[64,128]{1,0:T(8,128)S(1)} %bitcast.18, ...), custom_call_target="tpu_custom_call" | custom-call | flops 1258291200 | bytes 1228800 | tf_op jit(solution)/shard_map/temporal/pallas_call | solution.py:201
  62.4 3.3 %collective-permute-start.6 = (bf16[512,640]{1,0:T(8,128)(2,1)S(1)}, bf16[512,640]{1,0:T(8,128)(2,1)S(1)}, u32[]{:S(2)}, u32[]{:S(2)}) collective-permute-start(bf16[512,640]{1,0:T(8,128)(2,1)S(1)} %get-tuple-element.26), channel_id=1, source_target_pairs={{0,1},{1,0},{2,3},{3,2},{4,5},{5,4},{6,7},{7,6},{8,9},{9,8},{10,11... | collective-permute-start | bytes 1966088 | tf_op jit(solution)/shard_map/ppermute | solution.py:300
  65.7 1.7 %collective-permute-done.6.got_ref = bf16[512,640]{1,0:T(8,128)(2,1)S(1)} collective-permute-done((bf16[512,640]{1,0:T(8,128)(2,1)S(1)}, bf16[512,640]{1,0:T(8,128)(2,1)S(1)}, u32[]{:S(2)}, u32[]{:S(2)}) %collective-permute-start.6) | collective-permute-done | bytes 655392 | tf_op jit(solution)/shard_map/ppermute | solution.py:300
  67.4 0.2 chip_sum.3.after_ref
  67.5 2.7 %collective-permute-start.9 = (bf16[512,640]{1,0:T(8,128)(2,1)S(1)}, bf16[512,640]{1,0:T(8,128)(2,1)S(1)}, u32[]{:S(2)}, u32[]{:S(2)}) collective-permute-start(bf16[512,640]{1,0:T(8,128)(2,1)S(1)} %chip_sum.3.after_ref), channel_id=1, source_target_pairs={{0,2},{2,0},{1,3},{3,1},{4,6},{6,4},{5,7},{7,5},{8,10},{10,8},{9,1... | collective-permute-start | bytes 1966088 | tf_op jit(solution)/shard_map/ppermute | solution.py:300
  70.3 3.6 %temporal.3 = (bf16[512,640]{1,0:T(8,128)(2,1)S(1)}, bf16[512,640]{1,0:T(8,128)(2,1)S(1)}) custom-call(f32[1024,320]{1,0:T(8,128)S(1)} %get-tuple-element.21.hidden_ref.after_ref, bf16[256,640]{1,0:T(8,128)(2,1)S(1)} %collective-permute-done.4.before_ref, bf16[256,640]{1,0:T(8,128)(2,1)S(1)} %collective-permute-done.5.next_ref, f32[64,128]{1,0:T(8,128)S(1)} %bitcast.19, ...), custom_call_target="tpu_custom_call" | custom-call | flops 1258291200 | bytes 1228800 | tf_op jit(solution)/shard_map/temporal/pallas_call | solution.py:201
  73.9 0.1 fusion
  74.0 0.7 collective-permute-start.8
  74.7 0.1 collective-permute-start.7
  75.4 0.5 collective-permute-done.8.refs_1_
  75.9 0.5 collective-permute-done.7.refs_0_
  76.4 8.7 %collective-permute-done.9.refs_2_ = bf16[512,640]{1,0:T(8,128)(2,1)S(1)} collective-permute-done((bf16[512,640]{1,0:T(8,128)(2,1)S(1)}, bf16[512,640]{1,0:T(8,128)(2,1)S(1)}, u32[]{:S(2)}, u32[]{:S(2)}) %collective-permute-start.9) | collective-permute-done | bytes 655392 | tf_op jit(solution)/shard_map/ppermute | solution.py:300
  85.1 1.6 %blend.1 = bf16[1024,320]{1,0:T(8,128)(2,1)} custom-call(f32[1]{0:T(128)S(6)} %copy.6.mix_ref, f32[1024,320]{1,0:T(8,128)S(1)} %get-tuple-element.21.hidden_ref.after_ref, bf16[512,640]{1,0:T(8,128)(2,1)S(1)} %get-tuple-element.27.own_ref, bf16[256,640]{1,0:T(8,128)(2,1)S(1)} %collective-permute-done.7.refs_0_, ...), custom_call_target="tpu_custom_call" | custom-call | flops 983040 | bytes 2621440 | tf_op jit(solution)/shard_map/blend/pallas_call | solution.py:287
  (3 shorter events, 0.0 us)
Async XLA Ops:
  8.1 5.0 %collective-permute-start = (bf16[512,640]{1,0:T(8,128)(2,1)S(1)}, bf16[512,640]{1,0:T(8,128)(2,1)S(1)}, u32[]{:S(2)}, u32[]{:S(2)}) collective-permute-start(bf16[512,640]{1,0:T(8,128)(2,1)S(1)} %get-tuple-element.18), channel_id=1, source_target_pairs={{0,1},{1,0},{2,3},{3,2},{4,5},{5,4},{6,7},{7,6},{8,9},{9,8},{10,11... | collective-permute-start | bytes 1966088 | tf_op jit(solution)/shard_map/ppermute | solution.py:300
  13.3 17.7 %copy-start.1 = (bf16[2,320,16,32]{1,3,2,0:T(8,128)(2,1)S(1)}, bf16[2,320,16,32]{1,3,2,0:T(8,128)(2,1)}, u32[]{:S(2)}) copy-start(bf16[2,320,16,32]{1,3,2,0:T(8,128)(2,1)} %param.4) | copy-start | bytes 1966084
  13.3 17.7 %collective-permute-start.3 = (bf16[512,640]{1,0:T(8,128)(2,1)S(1)}, bf16[512,640]{1,0:T(8,128)(2,1)S(1)}, u32[]{:S(2)}, u32[]{:S(2)}) collective-permute-start(bf16[512,640]{1,0:T(8,128)(2,1)S(1)} %chip_sum.2.after_ref), channel_id=1, source_target_pairs={{0,2},{2,0},{1,3},{3,1},{4,6},{6,4},{5,7},{7,5},{8,10},{10,8},{9,1... | collective-permute-start | bytes 1966088 | tf_op jit(solution)/shard_map/ppermute | solution.py:300
  22.9 35.7 %copy-start = (bf16[3,320,1280]{2,1,0:T(8,128)(2,1)S(1)}, bf16[3,320,1280]{2,1,0:T(8,128)(2,1)}, u32[]{:S(2)}) copy-start(bf16[3,320,1280]{2,1,0:T(8,128)(2,1)} %param.6) | copy-start | bytes 7372804
  22.9 2.0 %collective-permute-start.2 = (bf16[256,640]{1,0:T(8,128)(2,1)S(1)}, bf16[256,640]{1,0:T(8,128)(2,1)S(1)}, u32[]{:S(2)}, u32[]{:S(2)}) collective-permute-start(bf16[256,640]{1,0:T(8,128)(2,1)S(1)} %get-tuple-element.31), channel_id=1, source_target_pairs={{0,1},{1,0},{2,3},{3,2},{4,5},{5,4},{6,7},{7,6},{8,9},{9,8},{10,11... | collective-permute-start | bytes 983048 | tf_op jit(solution)/shard_map/ppermute | solution.py:300
  23.7 1.7 %collective-permute-start.1 = (bf16[256,640]{1,0:T(8,128)(2,1)S(1)}, bf16[256,640]{1,0:T(8,128)(2,1)S(1)}, u32[]{:S(2)}, u32[]{:S(2)}) collective-permute-start(bf16[256,640]{1,0:T(8,128)(2,1)S(1)} %get-tuple-element.32), channel_id=1, source_target_pairs={{0,1},{1,0},{2,3},{3,2},{4,5},{5,4},{6,7},{7,6},{8,9},{9,8},{10,11... | collective-permute-start | bytes 983048 | tf_op jit(solution)/shard_map/ppermute | solution.py:300
  32.0 26.5 %collective-permute-start.4 = (bf16[256,640]{1,0:T(8,128)(2,1)S(1)}, bf16[256,640]{1,0:T(8,128)(2,1)S(1)}, u32[]{:S(2)}, u32[]{:S(2)}) collective-permute-start(bf16[256,640]{1,0:T(8,128)(2,1)S(1)} %get-tuple-element.22), channel_id=1, source_target_pairs={{0,4},{4,8},{8,12},{12,16},{16,20},{20,24},{24,28},{28,32},{32,36}... | collective-permute-start | bytes 983048 | tf_op jit(solution)/shard_map/ppermute | solution.py:320
  33.9 24.7 %collective-permute-start.5 = (bf16[256,640]{1,0:T(8,128)(2,1)S(1)}, bf16[256,640]{1,0:T(8,128)(2,1)S(1)}, u32[]{:S(2)}, u32[]{:S(2)}) collective-permute-start(bf16[256,640]{1,0:T(8,128)(2,1)S(1)} %get-tuple-element.23), channel_id=1, source_target_pairs={{4,0},{8,4},{12,8},{16,12},{20,16},{24,20},{28,24},{32,28},{36,32}... | collective-permute-start | bytes 983048 | tf_op jit(solution)/shard_map/ppermute | solution.py:319
  62.4 5.0 %collective-permute-start.6 = (bf16[512,640]{1,0:T(8,128)(2,1)S(1)}, bf16[512,640]{1,0:T(8,128)(2,1)S(1)}, u32[]{:S(2)}, u32[]{:S(2)}) collective-permute-start(bf16[512,640]{1,0:T(8,128)(2,1)S(1)} %get-tuple-element.26), channel_id=1, source_target_pairs={{0,1},{1,0},{2,3},{3,2},{4,5},{5,4},{6,7},{7,6},{8,9},{9,8},{10,11... | collective-permute-start | bytes 1966088 | tf_op jit(solution)/shard_map/ppermute | solution.py:300
  67.5 17.5 %collective-permute-start.9 = (bf16[512,640]{1,0:T(8,128)(2,1)S(1)}, bf16[512,640]{1,0:T(8,128)(2,1)S(1)}, u32[]{:S(2)}, u32[]{:S(2)}) collective-permute-start(bf16[512,640]{1,0:T(8,128)(2,1)S(1)} %chip_sum.3.after_ref), channel_id=1, source_target_pairs={{0,2},{2,0},{1,3},{3,1},{4,6},{6,4},{5,7},{7,5},{8,10},{10,8},{9,1... | collective-permute-start | bytes 1966088 | tf_op jit(solution)/shard_map/ppermute | solution.py:300
  74.0 2.0 %collective-permute-start.8 = (bf16[256,640]{1,0:T(8,128)(2,1)S(1)}, bf16[256,640]{1,0:T(8,128)(2,1)S(1)}, u32[]{:S(2)}, u32[]{:S(2)}) collective-permute-start(bf16[256,640]{1,0:T(8,128)(2,1)S(1)} %get-tuple-element.29), channel_id=1, source_target_pairs={{0,1},{1,0},{2,3},{3,2},{4,5},{5,4},{6,7},{7,6},{8,9},{9,8},{10,11... | collective-permute-start | bytes 983048 | tf_op jit(solution)/shard_map/ppermute | solution.py:300
  74.7 1.7 %collective-permute-start.7 = (bf16[256,640]{1,0:T(8,128)(2,1)S(1)}, bf16[256,640]{1,0:T(8,128)(2,1)S(1)}, u32[]{:S(2)}, u32[]{:S(2)}) collective-permute-start(bf16[256,640]{1,0:T(8,128)(2,1)S(1)} %get-tuple-element.30), channel_id=1, source_target_pairs={{0,1},{1,0},{2,3},{3,2},{4,5},{5,4},{6,7},{7,6},{8,9},{9,8},{10,11... | collective-permute-start | bytes 983048 | tf_op jit(solution)/shard_map/ppermute | solution.py:300

commit v3 on v2

--- a/solution.py
+++ b/solution.py
@@ -22,8 +22,9 @@
 
 CORE_SWAP = [(0, 1), (1, 0), (2, 3), (3, 2)]
 HALF_SWAP = [(0, 2), (2, 0), (1, 3), (3, 1)]
+FIRST = 256
+REST = LOCAL - FIRST
 CORE_PIECES = 2
-HALF_PIECES = 1
 VMEM_LIMIT = 40 * 1024 * 1024
 BF16 = jnp.bfloat16
 F32 = jnp.float32
@@ -73,38 +74,81 @@
     return jnp.concatenate([ref[:, :LOCAL], ref[:, LOCAL:]], axis=0)
 
 
-def split_cores(total_ref, send_ref, own_ref):
+def copy_columns(other, weight_hbm, weight_ref, sems):
+    half = lax.axis_index("ch") // 2
+    away, home = (1 - half) * HALF, half * HALF
+    if other:
+        pieces = [(away, 0, FIRST), (away + HALF - FIRST, FIRST, FIRST)]
+    else:
+        pieces = [(away + FIRST, 0, 2 * REST), (home, 2 * REST, HALF)]
+    copies = []
+    for tap in range(weight_hbm.shape[0]):
+        copies.append([])
+        for i, (start, to, width) in enumerate(pieces):
+            source = weight_hbm.at[tap, :, pl.ds(pl.multiple_of(start, 128), width)]
+            copy = pltpu.make_async_copy(source, weight_ref.at[tap, :, to : to + width], sems.at[tap, i])
+            copy.start()
+            copies[-1].append(copy)
+    return copies
+
+
+def split_first(total_ref, send_ref, own_ref):
     core = lax.axis_index("ch") % 2
 
     def copy(ref, first):
         for frame in range(2):
-            ref[:, frame * LOCAL : (frame + 1) * LOCAL] = total_ref[frame, :, first : first + LOCAL]
+            ref[frame * PX : (frame + 1) * PX] = total_ref[frame, :, first : first + FIRST]
 
     @pl.when(core == 0)
     def _():
         copy(own_ref, 0)
-        copy(send_ref, LOCAL)
+        copy(send_ref, FIRST)
 
     @pl.when(core == 1)
     def _():
-        copy(own_ref, LOCAL)
+        copy(own_ref, FIRST)
         copy(send_ref, 0)
 
 
-def half_columns(other):
-    half = lax.axis_index("ch") // 2
-    half = 1 - half if other else half
-    return pl.ds(pl.multiple_of(half * HALF, HALF), HALF)
-
-
-def spatial_kernel(other, lat_hbm, weight_hbm, after_ref, send_ref, own_ref, lat_ref, weight_ref, taps_ref, total_ref, sems):
-    copies = [pltpu.make_async_copy(lat_hbm, lat_ref, sems.at[TAPS])]
-    for row_tap in range(TAPS):
-        source = weight_hbm.at[row_tap, :, half_columns(other)]
-        copies.append(pltpu.make_async_copy(source, weight_ref.at[row_tap], sems.at[row_tap]))
-    for copy in copies:
-        copy.start()
-    copies[0].wait()
+def split_second(total_ref, send_rest, own_rest, send_ref, own_ref):
+    core = lax.axis_index("ch") % 2
+
+    def copy(ref, first, width):
+        for frame in range(2):
+            ref[:, frame * width : (frame + 1) * width] = total_ref[frame, :, first : first + width]
+
+    @pl.when(core == 0)
+    def _():
+        copy(own_rest, 0, REST)
+        copy(send_rest, REST, REST)
+        copy(own_ref, 2 * REST, LOCAL)
+        copy(send_ref, 2 * REST + LOCAL, LOCAL)
+
+    @pl.when(core == 1)
+    def _():
+        copy(own_rest, REST, REST)
+        copy(send_rest, 0, REST)
+        copy(own_ref, 2 * REST + LOCAL, LOCAL)
+        copy(send_ref, 2 * REST, LOCAL)
+
+
+def part_shapes(other):
+    if other:
+        return [jax.ShapeDtypeStruct((2 * PX, FIRST), BF16)] * 2
+    rest, own = jax.ShapeDtypeStruct((PX, 2 * REST), BF16), jax.ShapeDtypeStruct((PX, 2 * LOCAL), BF16)
+    return [rest, rest, own, own]
+
+
+def part_columns(other):
+    return 2 * FIRST if other else 2 * REST + HALF
+
+
+def spatial_kernel(other, lat_hbm, weight_hbm, after_ref, *refs):
+    *outs, lat_ref, weight_ref, taps_ref, total_ref, lat_sem, sems = refs
+    lat_copy = pltpu.make_async_copy(lat_hbm, lat_ref, lat_sem)
+    lat_copy.start()
+    copies = copy_columns(other, weight_hbm, weight_ref, sems)
+    lat_copy.wait()
 
     rows = []
     for frame in range(2):
@@ -131,7 +175,7 @@
         taps_ref[frame, inside, LOCAL : 2 * LOCAL] = act.astype(BF16)
         taps_ref[frame, inside, 2 * LOCAL :] = jnp.concatenate(right, axis=0).astype(BF16)
 
-    for copy in copies[1:]:
+    for copy in sum(copies, []):
         copy.wait()
     for frame in range(2):
         total = None
@@ -140,39 +184,38 @@
             term = jnp.dot(taps_ref[frame, cells], weight_ref[row_tap], preferred_element_type=F32)
             total = term if total is None else total + term
         total_ref[frame] = total.astype(BF16)
-    split_cores(total_ref, send_ref, own_ref)
+    (split_first if other else split_second)(total_ref, *outs)
 
 
 def spatial_call(lat, weight, after, other):
-    shape = jax.ShapeDtypeStruct((PX, 2 * LOCAL), BF16)
     vmem, hbm = pl.BlockSpec(memory_space=pltpu.VMEM), pl.BlockSpec(memory_space=pltpu.HBM)
+    shapes, columns = part_shapes(other), part_columns(other)
     return pl.pallas_call(
         functools.partial(spatial_kernel, other),
         in_specs=[hbm, hbm, pl.BlockSpec(memory_space=pl.ANY)],
-        out_specs=[vmem, vmem],
-        out_shape=[shape, shape],
+        out_specs=[vmem] * len(shapes),
+        out_shape=shapes,
         scratch_shapes=[
             pltpu.VMEM((2 * PX, LOCAL), BF16),
-            pltpu.VMEM((TAPS, WIDE, HALF), BF16),
+            pltpu.VMEM((TAPS, WIDE, columns), BF16),
             pltpu.VMEM((2, PX + 2 * COLS, WIDE), BF16),
-            pltpu.VMEM((2, PX, HALF), BF16),
-            pltpu.SemaphoreType.DMA((TAPS + 1,)),
+            pltpu.VMEM((2, PX, columns), BF16),
+            pltpu.SemaphoreType.DMA,
+            pltpu.SemaphoreType.DMA((TAPS, 2)),
         ],
         compiler_params=params(),
         cost_estimate=pl.CostEstimate(
-            flops=4 * PX * TAPS * WIDE * HALF,
-            bytes_accessed=2 * TAPS * WIDE * HALF,
+            flops=4 * PX * TAPS * WIDE * columns,
+            bytes_accessed=2 * TAPS * WIDE * columns,
             transcendentals=2 * PX * LOCAL,
         ),
         name="spatial",
     )(lat, weight, after)
 
 
-def temporal_kernel(
-    other, hidden_ref, before_ref, next_ref, stats_ref, weight_hbm, after_ref, send_ref, own_ref, weight_ref, taps_ref, total_ref, sem
-):
-    copy = pltpu.make_async_copy(weight_hbm.at[:, half_columns(other)], weight_ref, sem)
-    copy.start()
+def temporal_kernel(other, hidden_ref, before_ref, next_ref, stats_ref, weight_hbm, after_ref, *refs):
+    *outs, weight_ref, taps_ref, total_ref, sems = refs
+    copies = copy_columns(other, weight_hbm, weight_ref, sems)
     seq, size = lax.axis_index("seq"), lax.axis_size("seq")
     sums = jnp.sum(stats_ref[...], axis=0, keepdims=True) * (1.0 / (GROUP * 2 * PX * size))
     sums = jnp.broadcast_to(sums, (8, 128))
@@ -189,30 +232,31 @@
     for frame in range(2):
         for tap in range(TAPS):
             taps_ref[frame, :, tap * LOCAL : (tap + 1) * LOCAL] = frames[frame + tap].astype(BF16)
-    copy.wait()
-    for frame in range(2):
-        total_ref[frame] = jnp.dot(taps_ref[frame], weight_ref[...], preferred_element_type=F32).astype(BF16)
-    split_cores(total_ref, send_ref, own_ref)
+    for copy in copies[0]:
+        copy.wait()
+    for frame in range(2):
+        total_ref[frame] = jnp.dot(taps_ref[frame], weight_ref[0], preferred_element_type=F32).astype(BF16)
+    (split_first if other else split_second)(total_ref, *outs)
 
 
 def temporal_call(hidden, before, next_, stats, weight, after, other):
-    shape = jax.ShapeDtypeStruct((PX, 2 * LOCAL), BF16)
     vmem = pl.BlockSpec(memory_space=pltpu.VMEM)
+    shapes, columns = part_shapes(other), part_columns(other)
     return pl.pallas_call(
         functools.partial(temporal_kernel, other),
         in_specs=[vmem] * 4 + [pl.BlockSpec(memory_space=pl.ANY)] * 2,
-        out_specs=[vmem, vmem],
-        out_shape=[shape, shape],
+        out_specs=[vmem] * len(shapes),
+        out_shape=shapes,
         scratch_shapes=[
-            pltpu.VMEM((WIDE, HALF), BF16),
+            pltpu.VMEM((1, WIDE, columns), BF16),
             pltpu.VMEM((2, PX, WIDE), BF16),
-            pltpu.VMEM((2, PX, HALF), BF16),
-            pltpu.SemaphoreType.DMA,
+            pltpu.VMEM((2, PX, columns), BF16),
+            pltpu.SemaphoreType.DMA((1, 2)),
         ],
         compiler_params=params(),
         cost_estimate=pl.CostEstimate(
-            flops=4 * PX * WIDE * HALF,
-            bytes_accessed=2 * WIDE * HALF,
+            flops=4 * PX * WIDE * columns,
+            bytes_accessed=2 * WIDE * columns,
             transcendentals=4 * PX * LOCAL,
         ),
         name="temporal",
@@ -226,27 +270,32 @@
 def chip_sum(own, got):
     return pl.pallas_call(
         chip_sum_kernel,
-        out_shape=jax.ShapeDtypeStruct((PX, 2 * LOCAL), BF16),
+        out_shape=jax.ShapeDtypeStruct(own.shape, BF16),
         compiler_params=params(),
-        cost_estimate=pl.CostEstimate(flops=2 * PX * LOCAL, bytes_accessed=12 * PX * LOCAL, transcendentals=0),
+        cost_estimate=pl.CostEstimate(flops=own.size, bytes_accessed=6 * own.size, transcendentals=0),
         name="chip_sum",
     )(own, got)
 
 
-def three_sums(own_ref, core_refs, half_refs, frame):
+def three_sums(own_ref, core_refs, first_ref, rest_ref, frame):
     cols = slice(frame * LOCAL, (frame + 1) * LOCAL)
     core = jnp.concatenate([ref[:, cols] for ref in core_refs], axis=0)
-    half = jnp.concatenate([ref[:, cols] for ref in half_refs], axis=0)
-    return own_ref[:, cols].astype(F32) + core.astype(F32) + half.astype(F32)
+    first = first_ref[frame * PX : (frame + 1) * PX].astype(F32)
+    rest = rest_ref[:, frame * REST : (frame + 1) * REST].astype(F32)
+    half = jnp.where(
+        lax.axis_index("ch") % 2 == 0,
+        jnp.concatenate([first, rest], axis=1),
+        jnp.concatenate([rest, first], axis=1),
+    )
+    return own_ref[:, cols].astype(F32) + core.astype(F32) + half
 
 
 def hidden_kernel(lat_ref, own_ref, *refs):
-    cores, halves = refs[:CORE_PIECES], refs[CORE_PIECES : CORE_PIECES + HALF_PIECES]
-    hidden_ref, first_ref, last_ref, stats_ref = refs[CORE_PIECES + HALF_PIECES :]
+    *cores, half_first, half_rest, hidden_ref, first_ref, last_ref, stats_ref = refs
     sums, squares = 0.0, 0.0
     for frame, edge in enumerate((first_ref, last_ref)):
         cells = slice(frame * PX, (frame + 1) * PX)
-        hidden = lat_ref[cells].astype(F32) + three_sums(own_ref, cores, halves, frame)
+        hidden = lat_ref[cells].astype(F32) + three_sums(own_ref, cores, half_first, half_rest, frame)
         hidden_ref[cells] = hidden
         edge[...] = pack(hidden).astype(BF16)
         sums += jnp.sum(hidden, axis=0, keepdims=True)
@@ -273,12 +322,12 @@
 
 
 def blend_kernel(mix_ref, hidden_ref, own_ref, *refs):
-    cores, halves, out_ref = refs[:CORE_PIECES], refs[CORE_PIECES:-1], refs[-1]
+    *cores, half_first, half_rest, out_ref = refs
     mix = jnp.full((1, LOCAL), mix_ref[0], F32)
     weight = 1.0 - jax.nn.sigmoid(mix)
     for frame in range(2):
         cells = slice(frame * PX, (frame + 1) * PX)
-        branch = three_sums(own_ref, cores, halves, frame).astype(BF16).astype(F32)
+        branch = three_sums(own_ref, cores, half_first, half_rest, frame).astype(BF16).astype(F32)
         out_ref[cells] = (hidden_ref[cells] + weight * branch).astype(BF16)
 
 
@@ -286,7 +335,7 @@
     whole = pl.BlockSpec(memory_space=pltpu.VMEM)
     return pl.pallas_call(
         blend_kernel,
-        in_specs=[pl.BlockSpec(memory_space=pltpu.SMEM)] + [whole] * (2 + CORE_PIECES + HALF_PIECES),
+        in_specs=[pl.BlockSpec(memory_space=pltpu.SMEM)] + [whole] * (4 + CORE_PIECES),
         out_specs=whole,
         out_shape=jax.ShapeDtypeStruct((2 * PX, LOCAL), BF16),
         compiler_params=params(),
@@ -295,17 +344,35 @@
     )(mix, hidden, *shares)
 
 
-def permute(array, perm, pieces):
+def to_core(array, pieces=1):
     rows = array.shape[0] // pieces
-    return [lax.ppermute(array[i * rows : (i + 1) * rows], "ch", perm) for i in range(pieces)]
+    return [lax.ppermute(array[i * rows : (i + 1) * rows], "ch", CORE_SWAP) for i in range(pieces)]
+
+
+def to_half(array):
+    return lax.ppermute(array, "ch", HALF_SWAP)
+
+
+def settle(array):
+    return pl.pallas_call(
+        lambda in_ref, out_ref: None,
+        in_specs=[pl.BlockSpec(memory_space=pl.ANY)],
+        out_specs=pl.BlockSpec(memory_space=pl.ANY),
+        out_shape=jax.ShapeDtypeStruct(array.shape, array.dtype),
+        input_output_aliases={0: 0},
+        compiler_params=pltpu.CompilerParams(vmem_limit_bytes=1024 * 1024),
+        cost_estimate=pl.CostEstimate(flops=10**10, bytes_accessed=0, transcendentals=0),
+        name="settle",
+    )(array)
 
 
 def reduce_channels(conv, after):
     send, own = conv(after, True)
-    chip = chip_sum(own, permute(send, CORE_SWAP, 1)[0])
-    halves = permute(chip, HALF_SWAP, HALF_PIECES)
-    send, own = conv(chip, False)
-    return own, *permute(send, CORE_SWAP, CORE_PIECES), *halves
+    first = chip_sum(own, *to_core(send))
+    half_first = settle(to_half(first))
+    send_rest, own_rest, send, own = conv(first, False)
+    half_rest = to_half(chip_sum(own_rest, *to_core(send_rest)))
+    return own, *to_core(send, CORE_PIECES), half_first, half_rest
 
 
 def per_device(latents, spatial_weight, temporal_weight, mix_factor):
@@ -313,7 +380,7 @@
     lat = latents.transpose(0, 2, 3, 1).reshape(2 * PX, LOCAL)
     lat_hbm = pltpu.with_memory_space_constraint(lat, pltpu.HBM)
     weight_s = pltpu.with_memory_space_constraint(spatial_weight.reshape(TAPS, WIDE, CH), pltpu.HBM)
-    weight_t = temporal_weight.reshape(WIDE, CH)
+    weight_t = temporal_weight.reshape(1, WIDE, CH)
     shares = reduce_channels(functools.partial(spatial_call, lat_hbm, weight_s), lat_hbm)
     hidden, first, last, stats = hidden_call(lat, shares, size)
     next_ = lax.ppermute(first, "seq", [(i + 1, i) for i in range(size - 1)])

time: 86.8 us -> 84.6 us (0.975)
  starting transfers between devices: 15.5 us -> 20.6 us
  waiting for transfers between devices: 20.4 us -> 16.1 us
  Pallas kernels: 26.5 us -> 24.4 us
  blocking collectives: 23.4 us -> 22.5 us
    ppermute x8 -> x12, waiting for transfers between devices: 20.4 us -> 16.1 us  [the longest x4 12.6 us: to_half(): return lax.ppermute(array, 'ch', HALF_SWAP)]
    ppermute x8 -> x12, starting transfers between devices: 12.4 us -> 15.7 us  [the longest x8 9.4 us: to_core(): lax.ppermute(array[i * rows:(i + 1) * rows], 'ch', CORE_SWAP)]
    ppermute x1, starting transfers between devices: 1.83 us -> 3.57 us  [per_device(): before = lax.ppermute(last, 'seq', [(i, i + 1) for i in range(size - 1)])]
    pallas_call x2, Pallas kernels: 16.2 us -> 14.5 us  [spatial_call(): pl.pallas_call(functools.partial(spatial_kernel, other), in_specs=[hbm, h...]
    all_to_all x1, blocking collectives: 23.4 us -> 22.5 us  [per_device(): stats = lax.all_to_all(stats, 'seq', 0, 0, tiled=True)]
  transfers between devices with their start and end apart: 10 -> 14, of which waited for: 8 -> 8; matrix products, arithmetic and copies ran while one was open for 0% -> 0% of each run, Pallas kernels for 14% -> 14%
where the time goes in v3:
time: 84.6 us; the launch traced here: 84.4 us
  Pallas kernels  24.4 us (29%)
  blocking collectives  22.5 us (27%)
  starting transfers between devices  20.6 us (24%)
  waiting for transfers between devices  16.1 us (19%)
    all_to_all x1, blocking collectives, per_device(): stats = lax.all_to_all(stats, 'seq', 0, 0, tiled=True)  22.5 us
    pallas_call x2, Pallas kernels, spatial_call(): pl.pallas_call(functools.partial(spatial_kernel, other), in_specs=[hbm, h...  14.5 us
    ppermute x4, waiting for transfers between devices, to_half(): return lax.ppermute(array, 'ch', HALF_SWAP)  12.6 us
    ppermute x8, starting transfers between devices, to_core(): lax.ppermute(array[i * rows:(i + 1) * rows], 'ch', CORE_SWAP)  9.4 us
    pallas_call x2, Pallas kernels, temporal_call(): pl.pallas_call(functools.partial(temporal_kernel, other), in_specs=[vmem]...  6.64 us
    ppermute x4, starting transfers between devices, to_half(): return lax.ppermute(array, 'ch', HALF_SWAP)  6.29 us
    ppermute x1, starting transfers between devices, per_device(): before = lax.ppermute(last, 'seq', [(i, i + 1) for i in range(size - 1)])  3.57 us
    ppermute x8, waiting for transfers between devices, to_core(): lax.ppermute(array[i * rows:(i + 1) * rows], 'ch', CORE_SWAP)  3.56 us
  transfers between devices with their start and end apart: 14, of which 8 were waited for; matrix products, arithmetic and copies ran while one was open for 0% of the time, Pallas kernels for 14%

profile of v3, /device:TPU:1, one launch (start us, length us, event | category | flops | bytes accessed | tf_op | source)
XLA Modules:
  0.0 84.4 jit_solution(6713009801866628048)
XLA Ops:
  0.0 6.2 %spatial.2 = (bf16[1024,256]{1,0:T(8,128)(2,1)S(1)}, bf16[1024,256]{1,0:T(8,128)(2,1)S(1)}) custom-call(bf16[1024,320]{1,0:T(8,128)(2,1)} %bitcast.14, bf16[3,960,1280]{2,1,0:T(8,128)(2,1)} %bitcast.21, bf16[1024,320]{1,0:T(8,128)(2,1)} %bitcast.15), custom_call_target="tpu_custom_call" | custom-call | flops 3019898880 | bytes 2949120 | tf_op jit(solution)/shard_map/spatial/pallas_call | solution.py:193
  6.2 3.3 %collective-permute-start = (bf16[1024,256]{1,0:T(8,128)(2,1)S(1)}, bf16[1024,256]{1,0:T(8,128)(2,1)S(1)}, u32[]{:S(2)}, u32[]{:S(2)}) collective-permute-start(bf16[1024,256]{1,0:T(8,128)(2,1)S(1)} %get-tuple-element.22), channel_id=1, source_target_pairs={{0,1},{1,0},{2,3},{3,2},{4,5},{5,4},{6,7},{7,6},{8,9},{9,8},{10,11... | collective-permute-start | bytes 1572872 | tf_op jit(solution)/shard_map/ppermute | solution.py:349
  9.5 1.5 %collective-permute-done.got_ref = bf16[1024,256]{1,0:T(8,128)(2,1)S(1)} collective-permute-done((bf16[1024,256]{1,0:T(8,128)(2,1)S(1)}, bf16[1024,256]{1,0:T(8,128)(2,1)S(1)}, u32[]{:S(2)}, u32[]{:S(2)}) %collective-permute-start) | collective-permute-done | bytes 524320 | tf_op jit(solution)/shard_map/ppermute | solution.py:349
  11.1 0.1 chip_sum.4.after_ref
  11.2 1.3 %collective-permute-start.3 = (bf16[1024,256]{1,0:T(8,128)(2,1)S(1)}, bf16[1024,256]{1,0:T(8,128)(2,1)S(1)}, u32[]{:S(2)}, u32[]{:S(2)}) collective-permute-start(bf16[1024,256]{1,0:T(8,128)(2,1)S(1)} %chip_sum.4.after_ref), channel_id=1, source_target_pairs={{0,2},{2,0},{1,3},{3,1},{4,6},{6,4},{5,7},{7,5},{8,10},{10,8},{9,1... | collective-permute-start | bytes 1572872 | tf_op jit(solution)/shard_map/ppermute | solution.py:353
  12.5 8.3 %spatial.3 = (bf16[512,128]{1,0:T(8,128)(2,1)S(1)}, bf16[512,128]{1,0:T(8,128)(2,1)S(1)}, bf16[512,640]{1,0:T(8,128)(2,1)S(1)}, bf16[512,640]{1,0:T(8,128)(2,1)S(1)}) custom-call(bf16[1024,320]{1,0:T(8,128)(2,1)} %bitcast.16, bf16[3,960,1280]{2,1,0:T(8,128)(2,1)} %bitcast.22, bf16[1024,256]{1,0:T(8,128)(2,1)S(1)} %chip_sum.4.after_ref), custom_call_target="tpu_custom_call" | custom-call | flops 4529848320 | bytes 4423680 | tf_op jit(solution)/shard_map/spatial/pallas_call | solution.py:193
  20.7 0.7 collective-permute-start.4
  21.5 0.1 fusion.1
  21.5 0.3 collective-permute-start.1
  21.8 0.5 collective-permute-start.2
  22.3 0.1 collective-permute-done.4.got_ref
  22.5 1.9 %collective-permute-start.5 = (bf16[512,128]{1,0:T(8,128)(2,1)S(1)}, bf16[512,128]{1,0:T(8,128)(2,1)S(1)}, u32[]{:S(2)}, u32[]{:S(2)}) collective-permute-start(bf16[512,128]{1,0:T(8,128)(2,1)S(1)} %chip_sum.5), channel_id=1, source_target_pairs={{0,2},{2,0},{1,3},{3,1},{4,6},{6,4},{5,7},{7,5},{8,10},{10,8},{9,1... | collective-permute-start | bytes 393224 | tf_op jit(solution)/shard_map/ppermute | solution.py:353
  24.4 1.5 %collective-permute-done.3.in_ref = bf16[1024,256]{1,0:T(8,128)(2,1)S(1)} collective-permute-done((bf16[1024,256]{1,0:T(8,128)(2,1)S(1)}, bf16[1024,256]{1,0:T(8,128)(2,1)S(1)}, u32[]{:S(2)}, u32[]{:S(2)}) %collective-permute-start.3) | collective-permute-done | bytes 524320 | tf_op jit(solution)/shard_map/ppermute | solution.py:353
  25.9 2.9 %collective-permute-done.5.refs_3_ = bf16[512,128]{1,0:T(8,128)(2,1)S(1)} collective-permute-done((bf16[512,128]{1,0:T(8,128)(2,1)S(1)}, bf16[512,128]{1,0:T(8,128)(2,1)S(1)}, u32[]{:S(2)}, u32[]{:S(2)}) %collective-permute-start.5) | collective-permute-done | bytes 131104 | tf_op jit(solution)/shard_map/ppermute | solution.py:353
  28.8 1.2 %hidden.1 = (f32[1024,320]{1,0:T(8,128)S(1)}, bf16[256,640]{1,0:T(8,128)(2,1)S(1)}, bf16[256,640]{1,0:T(8,128)(2,1)S(1)}, f32[64,128]{1,0:T(8,128)S(1)}) custom-call(bf16[1024,320]{1,0:T(8,128)(2,1)S(1)} %bitcast.17, bf16[512,640]{1,0:T(8,128)(2,1)S(1)} %get-tuple-element.23.own_ref, bf16[256,640]{1,0:T(8,128)(2,1)S(1)} %collective-permute-done.1.refs_0_, ...), custom_call_target="tpu_custom_call" | custom-call | flops 1638400 | bytes 3276800 | tf_op jit(solution)/shard_map/hidden/pallas_call | solution.py:310
  30.1 3.6 %collective-permute-start.6 = (bf16[256,640]{1,0:T(8,128)(2,1)S(1)}, bf16[256,640]{1,0:T(8,128)(2,1)S(1)}, u32[]{:S(2)}, u32[]{:S(2)}) collective-permute-start(bf16[256,640]{1,0:T(8,128)(2,1)S(1)} %get-tuple-element.28), channel_id=1, source_target_pairs={{0,4},{4,8},{8,12},{12,16},{16,20},{20,24},{24,28},{28,32},{32,36}... | collective-permute-start | bytes 983048 | tf_op jit(solution)/shard_map/ppermute | solution.py:387
  33.7 1.3 %collective-permute-start.7 = (bf16[256,640]{1,0:T(8,128)(2,1)S(1)}, bf16[256,640]{1,0:T(8,128)(2,1)S(1)}, u32[]{:S(2)}, u32[]{:S(2)}) collective-permute-start(bf16[256,640]{1,0:T(8,128)(2,1)S(1)} %get-tuple-element.29), channel_id=1, source_target_pairs={{4,0},{8,4},{12,8},{16,12},{20,16},{24,20},{28,24},{32,28},{36,32}... | collective-permute-start | bytes 983048 | tf_op jit(solution)/shard_map/ppermute | solution.py:386
  35.0 22.5 %all_to_all.11 = f32[64,1,128]{2,1,0:T(1,128)S(1)} all-to-all(f32[64,1,128]{2,1,0:T(1,128)S(1)} %bitcast.20), channel_id=1, replica_groups=mesh['seq'=64,'ch'=4] {'seq'}, dimensions={0} | all-to-all | bytes 65536 | tf_op jit(solution)/shard_map/all_to_all | solution.py:388
  57.4 2.8 %temporal.2 = (bf16[1024,256]{1,0:T(8,128)(2,1)S(1)}, bf16[1024,256]{1,0:T(8,128)(2,1)S(1)}) custom-call(f32[1024,320]{1,0:T(8,128)S(1)} %get-tuple-element.27.hidden_ref.after_ref, bf16[256,640]{1,0:T(8,128)(2,1)S(1)} %collective-permute-done.6.before_ref, bf16[256,640]{1,0:T(8,128)(2,1)S(1)} %collective-permute-done.7.next_ref, f32[64,128]{1,0:T(8,128)S(1)} %bitcast.18, ...), custom_call_target="tpu_custom_call" | custom-call | flops 1006632960 | bytes 983040 | tf_op jit(solution)/shard_map/temporal/pallas_call | solution.py:245
  60.2 3.2 %collective-permute-start.8 = (bf16[1024,256]{1,0:T(8,128)(2,1)S(1)}, bf16[1024,256]{1,0:T(8,128)(2,1)S(1)}, u32[]{:S(2)}, u32[]{:S(2)}) collective-permute-start(bf16[1024,256]{1,0:T(8,128)(2,1)S(1)} %get-tuple-element.32), channel_id=1, source_target_pairs={{0,1},{1,0},{2,3},{3,2},{4,5},{5,4},{6,7},{7,6},{8,9},{9,8},{10,11... | collective-permute-start | bytes 1572872 | tf_op jit(solution)/shard_map/ppermute | solution.py:349
  63.5 1.5 %collective-permute-done.8.got_ref = bf16[1024,256]{1,0:T(8,128)(2,1)S(1)} collective-permute-done((bf16[1024,256]{1,0:T(8,128)(2,1)S(1)}, bf16[1024,256]{1,0:T(8,128)(2,1)S(1)}, u32[]{:S(2)}, u32[]{:S(2)}) %collective-permute-start.8) | collective-permute-done | bytes 524320 | tf_op jit(solution)/shard_map/ppermute | solution.py:349
  65.0 0.1 chip_sum.6.after_ref
  65.2 1.8 %collective-permute-start.11 = (bf16[1024,256]{1,0:T(8,128)(2,1)S(1)}, bf16[1024,256]{1,0:T(8,128)(2,1)S(1)}, u32[]{:S(2)}, u32[]{:S(2)}) collective-permute-start(bf16[1024,256]{1,0:T(8,128)(2,1)S(1)} %chip_sum.6.after_ref), channel_id=1, source_target_pairs={{0,2},{2,0},{1,3},{3,1},{4,6},{6,4},{5,7},{7,5},{8,10},{10,8},{9,1... | collective-permute-start | bytes 1572872 | tf_op jit(solution)/shard_map/ppermute | solution.py:353
  67.6 3.8 %temporal.3 = (bf16[512,128]{1,0:T(8,128)(2,1)S(1)}, bf16[512,128]{1,0:T(8,128)(2,1)S(1)}, bf16[512,640]{1,0:T(8,128)(2,1)S(1)}, bf16[512,640]{1,0:T(8,128)(2,1)S(1)}) custom-call(f32[1024,320]{1,0:T(8,128)S(1)} %get-tuple-element.27.hidden_ref.after_ref, bf16[256,640]{1,0:T(8,128)(2,1)S(1)} %collective-permute-done.6.before_ref, ...), custom_call_target="tpu_custom_call" | custom-call | flops 1509949440 | bytes 1474560 | tf_op jit(solution)/shard_map/temporal/pallas_call | solution.py:245
  71.4 0.7 collective-permute-start.12
  72.2 0.1 collective-permute-start.10
  72.3 0.5 collective-permute-start.9
  72.8 0.3 collective-permute-done.12.got_ref
  73.2 1.4 %collective-permute-start.13 = (bf16[512,128]{1,0:T(8,128)(2,1)S(1)}, bf16[512,128]{1,0:T(8,128)(2,1)S(1)}, u32[]{:S(2)}, u32[]{:S(2)}) collective-permute-start(bf16[512,128]{1,0:T(8,128)(2,1)S(1)} %chip_sum.7), channel_id=1, source_target_pairs={{0,2},{2,0},{1,3},{3,1},{4,6},{6,4},{5,7},{7,5},{8,10},{10,8},{9,1... | collective-permute-start | bytes 393224 | tf_op jit(solution)/shard_map/ppermute | solution.py:353
  74.6 5.3 %collective-permute-done.11.in_ref = bf16[1024,256]{1,0:T(8,128)(2,1)S(1)} collective-permute-done((bf16[1024,256]{1,0:T(8,128)(2,1)S(1)}, bf16[1024,256]{1,0:T(8,128)(2,1)S(1)}, u32[]{:S(2)}, u32[]{:S(2)}) %collective-permute-start.11) | collective-permute-done | bytes 524320 | tf_op jit(solution)/shard_map/ppermute | solution.py:353
  79.9 2.8 %collective-permute-done.13.refs_3_ = bf16[512,128]{1,0:T(8,128)(2,1)S(1)} collective-permute-done((bf16[512,128]{1,0:T(8,128)(2,1)S(1)}, bf16[512,128]{1,0:T(8,128)(2,1)S(1)}, u32[]{:S(2)}, u32[]{:S(2)}) %collective-permute-start.13) | collective-permute-done | bytes 131104 | tf_op jit(solution)/shard_map/ppermute | solution.py:353
  82.7 1.7 %blend.1 = bf16[1024,320]{1,0:T(8,128)(2,1)} custom-call(f32[1]{0:T(128)S(6)} %copy.10.mix_ref, f32[1024,320]{1,0:T(8,128)S(1)} %get-tuple-element.27.hidden_ref.after_ref, bf16[512,640]{1,0:T(8,128)(2,1)S(1)} %get-tuple-element.33.own_ref, bf16[256,640]{1,0:T(8,128)(2,1)S(1)} %collective-permute-done.9.refs_0_, ...), custom_call_target="tpu_custom_call" | custom-call | flops 983040 | bytes 2621440 | tf_op jit(solution)/shard_map/blend/pallas_call | solution.py:336
  (15 shorter events, 0.1 us)
Async XLA Ops:
  6.2 4.8 %collective-permute-start = (bf16[1024,256]{1,0:T(8,128)(2,1)S(1)}, bf16[1024,256]{1,0:T(8,128)(2,1)S(1)}, u32[]{:S(2)}, u32[]{:S(2)}) collective-permute-start(bf16[1024,256]{1,0:T(8,128)(2,1)S(1)} %get-tuple-element.22), channel_id=1, source_target_pairs={{0,1},{1,0},{2,3},{3,2},{4,5},{5,4},{6,7},{7,6},{8,9},{9,8},{10,11... | collective-permute-start | bytes 1572872 | tf_op jit(solution)/shard_map/ppermute | solution.py:349
  11.2 14.7 %collective-permute-start.3 = (bf16[1024,256]{1,0:T(8,128)(2,1)S(1)}, bf16[1024,256]{1,0:T(8,128)(2,1)S(1)}, u32[]{:S(2)}, u32[]{:S(2)}) collective-permute-start(bf16[1024,256]{1,0:T(8,128)(2,1)S(1)} %chip_sum.4.after_ref), channel_id=1, source_target_pairs={{0,2},{2,0},{1,3},{3,1},{4,6},{6,4},{5,7},{7,5},{8,10},{10,8},{9,1... | collective-permute-start | bytes 1572872 | tf_op jit(solution)/shard_map/ppermute | solution.py:353
  20.7 1.7 %collective-permute-start.4 = (bf16[512,128]{1,0:T(8,128)(2,1)S(1)}, bf16[512,128]{1,0:T(8,128)(2,1)S(1)}, u32[]{:S(2)}, u32[]{:S(2)}) collective-permute-start(bf16[512,128]{1,0:T(8,128)(2,1)S(1)} %get-tuple-element.26), channel_id=1, source_target_pairs={{0,1},{1,0},{2,3},{3,2},{4,5},{5,4},{6,7},{7,6},{8,9},{9,8},{10,11... | collective-permute-start | bytes 393224 | tf_op jit(solution)/shard_map/ppermute | solution.py:349
  21.5 7.3 %collective-permute-start.1 = (bf16[256,640]{1,0:T(8,128)(2,1)S(1)}, bf16[256,640]{1,0:T(8,128)(2,1)S(1)}, u32[]{:S(2)}, u32[]{:S(2)}) collective-permute-start(bf16[256,640]{1,0:T(8,128)(2,1)S(1)} %get-tuple-element.40), channel_id=1, source_target_pairs={{0,1},{1,0},{2,3},{3,2},{4,5},{5,4},{6,7},{7,6},{8,9},{9,8},{10,11... | collective-permute-start | bytes 983048 | tf_op jit(solution)/shard_map/ppermute | solution.py:349
  21.8 7.0 %collective-permute-start.2 = (bf16[256,640]{1,0:T(8,128)(2,1)S(1)}, bf16[256,640]{1,0:T(8,128)(2,1)S(1)}, u32[]{:S(2)}, u32[]{:S(2)}) collective-permute-start(bf16[256,640]{1,0:T(8,128)(2,1)S(1)} %get-tuple-element.39), channel_id=1, source_target_pairs={{0,1},{1,0},{2,3},{3,2},{4,5},{5,4},{6,7},{7,6},{8,9},{9,8},{10,11... | collective-permute-start | bytes 983048 | tf_op jit(solution)/shard_map/ppermute | solution.py:349
  22.5 6.3 %copy-start.1 = (bf16[2,320,16,32]{1,3,2,0:T(8,128)(2,1)S(1)}, bf16[2,320,16,32]{1,3,2,0:T(8,128)(2,1)}, u32[]{:S(2)}) copy-start(bf16[2,320,16,32]{1,3,2,0:T(8,128)(2,1)} %param.4) | copy-start | bytes 1966084
  22.5 6.3 %collective-permute-start.5 = (bf16[512,128]{1,0:T(8,128)(2,1)S(1)}, bf16[512,128]{1,0:T(8,128)(2,1)S(1)}, u32[]{:S(2)}, u32[]{:S(2)}) collective-permute-start(bf16[512,128]{1,0:T(8,128)(2,1)S(1)} %chip_sum.5), channel_id=1, source_target_pairs={{0,2},{2,0},{1,3},{3,1},{4,6},{6,4},{5,7},{7,5},{8,10},{10,8},{9,1... | collective-permute-start | bytes 393224 | tf_op jit(solution)/shard_map/ppermute | solution.py:353
  25.9 31.5 %copy-start = (bf16[3,320,1280]{2,1,0:T(8,128)(2,1)S(1)}, bf16[3,320,1280]{2,1,0:T(8,128)(2,1)}, u32[]{:S(2)}) copy-start(bf16[3,320,1280]{2,1,0:T(8,128)(2,1)} %param.6) | copy-start | bytes 7372804
  30.1 27.3 %collective-permute-start.6 = (bf16[256,640]{1,0:T(8,128)(2,1)S(1)}, bf16[256,640]{1,0:T(8,128)(2,1)S(1)}, u32[]{:S(2)}, u32[]{:S(2)}) collective-permute-start(bf16[256,640]{1,0:T(8,128)(2,1)S(1)} %get-tuple-element.28), channel_id=1, source_target_pairs={{0,4},{4,8},{8,12},{12,16},{16,20},{20,24},{24,28},{28,32},{32,36}... | collective-permute-start | bytes 983048 | tf_op jit(solution)/shard_map/ppermute | solution.py:387
  33.7 23.8 %collective-permute-start.7 = (bf16[256,640]{1,0:T(8,128)(2,1)S(1)}, bf16[256,640]{1,0:T(8,128)(2,1)S(1)}, u32[]{:S(2)}, u32[]{:S(2)}) collective-permute-start(bf16[256,640]{1,0:T(8,128)(2,1)S(1)} %get-tuple-element.29), channel_id=1, source_target_pairs={{4,0},{8,4},{12,8},{16,12},{20,16},{24,20},{28,24},{32,28},{36,32}... | collective-permute-start | bytes 983048 | tf_op jit(solution)/shard_map/ppermute | solution.py:386
  60.2 4.8 %collective-permute-start.8 = (bf16[1024,256]{1,0:T(8,128)(2,1)S(1)}, bf16[1024,256]{1,0:T(8,128)(2,1)S(1)}, u32[]{:S(2)}, u32[]{:S(2)}) collective-permute-start(bf16[1024,256]{1,0:T(8,128)(2,1)S(1)} %get-tuple-element.32), channel_id=1, source_target_pairs={{0,1},{1,0},{2,3},{3,2},{4,5},{5,4},{6,7},{7,6},{8,9},{9,8},{10,11... | collective-permute-start | bytes 1572872 | tf_op jit(solution)/shard_map/ppermute | solution.py:349
  65.2 14.7 %collective-permute-start.11 = (bf16[1024,256]{1,0:T(8,128)(2,1)S(1)}, bf16[1024,256]{1,0:T(8,128)(2,1)S(1)}, u32[]{:S(2)}, u32[]{:S(2)}) collective-permute-start(bf16[1024,256]{1,0:T(8,128)(2,1)S(1)} %chip_sum.6.after_ref), channel_id=1, source_target_pairs={{0,2},{2,0},{1,3},{3,1},{4,6},{6,4},{5,7},{7,5},{8,10},{10,8},{9,1... | collective-permute-start | bytes 1572872 | tf_op jit(solution)/shard_map/ppermute | solution.py:353
  71.4 1.7 %collective-permute-start.12 = (bf16[512,128]{1,0:T(8,128)(2,1)S(1)}, bf16[512,128]{1,0:T(8,128)(2,1)S(1)}, u32[]{:S(2)}, u32[]{:S(2)}) collective-permute-start(bf16[512,128]{1,0:T(8,128)(2,1)S(1)} %get-tuple-element.36), channel_id=1, source_target_pairs={{0,1},{1,0},{2,3},{3,2},{4,5},{5,4},{6,7},{7,6},{8,9},{9,8},{10,11... | collective-permute-start | bytes 393224 | tf_op jit(solution)/shard_map/ppermute | solution.py:349
  72.2 10.5 %collective-permute-start.10 = (bf16[256,640]{1,0:T(8,128)(2,1)S(1)}, bf16[256,640]{1,0:T(8,128)(2,1)S(1)}, u32[]{:S(2)}, u32[]{:S(2)}) collective-permute-start(bf16[256,640]{1,0:T(8,128)(2,1)S(1)} %get-tuple-element.37), channel_id=1, source_target_pairs={{0,1},{1,0},{2,3},{3,2},{4,5},{5,4},{6,7},{7,6},{8,9},{9,8},{10,11... | collective-permute-start | bytes 983048 | tf_op jit(solution)/shard_map/ppermute | solution.py:349
  72.3 10.3 %collective-permute-start.9 = (bf16[256,640]{1,0:T(8,128)(2,1)S(1)}, bf16[256,640]{1,0:T(8,128)(2,1)S(1)}, u32[]{:S(2)}, u32[]{:S(2)}) collective-permute-start(bf16[256,640]{1,0:T(8,128)(2,1)S(1)} %get-tuple-element.38), channel_id=1, source_target_pairs={{0,1},{1,0},{2,3},{3,2},{4,5},{5,4},{6,7},{7,6},{8,9},{9,8},{10,11... | collective-permute-start | bytes 983048 | tf_op jit(solution)/shard_map/ppermute | solution.py:349
  73.2 9.5 %collective-permute-start.13 = (bf16[512,128]{1,0:T(8,128)(2,1)S(1)}, bf16[512,128]{1,0:T(8,128)(2,1)S(1)}, u32[]{:S(2)}, u32[]{:S(2)}) collective-permute-start(bf16[512,128]{1,0:T(8,128)(2,1)S(1)} %chip_sum.7), channel_id=1, source_target_pairs={{0,2},{2,0},{1,3},{3,1},{4,6},{6,4},{5,7},{7,5},{8,10},{10,8},{9,1... | collective-permute-start | bytes 393224 | tf_op jit(solution)/shard_map/ppermute | solution.py:353

commit v4 on v3

--- a/solution.py
+++ b/solution.py
@@ -78,7 +78,9 @@
     half = lax.axis_index("ch") // 2
     away, home = (1 - half) * HALF, half * HALF
     if other:
-        pieces = [(away, 0, FIRST), (away + HALF - FIRST, FIRST, FIRST)]
+        core = lax.axis_index("ch") % 2
+        step = HALF - FIRST
+        pieces = [(away + core * step, 0, FIRST), (away + (1 - core) * step, FIRST, FIRST)]
     else:
         pieces = [(away + FIRST, 0, 2 * REST), (home, 2 * REST, HALF)]
     copies = []
@@ -92,22 +94,16 @@
     return copies
 
 
-def split_first(total_ref, send_ref, own_ref):
-    core = lax.axis_index("ch") % 2
-
-    def copy(ref, first):
-        for frame in range(2):
-            ref[frame * PX : (frame + 1) * PX] = total_ref[frame, :, first : first + FIRST]
-
-    @pl.when(core == 0)
-    def _():
-        copy(own_ref, 0)
-        copy(send_ref, FIRST)
-
-    @pl.when(core == 1)
-    def _():
-        copy(own_ref, FIRST)
-        copy(send_ref, 0)
+def store_sums(other, frame, total, outs, total_ref):
+    if other:
+        send_ref, own_ref = outs
+        cells = slice(frame * PX, (frame + 1) * PX)
+        own_ref[cells] = total[:, :FIRST].astype(BF16)
+        send_ref[cells] = total[:, FIRST:].astype(BF16)
+    else:
+        total_ref[frame] = total.astype(BF16)
+        if frame == 1:
+            split_second(total_ref, *outs)
 
 
 def split_second(total_ref, send_rest, own_rest, send_ref, own_ref):
@@ -143,13 +139,7 @@
     return 2 * FIRST if other else 2 * REST + HALF
 
 
-def spatial_kernel(other, lat_hbm, weight_hbm, after_ref, *refs):
-    *outs, lat_ref, weight_ref, taps_ref, total_ref, lat_sem, sems = refs
-    lat_copy = pltpu.make_async_copy(lat_hbm, lat_ref, lat_sem)
-    lat_copy.start()
-    copies = copy_columns(other, weight_hbm, weight_ref, sems)
-    lat_copy.wait()
-
+def spatial_taps(lat_ref, taps_ref):
     rows = []
     for frame in range(2):
         lat = lat_ref[frame * PX : (frame + 1) * PX].astype(F32)
@@ -158,7 +148,7 @@
     means = jnp.concatenate(rows + [jnp.zeros((4, LOCAL), F32)], axis=0)
     means = exact_dot(means, group_block()) * (1.0 / (GROUP * PX))
     col = lax.broadcasted_iota(jnp.int32, (COLS, LOCAL), 0)
-    for frame in range(2):
+    def frame_taps(frame):
         mean = means[2 * frame : 2 * frame + 1]
         var = means[2 * frame + 1 : 2 * frame + 2] - mean * mean
         lat = lat_ref[frame * PX : (frame + 1) * PX].astype(F32)
@@ -175,24 +165,36 @@
         taps_ref[frame, inside, LOCAL : 2 * LOCAL] = act.astype(BF16)
         taps_ref[frame, inside, 2 * LOCAL :] = jnp.concatenate(right, axis=0).astype(BF16)
 
+    return frame_taps
+
+
+def spatial_kernel(other, lat_hbm, weight_hbm, after_ref, *refs):
+    *outs, lat_ref, weight_ref, taps_ref, total_ref, lat_sem, sems = refs
+    lat_copy = pltpu.make_async_copy(lat_hbm, lat_ref, lat_sem)
+    lat_copy.start()
+    copies = copy_columns(other, weight_hbm, weight_ref, sems)
+    lat_copy.wait()
+    frame_taps = spatial_taps(lat_ref, taps_ref)
+    frame_taps(0)
     for copy in sum(copies, []):
         copy.wait()
     for frame in range(2):
+        if frame == 0:
+            frame_taps(1)
         total = None
         for row_tap in range(TAPS):
             cells = slice(row_tap * COLS, row_tap * COLS + PX)
             term = jnp.dot(taps_ref[frame, cells], weight_ref[row_tap], preferred_element_type=F32)
             total = term if total is None else total + term
-        total_ref[frame] = total.astype(BF16)
-    (split_first if other else split_second)(total_ref, *outs)
+        store_sums(other, frame, total, outs, total_ref)
 
 
 def spatial_call(lat, weight, after, other):
-    vmem, hbm = pl.BlockSpec(memory_space=pltpu.VMEM), pl.BlockSpec(memory_space=pltpu.HBM)
+    vmem, anywhere = pl.BlockSpec(memory_space=pltpu.VMEM), pl.BlockSpec(memory_space=pl.ANY)
     shapes, columns = part_shapes(other), part_columns(other)
     return pl.pallas_call(
         functools.partial(spatial_kernel, other),
-        in_specs=[hbm, hbm, pl.BlockSpec(memory_space=pl.ANY)],
+        in_specs=[anywhere] * 3,
         out_specs=[vmem] * len(shapes),
         out_shape=shapes,
         scratch_shapes=[
@@ -226,17 +228,20 @@
     def act(values):
         return silu((values - mean) * scale)
 
-    before = act(unpack(before_ref).astype(F32)) * jnp.where(seq == 0, 0.0, 1.0)
-    after = act(unpack(next_ref).astype(F32)) * jnp.where(seq == size - 1, 0.0, 1.0)
-    frames = [before, act(hidden_ref[:PX]), act(hidden_ref[PX:]), after]
-    for frame in range(2):
-        for tap in range(TAPS):
-            taps_ref[frame, :, tap * LOCAL : (tap + 1) * LOCAL] = frames[frame + tap].astype(BF16)
+    def put(values, *places):
+        values = values.astype(BF16)
+        for frame, tap in places:
+            taps_ref[frame, :, tap * LOCAL : (tap + 1) * LOCAL] = values
+
+    put(act(unpack(before_ref).astype(F32)) * jnp.where(seq == 0, 0.0, 1.0), (0, 0))
+    put(act(hidden_ref[:PX]), (0, 1), (1, 0))
+    put(act(hidden_ref[PX:]), (0, 2), (1, 1))
     for copy in copies[0]:
         copy.wait()
-    for frame in range(2):
-        total_ref[frame] = jnp.dot(taps_ref[frame], weight_ref[0], preferred_element_type=F32).astype(BF16)
-    (split_first if other else split_second)(total_ref, *outs)
+    put(act(unpack(next_ref).astype(F32)) * jnp.where(seq == size - 1, 0.0, 1.0), (1, 2))
+    for frame in range(2):
+        total = jnp.dot(taps_ref[frame], weight_ref[0], preferred_element_type=F32)
+        store_sums(other, frame, total, outs, total_ref)
 
 
 def temporal_call(hidden, before, next_, stats, weight, after, other):
@@ -271,31 +276,54 @@
     return pl.pallas_call(
         chip_sum_kernel,
         out_shape=jax.ShapeDtypeStruct(own.shape, BF16),
-        compiler_params=params(),
-        cost_estimate=pl.CostEstimate(flops=own.size, bytes_accessed=6 * own.size, transcendentals=0),
+        compiler_params=pltpu.CompilerParams(vmem_limit_bytes=8 * 1024 * 1024),
+        cost_estimate=pl.CostEstimate(flops=4 * 10**9, bytes_accessed=6 * own.size, transcendentals=0),
         name="chip_sum",
     )(own, got)
 
 
-def three_sums(own_ref, core_refs, first_ref, rest_ref, frame):
+def chip_part(own_ref, core_refs, frame):
     cols = slice(frame * LOCAL, (frame + 1) * LOCAL)
     core = jnp.concatenate([ref[:, cols] for ref in core_refs], axis=0)
+    return own_ref[:, cols].astype(F32) + core.astype(F32)
+
+
+def half_part(first_ref, rest_ref, frame):
     first = first_ref[frame * PX : (frame + 1) * PX].astype(F32)
     rest = rest_ref[:, frame * REST : (frame + 1) * REST].astype(F32)
-    half = jnp.where(
+    return jnp.where(
         lax.axis_index("ch") % 2 == 0,
         jnp.concatenate([first, rest], axis=1),
         jnp.concatenate([rest, first], axis=1),
     )
-    return own_ref[:, cols].astype(F32) + core.astype(F32) + half
-
-
-def hidden_kernel(lat_ref, own_ref, *refs):
-    *cores, half_first, half_rest, hidden_ref, first_ref, last_ref, stats_ref = refs
+
+
+def small_cost():
+    return pl.CostEstimate(flops=10 * PX * LOCAL, bytes_accessed=20 * PX * LOCAL, transcendentals=0)
+
+
+def base_kernel(lat_ref, own_ref, *refs):
+    *cores, base_ref = refs
+    for frame in range(2):
+        cells = slice(frame * PX, (frame + 1) * PX)
+        base_ref[cells] = lat_ref[cells].astype(F32) + chip_part(own_ref, cores, frame)
+
+
+def base_call(lat, own, cores):
+    return pl.pallas_call(
+        base_kernel,
+        out_shape=jax.ShapeDtypeStruct((2 * PX, LOCAL), F32),
+        compiler_params=params(),
+        cost_estimate=small_cost(),
+        name="base",
+    )(lat, own, *cores)
+
+
+def hidden_kernel(base_ref, half_first, half_rest, hidden_ref, first_ref, last_ref, stats_ref):
     sums, squares = 0.0, 0.0
     for frame, edge in enumerate((first_ref, last_ref)):
         cells = slice(frame * PX, (frame + 1) * PX)
-        hidden = lat_ref[cells].astype(F32) + three_sums(own_ref, cores, half_first, half_rest, frame)
+        hidden = base_ref[cells] + half_part(half_first, half_rest, frame)
         hidden_ref[cells] = hidden
         edge[...] = pack(hidden).astype(BF16)
         sums += jnp.sum(hidden, axis=0, keepdims=True)
@@ -305,7 +333,7 @@
     stats_ref[...] = jnp.broadcast_to(row[0:1], stats_ref.shape)
 
 
-def hidden_call(lat, shares, size):
+def hidden_call(base, half_first, half_rest, size):
     edge = jax.ShapeDtypeStruct((PX // 2, 2 * LOCAL), BF16)
     return pl.pallas_call(
         hidden_kernel,
@@ -316,32 +344,59 @@
             jax.ShapeDtypeStruct((size, 128), F32),
         ],
         compiler_params=params(),
-        cost_estimate=pl.CostEstimate(flops=10 * PX * LOCAL, bytes_accessed=20 * PX * LOCAL, transcendentals=0),
+        cost_estimate=small_cost(),
         name="hidden",
-    )(lat, *shares)
-
-
-def blend_kernel(mix_ref, hidden_ref, own_ref, *refs):
-    *cores, half_first, half_rest, out_ref = refs
-    mix = jnp.full((1, LOCAL), mix_ref[0], F32)
-    weight = 1.0 - jax.nn.sigmoid(mix)
+    )(base, half_first, half_rest)
+
+
+def branch_weight(mix_ref):
+    return 1.0 - jax.nn.sigmoid(jnp.full((1, LOCAL), mix_ref[0], F32))
+
+
+def mixed_kernel(mix_ref, hidden_ref, own_ref, *refs):
+    *cores, mixed_ref = refs
     for frame in range(2):
         cells = slice(frame * PX, (frame + 1) * PX)
-        branch = three_sums(own_ref, cores, half_first, half_rest, frame).astype(BF16).astype(F32)
-        out_ref[cells] = (hidden_ref[cells] + weight * branch).astype(BF16)
-
-
-def blend_call(mix, hidden, shares):
+        mixed_ref[cells] = hidden_ref[cells] + branch_weight(mix_ref) * chip_part(own_ref, cores, frame)
+
+
+def blend_kernel(mix_ref, mixed_ref, half_first, half_rest, out_hbm, out_ref, sems):
+    copies = []
+    for frame in range(2):
+        cells = slice(frame * PX, (frame + 1) * PX)
+        half = half_part(half_first, half_rest, frame)
+        out_ref[cells] = (mixed_ref[cells] + branch_weight(mix_ref) * half).astype(BF16)
+        copies.append(pltpu.make_async_copy(out_ref.at[cells], out_hbm.at[cells], sems.at[frame]))
+        copies[-1].start()
+    for copy in copies:
+        copy.wait()
+
+
+def blend_call(mix, *arrays):
     whole = pl.BlockSpec(memory_space=pltpu.VMEM)
     return pl.pallas_call(
         blend_kernel,
-        in_specs=[pl.BlockSpec(memory_space=pltpu.SMEM)] + [whole] * (4 + CORE_PIECES),
+        in_specs=[pl.BlockSpec(memory_space=pltpu.SMEM)] + [whole] * len(arrays),
+        out_specs=pl.BlockSpec(memory_space=pl.ANY),
+        out_shape=jax.ShapeDtypeStruct((2 * PX, LOCAL), BF16),
+        scratch_shapes=[pltpu.VMEM((2 * PX, LOCAL), BF16), pltpu.SemaphoreType.DMA((2,))],
+        compiler_params=params(),
+        cost_estimate=small_cost(),
+        name="blend",
+    )(mix, *arrays)
+
+
+def mix_call(kernel, mix, dtype, name, *arrays):
+    whole = pl.BlockSpec(memory_space=pltpu.VMEM)
+    return pl.pallas_call(
+        kernel,
+        in_specs=[pl.BlockSpec(memory_space=pltpu.SMEM)] + [whole] * len(arrays),
         out_specs=whole,
-        out_shape=jax.ShapeDtypeStruct((2 * PX, LOCAL), BF16),
-        compiler_params=params(),
-        cost_estimate=pl.CostEstimate(flops=6 * PX * LOCAL, bytes_accessed=16 * PX * LOCAL, transcendentals=0),
-        name="blend",
-    )(mix, hidden, *shares)
+        out_shape=jax.ShapeDtypeStruct((2 * PX, LOCAL), dtype),
+        compiler_params=params(),
+        cost_estimate=small_cost(),
+        name=name,
+    )(mix, *arrays)
 
 
 def to_core(array, pieces=1):
@@ -353,26 +408,28 @@
     return lax.ppermute(array, "ch", HALF_SWAP)
 
 
-def settle(array):
-    return pl.pallas_call(
-        lambda in_ref, out_ref: None,
-        in_specs=[pl.BlockSpec(memory_space=pl.ANY)],
-        out_specs=pl.BlockSpec(memory_space=pl.ANY),
+def settle(array, after):
+    anywhere = pl.BlockSpec(memory_space=pl.ANY)
+    return pl.pallas_call(
+        lambda in_ref, after_ref, out_ref: None,
+        in_specs=[anywhere, anywhere],
+        out_specs=anywhere,
         out_shape=jax.ShapeDtypeStruct(array.shape, array.dtype),
         input_output_aliases={0: 0},
         compiler_params=pltpu.CompilerParams(vmem_limit_bytes=1024 * 1024),
         cost_estimate=pl.CostEstimate(flops=10**10, bytes_accessed=0, transcendentals=0),
         name="settle",
-    )(array)
-
-
-def reduce_channels(conv, after):
-    send, own = conv(after, True)
-    first = chip_sum(own, *to_core(send))
-    half_first = settle(to_half(first))
-    send_rest, own_rest, send, own = conv(first, False)
+    )(array, after)
+
+
+def reduce_channels(first, second, combine):
+    send, own = first()
+    chip = chip_sum(own, *to_core(send))
+    half_first = to_half(chip)
+    send_rest, own_rest, send, own = second(chip)
     half_rest = to_half(chip_sum(own_rest, *to_core(send_rest)))
-    return own, *to_core(send, CORE_PIECES), half_first, half_rest
+    combined = combine(own, to_core(send, CORE_PIECES))
+    return combined, settle(half_first, combined), half_rest
 
 
 def per_device(latents, spatial_weight, temporal_weight, mix_factor):
@@ -381,13 +438,21 @@
     lat_hbm = pltpu.with_memory_space_constraint(lat, pltpu.HBM)
     weight_s = pltpu.with_memory_space_constraint(spatial_weight.reshape(TAPS, WIDE, CH), pltpu.HBM)
     weight_t = temporal_weight.reshape(1, WIDE, CH)
-    shares = reduce_channels(functools.partial(spatial_call, lat_hbm, weight_s), lat_hbm)
-    hidden, first, last, stats = hidden_call(lat, shares, size)
+    base, half_first, half_rest = reduce_channels(
+        lambda: spatial_call(lat_hbm, weight_s, lat_hbm, True),
+        lambda after: spatial_call(lat_hbm, weight_s, after, False),
+        lambda own, cores: base_call(lat, own, cores),
+    )
+    hidden, first, last, stats = hidden_call(base, half_first, half_rest, size)
     next_ = lax.ppermute(first, "seq", [(i + 1, i) for i in range(size - 1)])
     before = lax.ppermute(last, "seq", [(i, i + 1) for i in range(size - 1)])
     stats = lax.all_to_all(stats, "seq", 0, 0, tiled=True)
-    shares = reduce_channels(functools.partial(temporal_call, hidden, before, next_, stats, weight_t), hidden)
-    out = blend_call(mix_factor, hidden, shares)
+    mixed, half_first, half_rest = reduce_channels(
+        lambda: temporal_call(hidden, before, next_, stats, weight_t, hidden, True),
+        lambda after: temporal_call(hidden, before, next_, stats, weight_t, after, False),
+        lambda own, cores: mix_call(mixed_kernel, mix_factor, F32, "mixed", hidden, own, *cores),
+    )
+    out = blend_call(mix_factor, mixed, half_first, half_rest)
     return out.reshape(2, ROWS, COLS, LOCAL).transpose(0, 3, 1, 2)
 
 

time: 84.6 us -> 83.3 us (0.985)
    pallas_call x4 -> x6, Pallas kernels: 14.5 us -> 15.1 us  [the longest x2 14.2 us: spatial_call(): pl.pallas_call(functools.partial(spatial_kernel, other), in_specs=[anywhe...]
  transfers between devices with their start and end apart: 14 -> 14, of which waited for: 8 -> 8; matrix products, arithmetic and copies ran while one was open for 0% -> 0% of each run, Pallas kernels for 14% -> 16%
where the time goes in v4:
time: 83.3 us; the launch traced here: 83.2 us
  Pallas kernels  23.6 us (28%)
  blocking collectives  22.5 us (27%)
  starting transfers between devices  20.6 us (25%)
  waiting for transfers between devices  15.4 us (18%)
  between operations  0.91 us (1%)
    all_to_all x1, blocking collectives, per_device(): stats = lax.all_to_all(stats, 'seq', 0, 0, tiled=True)  22.5 us
    pallas_call x2, Pallas kernels, spatial_call(): pl.pallas_call(functools.partial(spatial_kernel, other), in_specs=[anywhe...  14.2 us
    ppermute x4, waiting for transfers between devices, to_half(): return lax.ppermute(array, 'ch', HALF_SWAP)  12.5 us
    ppermute x8, starting transfers between devices, to_core(): lax.ppermute(array[i * rows:(i + 1) * rows], 'ch', CORE_SWAP)  9.46 us
    ppermute x4, starting transfers between devices, to_half(): return lax.ppermute(array, 'ch', HALF_SWAP)  6.28 us
    pallas_call x2, Pallas kernels, temporal_call(): pl.pallas_call(functools.partial(temporal_kernel, other), in_specs=[vmem]...  6.07 us
    ppermute x1, starting transfers between devices, per_device(): before = lax.ppermute(last, 'seq', [(i, i + 1) for i in range(size - 1)])  3.56 us
    ppermute x8, waiting for transfers between devices, to_core(): lax.ppermute(array[i * rows:(i + 1) * rows], 'ch', CORE_SWAP)  2.91 us
  transfers between devices with their start and end apart: 14, of which 8 were waited for; matrix products, arithmetic and copies ran while one was open for 0% of the time, Pallas kernels for 16%

profile of v4, /device:TPU:1, one launch (start us, length us, event | category | flops | bytes accessed | tf_op | source)
XLA Modules:
  0.0 83.2 jit_solution(10254119499518194267)
XLA Ops:
  0.0 5.8 %spatial.2 = (bf16[1024,256]{1,0:T(8,128)(2,1)S(1)}, bf16[1024,256]{1,0:T(8,128)(2,1)S(1)}) custom-call(bf16[1024,320]{1,0:T(8,128)(2,1)} %bitcast.14, bf16[3,960,1280]{2,1,0:T(8,128)(2,1)} %bitcast.21, bf16[1024,320]{1,0:T(8,128)(2,1)} %bitcast.15), custom_call_target="tpu_custom_call" | custom-call | flops 3019898880 | bytes 2949120 | tf_op jit(solution)/shard_map/spatial/pallas_call | solution.py:195
  5.8 3.3 %collective-permute-start = (bf16[1024,256]{1,0:T(8,128)(2,1)S(1)}, bf16[1024,256]{1,0:T(8,128)(2,1)S(1)}, u32[]{:S(2)}, u32[]{:S(2)}) collective-permute-start(bf16[1024,256]{1,0:T(8,128)(2,1)S(1)} %get-tuple-element.22), channel_id=1, source_target_pairs={{0,1},{1,0},{2,3},{3,2},{4,5},{5,4},{6,7},{7,6},{8,9},{9,8},{10,11... | collective-permute-start | bytes 1572872 | tf_op jit(solution)/shard_map/ppermute | solution.py:404
  9.1 1.5 %collective-permute-done.got_ref = bf16[1024,256]{1,0:T(8,128)(2,1)S(1)} collective-permute-done((bf16[1024,256]{1,0:T(8,128)(2,1)S(1)}, bf16[1024,256]{1,0:T(8,128)(2,1)S(1)}, u32[]{:S(2)}, u32[]{:S(2)}) %collective-permute-start) | collective-permute-done | bytes 524320 | tf_op jit(solution)/shard_map/ppermute | solution.py:404
  10.7 0.1 chip_sum.4.after_ref
  10.8 1.3 %collective-permute-start.3 = (bf16[1024,256]{1,0:T(8,128)(2,1)S(1)}, bf16[1024,256]{1,0:T(8,128)(2,1)S(1)}, u32[]{:S(2)}, u32[]{:S(2)}) collective-permute-start(bf16[1024,256]{1,0:T(8,128)(2,1)S(1)} %chip_sum.4.after_ref), channel_id=1, source_target_pairs={{0,2},{2,0},{1,3},{3,1},{4,6},{6,4},{5,7},{7,5},{8,10},{10,8},{9,1... | collective-permute-start | bytes 1572872 | tf_op jit(solution)/shard_map/ppermute | solution.py:408
  12.1 8.4 %spatial.3 = (bf16[512,128]{1,0:T(8,128)(2,1)S(1)}, bf16[512,128]{1,0:T(8,128)(2,1)S(1)}, bf16[512,640]{1,0:T(8,128)(2,1)S(1)}, bf16[512,640]{1,0:T(8,128)(2,1)S(1)}) custom-call(bf16[1024,320]{1,0:T(8,128)(2,1)} %bitcast.16, bf16[3,960,1280]{2,1,0:T(8,128)(2,1)} %bitcast.22, bf16[1024,256]{1,0:T(8,128)(2,1)S(1)} %chip_sum.4.after_ref), custom_call_target="tpu_custom_call" | custom-call | flops 4529848320 | bytes 4423680 | tf_op jit(solution)/shard_map/spatial/pallas_call | solution.py:195
  20.5 0.8 collective-permute-start.4
  21.3 0.3 collective-permute-start.2
  21.6 0.5 collective-permute-start.1
  22.1 0.1 collective-permute-done.4.got_ref
  22.3 1.9 %collective-permute-start.5 = (bf16[512,128]{1,0:T(8,128)(2,1)S(1)}, bf16[512,128]{1,0:T(8,128)(2,1)S(1)}, u32[]{:S(2)}, u32[]{:S(2)}) collective-permute-start(bf16[512,128]{1,0:T(8,128)(2,1)S(1)} %chip_sum.5), channel_id=1, source_target_pairs={{0,2},{2,0},{1,3},{3,1},{4,6},{6,4},{5,7},{7,5},{8,10},{10,8},{9,1... | collective-permute-start | bytes 393224 | tf_op jit(solution)/shard_map/ppermute | solution.py:408
  24.2 0.4 base.1.after_ref.base_ref
  24.6 0.9 %collective-permute-done.3.in_ref = bf16[1024,256]{1,0:T(8,128)(2,1)S(1)} collective-permute-done((bf16[1024,256]{1,0:T(8,128)(2,1)S(1)}, bf16[1024,256]{1,0:T(8,128)(2,1)S(1)}, u32[]{:S(2)}, u32[]{:S(2)}) %collective-permute-start.3) | collective-permute-done | bytes 524320 | tf_op jit(solution)/shard_map/ppermute | solution.py:408
  25.5 3.1 %collective-permute-done.5.half_rest = bf16[512,128]{1,0:T(8,128)(2,1)S(1)} collective-permute-done((bf16[512,128]{1,0:T(8,128)(2,1)S(1)}, bf16[512,128]{1,0:T(8,128)(2,1)S(1)}, u32[]{:S(2)}, u32[]{:S(2)}) %collective-permute-start.5) | collective-permute-done | bytes 131104 | tf_op jit(solution)/shard_map/ppermute | solution.py:408
  28.6 0.9 %hidden.1 = (f32[1024,320]{1,0:T(8,128)S(1)}, bf16[256,640]{1,0:T(8,128)(2,1)S(1)}, bf16[256,640]{1,0:T(8,128)(2,1)S(1)}, f32[64,128]{1,0:T(8,128)S(1)}) custom-call(f32[1024,320]{1,0:T(8,128)S(1)} %base.1.after_ref.base_ref, bf16[1024,256]{1,0:T(8,128)(2,1)S(1)} %settle.2.half_first, bf16[512,128]{1,0:T(8,128)(2,1)S(1)} %collective-permute-done.5.half_rest), custom_call_target="tpu_custom_call" | custom-call | flops 1638400 | bytes 3276800 | tf_op jit(solution)/shard_map/hidden/pallas_call | solution.py:338
  29.5 3.6 %collective-permute-start.6 = (bf16[256,640]{1,0:T(8,128)(2,1)S(1)}, bf16[256,640]{1,0:T(8,128)(2,1)S(1)}, u32[]{:S(2)}, u32[]{:S(2)}) collective-permute-start(bf16[256,640]{1,0:T(8,128)(2,1)S(1)} %get-tuple-element.28), channel_id=1, source_target_pairs={{0,4},{4,8},{8,12},{12,16},{16,20},{20,24},{24,28},{28,32},{32,36}... | collective-permute-start | bytes 983048 | tf_op jit(solution)/shard_map/ppermute | solution.py:448
  33.1 1.3 %collective-permute-start.7 = (bf16[256,640]{1,0:T(8,128)(2,1)S(1)}, bf16[256,640]{1,0:T(8,128)(2,1)S(1)}, u32[]{:S(2)}, u32[]{:S(2)}) collective-permute-start(bf16[256,640]{1,0:T(8,128)(2,1)S(1)} %get-tuple-element.29), channel_id=1, source_target_pairs={{4,0},{8,4},{12,8},{16,12},{20,16},{24,20},{28,24},{32,28},{36,32}... | collective-permute-start | bytes 983048 | tf_op jit(solution)/shard_map/ppermute | solution.py:447
  34.4 22.5 %all_to_all.11 = f32[64,1,128]{2,1,0:T(1,128)S(1)} all-to-all(f32[64,1,128]{2,1,0:T(1,128)S(1)} %bitcast.20), channel_id=1, replica_groups=mesh['seq'=64,'ch'=4] {'seq'}, dimensions={0} | all-to-all | bytes 65536 | tf_op jit(solution)/shard_map/all_to_all | solution.py:449
  56.9 2.5 %temporal.2 = (bf16[1024,256]{1,0:T(8,128)(2,1)S(1)}, bf16[1024,256]{1,0:T(8,128)(2,1)S(1)}) custom-call(f32[1024,320]{1,0:T(8,128)S(1)} %get-tuple-element.27.hidden_ref.after_ref, bf16[256,640]{1,0:T(8,128)(2,1)S(1)} %collective-permute-done.6.before_ref, bf16[256,640]{1,0:T(8,128)(2,1)S(1)} %collective-permute-done.7.next_ref, f32[64,128]{1,0:T(8,128)S(1)} %bitcast.18, ...), custom_call_target="tpu_custom_call" | custom-call | flops 1006632960 | bytes 983040 | tf_op jit(solution)/shard_map/temporal/pallas_call | solution.py:250
  59.4 3.3 %collective-permute-start.8 = (bf16[1024,256]{1,0:T(8,128)(2,1)S(1)}, bf16[1024,256]{1,0:T(8,128)(2,1)S(1)}, u32[]{:S(2)}, u32[]{:S(2)}) collective-permute-start(bf16[1024,256]{1,0:T(8,128)(2,1)S(1)} %get-tuple-element.32), channel_id=1, source_target_pairs={{0,1},{1,0},{2,3},{3,2},{4,5},{5,4},{6,7},{7,6},{8,9},{9,8},{10,11... | collective-permute-start | bytes 1572872 | tf_op jit(solution)/shard_map/ppermute | solution.py:404
  63.3 0.9 %collective-permute-done.8.got_ref = bf16[1024,256]{1,0:T(8,128)(2,1)S(1)} collective-permute-done((bf16[1024,256]{1,0:T(8,128)(2,1)S(1)}, bf16[1024,256]{1,0:T(8,128)(2,1)S(1)}, u32[]{:S(2)}, u32[]{:S(2)}) %collective-permute-start.8) | collective-permute-done | bytes 524320 | tf_op jit(solution)/shard_map/ppermute | solution.py:404
  64.2 0.1 chip_sum.6.after_ref
  64.3 1.6 %collective-permute-start.11 = (bf16[1024,256]{1,0:T(8,128)(2,1)S(1)}, bf16[1024,256]{1,0:T(8,128)(2,1)S(1)}, u32[]{:S(2)}, u32[]{:S(2)}) collective-permute-start(bf16[1024,256]{1,0:T(8,128)(2,1)S(1)} %chip_sum.6.after_ref), channel_id=1, source_target_pairs={{0,2},{2,0},{1,3},{3,1},{4,6},{6,4},{5,7},{7,5},{8,10},{10,8},{9,1... | collective-permute-start | bytes 1572872 | tf_op jit(solution)/shard_map/ppermute | solution.py:408
  65.9 3.6 %temporal.3 = (bf16[512,128]{1,0:T(8,128)(2,1)S(1)}, bf16[512,128]{1,0:T(8,128)(2,1)S(1)}, bf16[512,640]{1,0:T(8,128)(2,1)S(1)}, bf16[512,640]{1,0:T(8,128)(2,1)S(1)}) custom-call(f32[1024,320]{1,0:T(8,128)S(1)} %get-tuple-element.27.hidden_ref.after_ref, bf16[256,640]{1,0:T(8,128)(2,1)S(1)} %collective-permute-done.6.before_ref, ...), custom_call_target="tpu_custom_call" | custom-call | flops 1509949440 | bytes 1474560 | tf_op jit(solution)/shard_map/temporal/pallas_call | solution.py:250
  69.5 0.7 collective-permute-start.12
  70.4 0.5 collective-permute-start.9
  70.9 0.3 collective-permute-done.12.got_ref
  71.3 1.5 %collective-permute-start.13 = (bf16[512,128]{1,0:T(8,128)(2,1)S(1)}, bf16[512,128]{1,0:T(8,128)(2,1)S(1)}, u32[]{:S(2)}, u32[]{:S(2)}) collective-permute-start(bf16[512,128]{1,0:T(8,128)(2,1)S(1)} %chip_sum.7), channel_id=1, source_target_pairs={{0,2},{2,0},{1,3},{3,1},{4,6},{6,4},{5,7},{7,5},{8,10},{10,8},{9,1... | collective-permute-start | bytes 393224 | tf_op jit(solution)/shard_map/ppermute | solution.py:408
  72.8 0.5 mixed.1.after_ref.mixed_ref
  73.3 5.7 %collective-permute-done.11.in_ref = bf16[1024,256]{1,0:T(8,128)(2,1)S(1)} collective-permute-done((bf16[1024,256]{1,0:T(8,128)(2,1)S(1)}, bf16[1024,256]{1,0:T(8,128)(2,1)S(1)}, u32[]{:S(2)}, u32[]{:S(2)}) %collective-permute-start.11) | collective-permute-done | bytes 524320 | tf_op jit(solution)/shard_map/ppermute | solution.py:408
  79.0 2.8 %collective-permute-done.13.half_rest = bf16[512,128]{1,0:T(8,128)(2,1)S(1)} collective-permute-done((bf16[512,128]{1,0:T(8,128)(2,1)S(1)}, bf16[512,128]{1,0:T(8,128)(2,1)S(1)}, u32[]{:S(2)}, u32[]{:S(2)}) %collective-permute-start.13) | collective-permute-done | bytes 131104 | tf_op jit(solution)/shard_map/ppermute | solution.py:408
  81.8 1.2 %blend.1 = bf16[1024,320]{1,0:T(8,128)(2,1)} custom-call(f32[1]{0:T(128)S(6)} %copy.10.mix_ref, f32[1024,320]{1,0:T(8,128)S(1)} %mixed.1.after_ref.mixed_ref, bf16[1024,256]{1,0:T(8,128)(2,1)S(1)} %settle.3.half_first, bf16[512,128]{1,0:T(8,128)(2,1)S(1)} %collective-permute-done.13.half_rest), custom_call_target="tpu_custom_call" | custom-call | flops 1638400 | bytes 3276800 | tf_op jit(solution)/shard_map/blend/pallas_call | solution.py:377
  (17 shorter events, 0.3 us)
Async XLA Ops:
  5.8 4.9 %collective-permute-start = (bf16[1024,256]{1,0:T(8,128)(2,1)S(1)}, bf16[1024,256]{1,0:T(8,128)(2,1)S(1)}, u32[]{:S(2)}, u32[]{:S(2)}) collective-permute-start(bf16[1024,256]{1,0:T(8,128)(2,1)S(1)} %get-tuple-element.22), channel_id=1, source_target_pairs={{0,1},{1,0},{2,3},{3,2},{4,5},{5,4},{6,7},{7,6},{8,9},{9,8},{10,11... | collective-permute-start | bytes 1572872 | tf_op jit(solution)/shard_map/ppermute | solution.py:404
  10.8 14.7 %collective-permute-start.3 = (bf16[1024,256]{1,0:T(8,128)(2,1)S(1)}, bf16[1024,256]{1,0:T(8,128)(2,1)S(1)}, u32[]{:S(2)}, u32[]{:S(2)}) collective-permute-start(bf16[1024,256]{1,0:T(8,128)(2,1)S(1)} %chip_sum.4.after_ref), channel_id=1, source_target_pairs={{0,2},{2,0},{1,3},{3,1},{4,6},{6,4},{5,7},{7,5},{8,10},{10,8},{9,1... | collective-permute-start | bytes 1572872 | tf_op jit(solution)/shard_map/ppermute | solution.py:408
  20.5 1.7 %collective-permute-start.4 = (bf16[512,128]{1,0:T(8,128)(2,1)S(1)}, bf16[512,128]{1,0:T(8,128)(2,1)S(1)}, u32[]{:S(2)}, u32[]{:S(2)}) collective-permute-start(bf16[512,128]{1,0:T(8,128)(2,1)S(1)} %get-tuple-element.26), channel_id=1, source_target_pairs={{0,1},{1,0},{2,3},{3,2},{4,5},{5,4},{6,7},{7,6},{8,9},{9,8},{10,11... | collective-permute-start | bytes 393224 | tf_op jit(solution)/shard_map/ppermute | solution.py:404
  21.3 2.8 %collective-permute-start.2 = (bf16[256,640]{1,0:T(8,128)(2,1)S(1)}, bf16[256,640]{1,0:T(8,128)(2,1)S(1)}, u32[]{:S(2)}, u32[]{:S(2)}) collective-permute-start(bf16[256,640]{1,0:T(8,128)(2,1)S(1)} %get-tuple-element.39), channel_id=1, source_target_pairs={{0,1},{1,0},{2,3},{3,2},{4,5},{5,4},{6,7},{7,6},{8,9},{9,8},{10,11... | collective-permute-start | bytes 983048 | tf_op jit(solution)/shard_map/ppermute | solution.py:404
  21.6 2.6 %collective-permute-start.1 = (bf16[256,640]{1,0:T(8,128)(2,1)S(1)}, bf16[256,640]{1,0:T(8,128)(2,1)S(1)}, u32[]{:S(2)}, u32[]{:S(2)}) collective-permute-start(bf16[256,640]{1,0:T(8,128)(2,1)S(1)} %get-tuple-element.40), channel_id=1, source_target_pairs={{0,1},{1,0},{2,3},{3,2},{4,5},{5,4},{6,7},{7,6},{8,9},{9,8},{10,11... | collective-permute-start | bytes 983048 | tf_op jit(solution)/shard_map/ppermute | solution.py:404
  22.2 1.9 %copy-start.1 = (bf16[2,320,16,32]{1,3,2,0:T(8,128)(2,1)S(1)}, bf16[2,320,16,32]{1,3,2,0:T(8,128)(2,1)}, u32[]{:S(2)}) copy-start(bf16[2,320,16,32]{1,3,2,0:T(8,128)(2,1)} %param.4) | copy-start | bytes 1966084
  22.3 6.3 %collective-permute-start.5 = (bf16[512,128]{1,0:T(8,128)(2,1)S(1)}, bf16[512,128]{1,0:T(8,128)(2,1)S(1)}, u32[]{:S(2)}, u32[]{:S(2)}) collective-permute-start(bf16[512,128]{1,0:T(8,128)(2,1)S(1)} %chip_sum.5), channel_id=1, source_target_pairs={{0,2},{2,0},{1,3},{3,1},{4,6},{6,4},{5,7},{7,5},{8,10},{10,8},{9,1... | collective-permute-start | bytes 393224 | tf_op jit(solution)/shard_map/ppermute | solution.py:408
  25.5 31.3 %copy-start = (bf16[3,320,1280]{2,1,0:T(8,128)(2,1)S(1)}, bf16[3,320,1280]{2,1,0:T(8,128)(2,1)}, u32[]{:S(2)}) copy-start(bf16[3,320,1280]{2,1,0:T(8,128)(2,1)} %param.6) | copy-start | bytes 7372804
  29.5 27.3 %collective-permute-start.6 = (bf16[256,640]{1,0:T(8,128)(2,1)S(1)}, bf16[256,640]{1,0:T(8,128)(2,1)S(1)}, u32[]{:S(2)}, u32[]{:S(2)}) collective-permute-start(bf16[256,640]{1,0:T(8,128)(2,1)S(1)} %get-tuple-element.28), channel_id=1, source_target_pairs={{0,4},{4,8},{8,12},{12,16},{16,20},{20,24},{24,28},{28,32},{32,36}... | collective-permute-start | bytes 983048 | tf_op jit(solution)/shard_map/ppermute | solution.py:448
  33.1 23.8 %collective-permute-start.7 = (bf16[256,640]{1,0:T(8,128)(2,1)S(1)}, bf16[256,640]{1,0:T(8,128)(2,1)S(1)}, u32[]{:S(2)}, u32[]{:S(2)}) collective-permute-start(bf16[256,640]{1,0:T(8,128)(2,1)S(1)} %get-tuple-element.29), channel_id=1, source_target_pairs={{4,0},{8,4},{12,8},{16,12},{20,16},{24,20},{28,24},{32,28},{36,32}... | collective-permute-start | bytes 983048 | tf_op jit(solution)/shard_map/ppermute | solution.py:447
  59.4 4.8 %collective-permute-start.8 = (bf16[1024,256]{1,0:T(8,128)(2,1)S(1)}, bf16[1024,256]{1,0:T(8,128)(2,1)S(1)}, u32[]{:S(2)}, u32[]{:S(2)}) collective-permute-start(bf16[1024,256]{1,0:T(8,128)(2,1)S(1)} %get-tuple-element.32), channel_id=1, source_target_pairs={{0,1},{1,0},{2,3},{3,2},{4,5},{5,4},{6,7},{7,6},{8,9},{9,8},{10,11... | collective-permute-start | bytes 1572872 | tf_op jit(solution)/shard_map/ppermute | solution.py:404
  64.3 14.7 %collective-permute-start.11 = (bf16[1024,256]{1,0:T(8,128)(2,1)S(1)}, bf16[1024,256]{1,0:T(8,128)(2,1)S(1)}, u32[]{:S(2)}, u32[]{:S(2)}) collective-permute-start(bf16[1024,256]{1,0:T(8,128)(2,1)S(1)} %chip_sum.6.after_ref), channel_id=1, source_target_pairs={{0,2},{2,0},{1,3},{3,1},{4,6},{6,4},{5,7},{7,5},{8,10},{10,8},{9,1... | collective-permute-start | bytes 1572872 | tf_op jit(solution)/shard_map/ppermute | solution.py:408
  69.5 1.7 %collective-permute-start.12 = (bf16[512,128]{1,0:T(8,128)(2,1)S(1)}, bf16[512,128]{1,0:T(8,128)(2,1)S(1)}, u32[]{:S(2)}, u32[]{:S(2)}) collective-permute-start(bf16[512,128]{1,0:T(8,128)(2,1)S(1)} %get-tuple-element.36), channel_id=1, source_target_pairs={{0,1},{1,0},{2,3},{3,2},{4,5},{5,4},{6,7},{7,6},{8,9},{9,8},{10,11... | collective-permute-start | bytes 393224 | tf_op jit(solution)/shard_map/ppermute | solution.py:404
  70.3 2.5 %collective-permute-start.10 = (bf16[256,640]{1,0:T(8,128)(2,1)S(1)}, bf16[256,640]{1,0:T(8,128)(2,1)S(1)}, u32[]{:S(2)}, u32[]{:S(2)}) collective-permute-start(bf16[256,640]{1,0:T(8,128)(2,1)S(1)} %get-tuple-element.37), channel_id=1, source_target_pairs={{0,1},{1,0},{2,3},{3,2},{4,5},{5,4},{6,7},{7,6},{8,9},{9,8},{10,11... | collective-permute-start | bytes 983048 | tf_op jit(solution)/shard_map/ppermute | solution.py:404
  70.4 2.4 %collective-permute-start.9 = (bf16[256,640]{1,0:T(8,128)(2,1)S(1)}, bf16[256,640]{1,0:T(8,128)(2,1)S(1)}, u32[]{:S(2)}, u32[]{:S(2)}) collective-permute-start(bf16[256,640]{1,0:T(8,128)(2,1)S(1)} %get-tuple-element.38), channel_id=1, source_target_pairs={{0,1},{1,0},{2,3},{3,2},{4,5},{5,4},{6,7},{7,6},{8,9},{9,8},{10,11... | collective-permute-start | bytes 983048 | tf_op jit(solution)/shard_map/ppermute | solution.py:404
  71.3 10.5 %collective-permute-start.13 = (bf16[512,128]{1,0:T(8,128)(2,1)S(1)}, bf16[512,128]{1,0:T(8,128)(2,1)S(1)}, u32[]{:S(2)}, u32[]{:S(2)}) collective-permute-start(bf16[512,128]{1,0:T(8,128)(2,1)S(1)} %chip_sum.7), channel_id=1, source_target_pairs={{0,2},{2,0},{1,3},{3,1},{4,6},{6,4},{5,7},{7,5},{8,10},{10,8},{9,1... | collective-permute-start | bytes 393224 | tf_op jit(solution)/shard_map/ppermute | solution.py:408

commit v5 on v4

--- a/solution.py
+++ b/solution.py
@@ -50,16 +50,16 @@
     return jnp.where(group_of(row) == group_of(col), 1.0, 0.0)
 
 
-def group_to_lane(shift):
+def group_to_lane():
     row = lax.broadcasted_iota(jnp.int32, (LOCAL, 128), 0)
     lane = lax.broadcasted_iota(jnp.int32, (LOCAL, 128), 1)
-    return jnp.where(group_of(row) == lane - shift, 1.0, 0.0)
-
-
-def lane_to_group(shift):
+    return jnp.where(group_of(row) == lane, 1.0, 0.0)
+
+
+def lane_to_group():
     lane = lax.broadcasted_iota(jnp.int32, (128, LOCAL), 0)
     col = lax.broadcasted_iota(jnp.int32, (128, LOCAL), 1)
-    return jnp.where(group_of(col) == lane - shift, 1.0, 0.0)
+    return jnp.where(group_of(col) == lane, 1.0, 0.0)
 
 
 def exact_dot(a, b):
@@ -215,14 +215,15 @@
     )(lat, weight, after)
 
 
-def temporal_kernel(other, hidden_ref, before_ref, next_ref, stats_ref, weight_hbm, after_ref, *refs):
+def temporal_kernel(other, hidden_ref, across_ref, pair_ref, stats_ref, weight_hbm, after_ref, *refs):
     *outs, weight_ref, taps_ref, total_ref, sems = refs
     copies = copy_columns(other, weight_hbm, weight_ref, sems)
     seq, size = lax.axis_index("seq"), lax.axis_size("seq")
     sums = jnp.sum(stats_ref[...], axis=0, keepdims=True) * (1.0 / (GROUP * 2 * PX * size))
-    sums = jnp.broadcast_to(sums, (8, 128))
-    mean = exact_dot(sums, lane_to_group(0))[0:1]
-    var = exact_dot(sums, lane_to_group(LOCAL_GROUPS))[0:1] - mean * mean
+    squares = pltpu.roll(jnp.broadcast_to(sums, (8, 128)), 128 - LOCAL_GROUPS, 1)[0:1]
+    both = exact_dot(jnp.concatenate([sums, squares, jnp.zeros((6, 128), F32)], axis=0), lane_to_group())
+    mean = both[0:1]
+    var = both[1:2] - mean * mean
     scale = lax.rsqrt(var + EPS)
 
     def act(values):
@@ -233,18 +234,22 @@
         for frame, tap in places:
             taps_ref[frame, :, tap * LOCAL : (tap + 1) * LOCAL] = values
 
-    put(act(unpack(before_ref).astype(F32)) * jnp.where(seq == 0, 0.0, 1.0), (0, 0))
+    def halo(even_ref, odd_ref, edge):
+        values = jnp.where(seq % 2 == 0, unpack(even_ref), unpack(odd_ref))
+        return act(values.astype(F32)) * jnp.where(edge, 0.0, 1.0)
+
+    put(halo(across_ref, pair_ref, seq == 0), (0, 0))
     put(act(hidden_ref[:PX]), (0, 1), (1, 0))
     put(act(hidden_ref[PX:]), (0, 2), (1, 1))
     for copy in copies[0]:
         copy.wait()
-    put(act(unpack(next_ref).astype(F32)) * jnp.where(seq == size - 1, 0.0, 1.0), (1, 2))
+    put(halo(pair_ref, across_ref, seq == size - 1), (1, 2))
     for frame in range(2):
         total = jnp.dot(taps_ref[frame], weight_ref[0], preferred_element_type=F32)
         store_sums(other, frame, total, outs, total_ref)
 
 
-def temporal_call(hidden, before, next_, stats, weight, after, other):
+def temporal_call(hidden, halos, stats, weight, after, other):
     vmem = pl.BlockSpec(memory_space=pltpu.VMEM)
     shapes, columns = part_shapes(other), part_columns(other)
     return pl.pallas_call(
@@ -265,7 +270,7 @@
             transcendentals=4 * PX * LOCAL,
         ),
         name="temporal",
-    )(hidden, before, next_, stats, weight, after)
+    )(hidden, *halos[::-1], stats, weight, after)
 
 
 def chip_sum_kernel(own_ref, got_ref, out_ref):
@@ -319,28 +324,29 @@
     )(lat, own, *cores)
 
 
-def hidden_kernel(base_ref, half_first, half_rest, hidden_ref, first_ref, last_ref, stats_ref):
+def hidden_kernel(base_ref, half_first, half_rest, hidden_ref, edges_ref, stats_ref):
+    odd = lax.axis_index("seq") % 2
     sums, squares = 0.0, 0.0
-    for frame, edge in enumerate((first_ref, last_ref)):
+    for frame in range(2):
         cells = slice(frame * PX, (frame + 1) * PX)
         hidden = base_ref[cells] + half_part(half_first, half_rest, frame)
         hidden_ref[cells] = hidden
-        edge[...] = pack(hidden).astype(BF16)
+        slot = 1 - odd if frame == 0 else odd
+        edges_ref[pl.ds(pl.multiple_of(slot * (PX // 2), PX // 2), PX // 2)] = pack(hidden).astype(BF16)
         sums += jnp.sum(hidden, axis=0, keepdims=True)
         squares += jnp.sum(hidden * hidden, axis=0, keepdims=True)
-    row = exact_dot(jnp.broadcast_to(sums, (8, LOCAL)), group_to_lane(0))
-    row += exact_dot(jnp.broadcast_to(squares, (8, LOCAL)), group_to_lane(LOCAL_GROUPS))
-    stats_ref[...] = jnp.broadcast_to(row[0:1], stats_ref.shape)
+    both = jnp.concatenate([sums, squares, jnp.zeros((6, LOCAL), F32)], axis=0)
+    both = exact_dot(both, group_to_lane())
+    row = both[0:1] + pltpu.roll(both, LOCAL_GROUPS, 1)[1:2]
+    stats_ref[...] = jnp.broadcast_to(row, stats_ref.shape)
 
 
 def hidden_call(base, half_first, half_rest, size):
-    edge = jax.ShapeDtypeStruct((PX // 2, 2 * LOCAL), BF16)
     return pl.pallas_call(
         hidden_kernel,
         out_shape=[
             jax.ShapeDtypeStruct((2 * PX, LOCAL), F32),
-            edge,
-            edge,
+            jax.ShapeDtypeStruct((PX, 2 * LOCAL), BF16),
             jax.ShapeDtypeStruct((size, 128), F32),
         ],
         compiler_params=params(),
@@ -443,13 +449,16 @@
         lambda after: spatial_call(lat_hbm, weight_s, after, False),
         lambda own, cores: base_call(lat, own, cores),
     )
-    hidden, first, last, stats = hidden_call(base, half_first, half_rest, size)
-    next_ = lax.ppermute(first, "seq", [(i + 1, i) for i in range(size - 1)])
-    before = lax.ppermute(last, "seq", [(i, i + 1) for i in range(size - 1)])
+    hidden, edges, stats = hidden_call(base, half_first, half_rest, size)
+    halos = []
+    for start in range(2):
+        pairs = [(i, i + 1) for i in range(start, size - 1, 2)]
+        edge = edges[start * (PX // 2) : (start + 1) * (PX // 2)]
+        halos.append(lax.ppermute(edge, "seq", pairs + [(b, a) for a, b in pairs]))
     stats = lax.all_to_all(stats, "seq", 0, 0, tiled=True)
     mixed, half_first, half_rest = reduce_channels(
-        lambda: temporal_call(hidden, before, next_, stats, weight_t, hidden, True),
-        lambda after: temporal_call(hidden, before, next_, stats, weight_t, after, False),
+        lambda: temporal_call(hidden, halos, stats, weight_t, hidden, True),
+        lambda after: temporal_call(hidden, halos, stats, weight_t, after, False),
         lambda own, cores: mix_call(mixed_kernel, mix_factor, F32, "mixed", hidden, own, *cores),
     )
     out = blend_call(mix_factor, mixed, half_first, half_rest)

time: 83.3 us -> 79.9 us (0.959)
  starting transfers between devices: 20.6 us -> 18.1 us
  blocking collectives: 22.5 us -> 21.4 us
    ppermute x2, starting transfers between devices: 4.85 us -> 2.39 us  [per_device(): halos.append(lax.ppermute(edge, 'seq', pairs + [(b, a) for a, b in pairs]))]
    all_to_all x1, blocking collectives: 22.5 us -> 21.4 us  [per_device(): stats = lax.all_to_all(stats, 'seq', 0, 0, tiled=True)]
where the time goes in v5:
time: 79.9 us; the launch traced here: 79.7 us
  Pallas kernels  23.5 us (29%)
  blocking collectives  21.4 us (27%)
  starting transfers between devices  18.1 us (23%)
  waiting for transfers between devices  15.5 us (19%)
  between operations  0.92 us (1%)
    all_to_all x1, blocking collectives, per_device(): stats = lax.all_to_all(stats, 'seq', 0, 0, tiled=True)  21.4 us
    pallas_call x2, Pallas kernels, spatial_call(): pl.pallas_call(functools.partial(spatial_kernel, other), in_specs=[anywhe...  14.2 us
    ppermute x4, waiting for transfers between devices, to_half(): return lax.ppermute(array, 'ch', HALF_SWAP)  12.6 us
    ppermute x8, starting transfers between devices, to_core(): lax.ppermute(array[i * rows:(i + 1) * rows], 'ch', CORE_SWAP)  9.46 us
    ppermute x4, starting transfers between devices, to_half(): return lax.ppermute(array, 'ch', HALF_SWAP)  6.28 us
    pallas_call x2, Pallas kernels, temporal_call(): pl.pallas_call(functools.partial(temporal_kernel, other), in_specs=[vmem]...  6.02 us
    ppermute x8, waiting for transfers between devices, to_core(): lax.ppermute(array[i * rows:(i + 1) * rows], 'ch', CORE_SWAP)  2.91 us
    ppermute x2, starting transfers between devices, per_device(): halos.append(lax.ppermute(edge, 'seq', pairs + [(b, a) for a, b in pairs]))  2.39 us
  transfers between devices with their start and end apart: 14, of which 8 were waited for; matrix products, arithmetic and copies ran while one was open for 0% of the time, Pallas kernels for 16%

profile of v5, /device:TPU:1, one launch (start us, length us, event | category | flops | bytes accessed | tf_op | source)
XLA Modules:
  0.0 79.7 jit_solution(3653322552901661469)
XLA Ops:
  0.0 5.8 %spatial.2 = (bf16[1024,256]{1,0:T(8,128)(2,1)S(1)}, bf16[1024,256]{1,0:T(8,128)(2,1)S(1)}) custom-call(bf16[1024,320]{1,0:T(8,128)(2,1)} %bitcast.14, bf16[3,960,1280]{2,1,0:T(8,128)(2,1)} %bitcast.21, bf16[1024,320]{1,0:T(8,128)(2,1)} %bitcast.15), custom_call_target="tpu_custom_call" | custom-call | flops 3019898880 | bytes 2949120 | tf_op jit(solution)/shard_map/spatial/pallas_call | solution.py:195
  5.8 3.3 %collective-permute-start = (bf16[1024,256]{1,0:T(8,128)(2,1)S(1)}, bf16[1024,256]{1,0:T(8,128)(2,1)S(1)}, u32[]{:S(2)}, u32[]{:S(2)}) collective-permute-start(bf16[1024,256]{1,0:T(8,128)(2,1)S(1)} %get-tuple-element.21), channel_id=1, source_target_pairs={{0,1},{1,0},{2,3},{3,2},{4,5},{5,4},{6,7},{7,6},{8,9},{9,8},{10,11... | collective-permute-start | bytes 1572872 | tf_op jit(solution)/shard_map/ppermute | solution.py:410
  9.1 1.5 %collective-permute-done.got_ref = bf16[1024,256]{1,0:T(8,128)(2,1)S(1)} collective-permute-done((bf16[1024,256]{1,0:T(8,128)(2,1)S(1)}, bf16[1024,256]{1,0:T(8,128)(2,1)S(1)}, u32[]{:S(2)}, u32[]{:S(2)}) %collective-permute-start) | collective-permute-done | bytes 524320 | tf_op jit(solution)/shard_map/ppermute | solution.py:410
  10.7 0.1 chip_sum.4.after_ref
  10.8 1.3 %collective-permute-start.3 = (bf16[1024,256]{1,0:T(8,128)(2,1)S(1)}, bf16[1024,256]{1,0:T(8,128)(2,1)S(1)}, u32[]{:S(2)}, u32[]{:S(2)}) collective-permute-start(bf16[1024,256]{1,0:T(8,128)(2,1)S(1)} %chip_sum.4.after_ref), channel_id=1, source_target_pairs={{0,2},{2,0},{1,3},{3,1},{4,6},{6,4},{5,7},{7,5},{8,10},{10,8},{9,1... | collective-permute-start | bytes 1572872 | tf_op jit(solution)/shard_map/ppermute | solution.py:414
  12.1 8.4 %spatial.3 = (bf16[512,128]{1,0:T(8,128)(2,1)S(1)}, bf16[512,128]{1,0:T(8,128)(2,1)S(1)}, bf16[512,640]{1,0:T(8,128)(2,1)S(1)}, bf16[512,640]{1,0:T(8,128)(2,1)S(1)}) custom-call(bf16[1024,320]{1,0:T(8,128)(2,1)} %bitcast.16, bf16[3,960,1280]{2,1,0:T(8,128)(2,1)} %bitcast.22, bf16[1024,256]{1,0:T(8,128)(2,1)S(1)} %chip_sum.4.after_ref), custom_call_target="tpu_custom_call" | custom-call | flops 4529848320 | bytes 4423680 | tf_op jit(solution)/shard_map/spatial/pallas_call | solution.py:195
  20.5 0.8 collective-permute-start.4
  21.3 0.3 collective-permute-start.2
  21.6 0.5 collective-permute-start.1
  22.1 0.1 collective-permute-done.4.got_ref
  22.3 1.9 %collective-permute-start.5 = (bf16[512,128]{1,0:T(8,128)(2,1)S(1)}, bf16[512,128]{1,0:T(8,128)(2,1)S(1)}, u32[]{:S(2)}, u32[]{:S(2)}) collective-permute-start(bf16[512,128]{1,0:T(8,128)(2,1)S(1)} %chip_sum.5), channel_id=1, source_target_pairs={{0,2},{2,0},{1,3},{3,1},{4,6},{6,4},{5,7},{7,5},{8,10},{10,8},{9,1... | collective-permute-start | bytes 393224 | tf_op jit(solution)/shard_map/ppermute | solution.py:414
  24.2 0.4 base.1.after_ref.base_ref
  24.6 0.9 %collective-permute-done.3.in_ref = bf16[1024,256]{1,0:T(8,128)(2,1)S(1)} collective-permute-done((bf16[1024,256]{1,0:T(8,128)(2,1)S(1)}, bf16[1024,256]{1,0:T(8,128)(2,1)S(1)}, u32[]{:S(2)}, u32[]{:S(2)}) %collective-permute-start.3) | collective-permute-done | bytes 524320 | tf_op jit(solution)/shard_map/ppermute | solution.py:414
  25.5 3.1 %collective-permute-done.5.half_rest = bf16[512,128]{1,0:T(8,128)(2,1)S(1)} collective-permute-done((bf16[512,128]{1,0:T(8,128)(2,1)S(1)}, bf16[512,128]{1,0:T(8,128)(2,1)S(1)}, u32[]{:S(2)}, u32[]{:S(2)}) %collective-permute-start.5) | collective-permute-done | bytes 131104 | tf_op jit(solution)/shard_map/ppermute | solution.py:414
  28.6 0.9 %hidden.1 = (f32[1024,320]{1,0:T(8,128)S(1)}, bf16[512,640]{1,0:T(8,128)(2,1)S(1)}, f32[64,128]{1,0:T(8,128)S(1)}) custom-call(f32[1024,320]{1,0:T(8,128)S(1)} %base.1.after_ref.base_ref, bf16[1024,256]{1,0:T(8,128)(2,1)S(1)} %settle.2.half_first, bf16[512,128]{1,0:T(8,128)(2,1)S(1)} %collective-permute-done.5.half_rest), custom_call_target="tpu_custom_call" | custom-call | flops 1638400 | bytes 3276800 | tf_op jit(solution)/shard_map/hidden/pallas_call | solution.py:345
  29.6 1.7 %collective-permute-start.7 = (bf16[256,640]{1,0:T(8,128)(2,1)S(1)}, bf16[256,640]{1,0:T(8,128)(2,1)S(1)}, u32[]{:S(2)}, u32[]{:S(2)}) collective-permute-start(bf16[256,640]{1,0:T(8,128)(2,1)S(1)} %get-tuple-element.37), channel_id=1, source_target_pairs={{0,4},{8,12},{16,20},{24,28},{32,36},{40,44},{48,52},{56,60},{64,6... | collective-permute-start | bytes 983048 | tf_op jit(solution)/shard_map/ppermute | solution.py:457
  31.3 0.7 collective-permute-start.6
  32.0 21.4 %all_to_all.11 = f32[64,1,128]{2,1,0:T(1,128)S(1)} all-to-all(f32[64,1,128]{2,1,0:T(1,128)S(1)} %bitcast.20), channel_id=1, replica_groups=mesh['seq'=64,'ch'=4] {'seq'}, dimensions={0} | all-to-all | bytes 65536 | tf_op jit(solution)/shard_map/all_to_all | solution.py:458
  53.4 2.5 %temporal.2 = (bf16[1024,256]{1,0:T(8,128)(2,1)S(1)}, bf16[1024,256]{1,0:T(8,128)(2,1)S(1)}) custom-call(f32[1024,320]{1,0:T(8,128)S(1)} %get-tuple-element.26.hidden_ref.after_ref, bf16[256,640]{1,0:T(8,128)(2,1)S(1)} %collective-permute-done.6.across_ref, bf16[256,640]{1,0:T(8,128)(2,1)S(1)} %collective-permute-done.7.pair_ref, f32[64,128]{1,0:T(8,128)S(1)} %bitcast.18, ...), custom_call_target="tpu_custom_call" | custom-call | flops 1006632960 | bytes 983040 | tf_op jit(solution)/shard_map/temporal/pallas_call | solution.py:255
  55.9 3.3 %collective-permute-start.8 = (bf16[1024,256]{1,0:T(8,128)(2,1)S(1)}, bf16[1024,256]{1,0:T(8,128)(2,1)S(1)}, u32[]{:S(2)}, u32[]{:S(2)}) collective-permute-start(bf16[1024,256]{1,0:T(8,128)(2,1)S(1)} %get-tuple-element.30), channel_id=1, source_target_pairs={{0,1},{1,0},{2,3},{3,2},{4,5},{5,4},{6,7},{7,6},{8,9},{9,8},{10,11... | collective-permute-start | bytes 1572872 | tf_op jit(solution)/shard_map/ppermute | solution.py:410
  59.8 0.9 %collective-permute-done.8.got_ref = bf16[1024,256]{1,0:T(8,128)(2,1)S(1)} collective-permute-done((bf16[1024,256]{1,0:T(8,128)(2,1)S(1)}, bf16[1024,256]{1,0:T(8,128)(2,1)S(1)}, u32[]{:S(2)}, u32[]{:S(2)}) %collective-permute-start.8) | collective-permute-done | bytes 524320 | tf_op jit(solution)/shard_map/ppermute | solution.py:410
  60.7 0.1 chip_sum.6.after_ref
  60.8 1.6 %collective-permute-start.11 = (bf16[1024,256]{1,0:T(8,128)(2,1)S(1)}, bf16[1024,256]{1,0:T(8,128)(2,1)S(1)}, u32[]{:S(2)}, u32[]{:S(2)}) collective-permute-start(bf16[1024,256]{1,0:T(8,128)(2,1)S(1)} %chip_sum.6.after_ref), channel_id=1, source_target_pairs={{0,2},{2,0},{1,3},{3,1},{4,6},{6,4},{5,7},{7,5},{8,10},{10,8},{9,1... | collective-permute-start | bytes 1572872 | tf_op jit(solution)/shard_map/ppermute | solution.py:414
  62.5 3.5 %temporal.3 = (bf16[512,128]{1,0:T(8,128)(2,1)S(1)}, bf16[512,128]{1,0:T(8,128)(2,1)S(1)}, bf16[512,640]{1,0:T(8,128)(2,1)S(1)}, bf16[512,640]{1,0:T(8,128)(2,1)S(1)}) custom-call(f32[1024,320]{1,0:T(8,128)S(1)} %get-tuple-element.26.hidden_ref.after_ref, bf16[256,640]{1,0:T(8,128)(2,1)S(1)} %collective-permute-done.6.across_ref, ...), custom_call_target="tpu_custom_call" | custom-call | flops 1509949440 | bytes 1474560 | tf_op jit(solution)/shard_map/temporal/pallas_call | solution.py:255
  66.0 0.7 collective-permute-start.12
  66.9 0.5 collective-permute-start.9
  67.4 0.3 collective-permute-done.12.got_ref
  67.8 1.5 %collective-permute-start.13 = (bf16[512,128]{1,0:T(8,128)(2,1)S(1)}, bf16[512,128]{1,0:T(8,128)(2,1)S(1)}, u32[]{:S(2)}, u32[]{:S(2)}) collective-permute-start(bf16[512,128]{1,0:T(8,128)(2,1)S(1)} %chip_sum.7), channel_id=1, source_target_pairs={{0,2},{2,0},{1,3},{3,1},{4,6},{6,4},{5,7},{7,5},{8,10},{10,8},{9,1... | collective-permute-start | bytes 393224 | tf_op jit(solution)/shard_map/ppermute | solution.py:414
  69.3 0.5 mixed.1.after_ref.mixed_ref
  69.8 5.8 %collective-permute-done.11.in_ref = bf16[1024,256]{1,0:T(8,128)(2,1)S(1)} collective-permute-done((bf16[1024,256]{1,0:T(8,128)(2,1)S(1)}, bf16[1024,256]{1,0:T(8,128)(2,1)S(1)}, u32[]{:S(2)}, u32[]{:S(2)}) %collective-permute-start.11) | collective-permute-done | bytes 524320 | tf_op jit(solution)/shard_map/ppermute | solution.py:414
  75.6 2.8 %collective-permute-done.13.half_rest = bf16[512,128]{1,0:T(8,128)(2,1)S(1)} collective-permute-done((bf16[512,128]{1,0:T(8,128)(2,1)S(1)}, bf16[512,128]{1,0:T(8,128)(2,1)S(1)}, u32[]{:S(2)}, u32[]{:S(2)}) %collective-permute-start.13) | collective-permute-done | bytes 131104 | tf_op jit(solution)/shard_map/ppermute | solution.py:414
  78.4 1.2 %blend.1 = bf16[1024,320]{1,0:T(8,128)(2,1)} custom-call(f32[1]{0:T(128)S(6)} %copy.10.mix_ref, f32[1024,320]{1,0:T(8,128)S(1)} %mixed.1.after_ref.mixed_ref, bf16[1024,256]{1,0:T(8,128)(2,1)S(1)} %settle.3.half_first, bf16[512,128]{1,0:T(8,128)(2,1)S(1)} %collective-permute-done.13.half_rest), custom_call_target="tpu_custom_call" | custom-call | flops 1638400 | bytes 3276800 | tf_op jit(solution)/shard_map/blend/pallas_call | solution.py:383
  (18 shorter events, 0.4 us)
Async XLA Ops:
  5.8 4.9 %collective-permute-start = (bf16[1024,256]{1,0:T(8,128)(2,1)S(1)}, bf16[1024,256]{1,0:T(8,128)(2,1)S(1)}, u32[]{:S(2)}, u32[]{:S(2)}) collective-permute-start(bf16[1024,256]{1,0:T(8,128)(2,1)S(1)} %get-tuple-element.21), channel_id=1, source_target_pairs={{0,1},{1,0},{2,3},{3,2},{4,5},{5,4},{6,7},{7,6},{8,9},{9,8},{10,11... | collective-permute-start | bytes 1572872 | tf_op jit(solution)/shard_map/ppermute | solution.py:410
  10.8 14.7 %collective-permute-start.3 = (bf16[1024,256]{1,0:T(8,128)(2,1)S(1)}, bf16[1024,256]{1,0:T(8,128)(2,1)S(1)}, u32[]{:S(2)}, u32[]{:S(2)}) collective-permute-start(bf16[1024,256]{1,0:T(8,128)(2,1)S(1)} %chip_sum.4.after_ref), channel_id=1, source_target_pairs={{0,2},{2,0},{1,3},{3,1},{4,6},{6,4},{5,7},{7,5},{8,10},{10,8},{9,1... | collective-permute-start | bytes 1572872 | tf_op jit(solution)/shard_map/ppermute | solution.py:414
  20.5 1.7 %collective-permute-start.4 = (bf16[512,128]{1,0:T(8,128)(2,1)S(1)}, bf16[512,128]{1,0:T(8,128)(2,1)S(1)}, u32[]{:S(2)}, u32[]{:S(2)}) collective-permute-start(bf16[512,128]{1,0:T(8,128)(2,1)S(1)} %get-tuple-element.25), channel_id=1, source_target_pairs={{0,1},{1,0},{2,3},{3,2},{4,5},{5,4},{6,7},{7,6},{8,9},{9,8},{10,11... | collective-permute-start | bytes 393224 | tf_op jit(solution)/shard_map/ppermute | solution.py:410
  21.3 2.8 %collective-permute-start.2 = (bf16[256,640]{1,0:T(8,128)(2,1)S(1)}, bf16[256,640]{1,0:T(8,128)(2,1)S(1)}, u32[]{:S(2)}, u32[]{:S(2)}) collective-permute-start(bf16[256,640]{1,0:T(8,128)(2,1)S(1)} %get-tuple-element.39), channel_id=1, source_target_pairs={{0,1},{1,0},{2,3},{3,2},{4,5},{5,4},{6,7},{7,6},{8,9},{9,8},{10,11... | collective-permute-start | bytes 983048 | tf_op jit(solution)/shard_map/ppermute | solution.py:410
  21.6 2.6 %collective-permute-start.1 = (bf16[256,640]{1,0:T(8,128)(2,1)S(1)}, bf16[256,640]{1,0:T(8,128)(2,1)S(1)}, u32[]{:S(2)}, u32[]{:S(2)}) collective-permute-start(bf16[256,640]{1,0:T(8,128)(2,1)S(1)} %get-tuple-element.40), channel_id=1, source_target_pairs={{0,1},{1,0},{2,3},{3,2},{4,5},{5,4},{6,7},{7,6},{8,9},{9,8},{10,11... | collective-permute-start | bytes 983048 | tf_op jit(solution)/shard_map/ppermute | solution.py:410
  22.2 1.9 %copy-start.1 = (bf16[2,320,16,32]{1,3,2,0:T(8,128)(2,1)S(1)}, bf16[2,320,16,32]{1,3,2,0:T(8,128)(2,1)}, u32[]{:S(2)}) copy-start(bf16[2,320,16,32]{1,3,2,0:T(8,128)(2,1)} %param.4) | copy-start | bytes 1966084
  22.3 6.3 %collective-permute-start.5 = (bf16[512,128]{1,0:T(8,128)(2,1)S(1)}, bf16[512,128]{1,0:T(8,128)(2,1)S(1)}, u32[]{:S(2)}, u32[]{:S(2)}) collective-permute-start(bf16[512,128]{1,0:T(8,128)(2,1)S(1)} %chip_sum.5), channel_id=1, source_target_pairs={{0,2},{2,0},{1,3},{3,1},{4,6},{6,4},{5,7},{7,5},{8,10},{10,8},{9,1... | collective-permute-start | bytes 393224 | tf_op jit(solution)/shard_map/ppermute | solution.py:414
  25.5 27.9 %copy-start = (bf16[3,320,1280]{2,1,0:T(8,128)(2,1)S(1)}, bf16[3,320,1280]{2,1,0:T(8,128)(2,1)}, u32[]{:S(2)}) copy-start(bf16[3,320,1280]{2,1,0:T(8,128)(2,1)} %param.6) | copy-start | bytes 7372804
  29.6 23.8 %collective-permute-start.7 = (bf16[256,640]{1,0:T(8,128)(2,1)S(1)}, bf16[256,640]{1,0:T(8,128)(2,1)S(1)}, u32[]{:S(2)}, u32[]{:S(2)}) collective-permute-start(bf16[256,640]{1,0:T(8,128)(2,1)S(1)} %get-tuple-element.37), channel_id=1, source_target_pairs={{0,4},{8,12},{16,20},{24,28},{32,36},{40,44},{48,52},{56,60},{64,6... | collective-permute-start | bytes 983048 | tf_op jit(solution)/shard_map/ppermute | solution.py:457
  31.3 22.1 %collective-permute-start.6 = (bf16[256,640]{1,0:T(8,128)(2,1)S(1)}, bf16[256,640]{1,0:T(8,128)(2,1)S(1)}, u32[]{:S(2)}, u32[]{:S(2)}) collective-permute-start(bf16[256,640]{1,0:T(8,128)(2,1)S(1)} %get-tuple-element.38), channel_id=1, source_target_pairs={{4,8},{12,16},{20,24},{28,32},{36,40},{44,48},{52,56},{60,64},{68,... | collective-permute-start | bytes 983048 | tf_op jit(solution)/shard_map/ppermute | solution.py:457
  55.9 4.8 %collective-permute-start.8 = (bf16[1024,256]{1,0:T(8,128)(2,1)S(1)}, bf16[1024,256]{1,0:T(8,128)(2,1)S(1)}, u32[]{:S(2)}, u32[]{:S(2)}) collective-permute-start(bf16[1024,256]{1,0:T(8,128)(2,1)S(1)} %get-tuple-element.30), channel_id=1, source_target_pairs={{0,1},{1,0},{2,3},{3,2},{4,5},{5,4},{6,7},{7,6},{8,9},{9,8},{10,11... | collective-permute-start | bytes 1572872 | tf_op jit(solution)/shard_map/ppermute | solution.py:410
  60.8 14.7 %collective-permute-start.11 = (bf16[1024,256]{1,0:T(8,128)(2,1)S(1)}, bf16[1024,256]{1,0:T(8,128)(2,1)S(1)}, u32[]{:S(2)}, u32[]{:S(2)}) collective-permute-start(bf16[1024,256]{1,0:T(8,128)(2,1)S(1)} %chip_sum.6.after_ref), channel_id=1, source_target_pairs={{0,2},{2,0},{1,3},{3,1},{4,6},{6,4},{5,7},{7,5},{8,10},{10,8},{9,1... | collective-permute-start | bytes 1572872 | tf_op jit(solution)/shard_map/ppermute | solution.py:414
  66.0 1.7 %collective-permute-start.12 = (bf16[512,128]{1,0:T(8,128)(2,1)S(1)}, bf16[512,128]{1,0:T(8,128)(2,1)S(1)}, u32[]{:S(2)}, u32[]{:S(2)}) collective-permute-start(bf16[512,128]{1,0:T(8,128)(2,1)S(1)} %get-tuple-element.34), channel_id=1, source_target_pairs={{0,1},{1,0},{2,3},{3,2},{4,5},{5,4},{6,7},{7,6},{8,9},{9,8},{10,11... | collective-permute-start | bytes 393224 | tf_op jit(solution)/shard_map/ppermute | solution.py:410
  66.8 2.5 %collective-permute-start.10 = (bf16[256,640]{1,0:T(8,128)(2,1)S(1)}, bf16[256,640]{1,0:T(8,128)(2,1)S(1)}, u32[]{:S(2)}, u32[]{:S(2)}) collective-permute-start(bf16[256,640]{1,0:T(8,128)(2,1)S(1)} %get-tuple-element.35), channel_id=1, source_target_pairs={{0,1},{1,0},{2,3},{3,2},{4,5},{5,4},{6,7},{7,6},{8,9},{9,8},{10,11... | collective-permute-start | bytes 983048 | tf_op jit(solution)/shard_map/ppermute | solution.py:410
  66.9 2.4 %collective-permute-start.9 = (bf16[256,640]{1,0:T(8,128)(2,1)S(1)}, bf16[256,640]{1,0:T(8,128)(2,1)S(1)}, u32[]{:S(2)}, u32[]{:S(2)}) collective-permute-start(bf16[256,640]{1,0:T(8,128)(2,1)S(1)} %get-tuple-element.36), channel_id=1, source_target_pairs={{0,1},{1,0},{2,3},{3,2},{4,5},{5,4},{6,7},{7,6},{8,9},{9,8},{10,11... | collective-permute-start | bytes 983048 | tf_op jit(solution)/shard_map/ppermute | solution.py:410
  67.8 10.6 %collective-permute-start.13 = (bf16[512,128]{1,0:T(8,128)(2,1)S(1)}, bf16[512,128]{1,0:T(8,128)(2,1)S(1)}, u32[]{:S(2)}, u32[]{:S(2)}) collective-permute-start(bf16[512,128]{1,0:T(8,128)(2,1)S(1)} %chip_sum.7), channel_id=1, source_target_pairs={{0,2},{2,0},{1,3},{3,1},{4,6},{6,4},{5,7},{7,5},{8,10},{10,8},{9,1... | collective-permute-start | bytes 393224 | tf_op jit(solution)/shard_map/ppermute | solution.py:414

commit v6 on v5

--- a/solution.py
+++ b/solution.py
@@ -74,24 +74,31 @@
     return jnp.concatenate([ref[:, :LOCAL], ref[:, LOCAL:]], axis=0)
 
 
-def copy_columns(other, weight_hbm, weight_ref, sems):
-    half = lax.axis_index("ch") // 2
-    away, home = (1 - half) * HALF, half * HALF
-    if other:
-        core = lax.axis_index("ch") % 2
-        step = HALF - FIRST
-        pieces = [(away + core * step, 0, FIRST), (away + (1 - core) * step, FIRST, FIRST)]
-    else:
-        pieces = [(away + FIRST, 0, 2 * REST), (home, 2 * REST, HALF)]
+def start_copies(pieces, weight_hbm, weight_ref, sems):
     copies = []
     for tap in range(weight_hbm.shape[0]):
-        copies.append([])
         for i, (start, to, width) in enumerate(pieces):
             source = weight_hbm.at[tap, :, pl.ds(pl.multiple_of(start, 128), width)]
             copy = pltpu.make_async_copy(source, weight_ref.at[tap, :, to : to + width], sems.at[tap, i])
             copy.start()
-            copies[-1].append(copy)
+            copies.append(copy)
     return copies
+
+
+def first_columns(own):
+    index = lax.axis_index("ch")
+    half, core = index // 2, index % 2
+    core = core if own else 1 - core
+    return (1 - half) * HALF + core * (HALF - FIRST)
+
+
+def copy_columns(other, weight_hbm, weight_ref, sems):
+    if other:
+        pieces = [(first_columns(True), 0, FIRST), (first_columns(False), FIRST, FIRST)]
+    else:
+        half = lax.axis_index("ch") // 2
+        pieces = [((1 - half) * HALF + FIRST, 0, 2 * REST), (half * HALF, 2 * REST, HALF)]
+    return start_copies(pieces, weight_hbm, weight_ref, sems)
 
 
 def store_sums(other, frame, total, outs, total_ref):
@@ -168,35 +175,102 @@
     return frame_taps
 
 
-def spatial_kernel(other, lat_hbm, weight_hbm, after_ref, *refs):
+def spatial_sums(taps_ref, weight_ref, frame):
+    total = None
+    for row_tap in range(TAPS):
+        cells = slice(row_tap * COLS, row_tap * COLS + PX)
+        term = jnp.dot(taps_ref[frame, cells], weight_ref[row_tap], preferred_element_type=F32)
+        total = term if total is None else total + term
+    return total
+
+
+def spatial_send_kernel(
+    lat_hbm, weight_hbm, send_ref, taps_ref, own_weight_ref, lat_ref, weight_ref, lat_sem, sems, own_sems
+):
+    lat_copy = pltpu.make_async_copy(lat_hbm, lat_ref, lat_sem)
+    lat_copy.start()
+    copies = start_copies([(first_columns(False), 0, FIRST)], weight_hbm, weight_ref, sems)
+    own_copies = start_copies([(first_columns(True), 0, FIRST)], weight_hbm, own_weight_ref, own_sems)
+    lat_copy.wait()
+    frame_taps = spatial_taps(lat_ref, taps_ref)
+    frame_taps(0)
+    for copy in copies:
+        copy.wait()
+    frame_taps(1)
+    for frame in range(2):
+        send_ref[frame * PX : (frame + 1) * PX] = spatial_sums(taps_ref, weight_ref, frame).astype(BF16)
+    for copy in own_copies:
+        copy.wait()
+
+
+def spatial_own_kernel(taps_ref, weight_ref, own_ref):
+    for frame in range(2):
+        own_ref[frame * PX : (frame + 1) * PX] = spatial_sums(taps_ref, weight_ref, frame).astype(BF16)
+
+
+def spatial_rest_kernel(lat_hbm, weight_hbm, after_ref, *refs):
     *outs, lat_ref, weight_ref, taps_ref, total_ref, lat_sem, sems = refs
     lat_copy = pltpu.make_async_copy(lat_hbm, lat_ref, lat_sem)
     lat_copy.start()
-    copies = copy_columns(other, weight_hbm, weight_ref, sems)
+    copies = copy_columns(False, weight_hbm, weight_ref, sems)
     lat_copy.wait()
     frame_taps = spatial_taps(lat_ref, taps_ref)
     frame_taps(0)
-    for copy in sum(copies, []):
+    for copy in copies:
         copy.wait()
-    for frame in range(2):
-        if frame == 0:
-            frame_taps(1)
-        total = None
-        for row_tap in range(TAPS):
-            cells = slice(row_tap * COLS, row_tap * COLS + PX)
-            term = jnp.dot(taps_ref[frame, cells], weight_ref[row_tap], preferred_element_type=F32)
-            total = term if total is None else total + term
-        store_sums(other, frame, total, outs, total_ref)
-
-
-def spatial_call(lat, weight, after, other):
+    frame_taps(1)
+    for frame in range(2):
+        store_sums(False, frame, spatial_sums(taps_ref, weight_ref, frame), outs, total_ref)
+
+
+def spatial_cost(columns):
+    return pl.CostEstimate(
+        flops=4 * PX * TAPS * WIDE * columns,
+        bytes_accessed=2 * TAPS * WIDE * columns,
+        transcendentals=2 * PX * LOCAL,
+    )
+
+
+def spatial_first(lat, weight):
     vmem, anywhere = pl.BlockSpec(memory_space=pltpu.VMEM), pl.BlockSpec(memory_space=pl.ANY)
-    shapes, columns = part_shapes(other), part_columns(other)
-    return pl.pallas_call(
-        functools.partial(spatial_kernel, other),
+    sums = jax.ShapeDtypeStruct((2 * PX, FIRST), BF16)
+    columns = jax.ShapeDtypeStruct((TAPS, WIDE, FIRST), BF16)
+    send, taps, own_weight = pl.pallas_call(
+        spatial_send_kernel,
+        in_specs=[anywhere] * 2,
+        out_specs=[vmem] * 3,
+        out_shape=[sums, jax.ShapeDtypeStruct((2, PX + 2 * COLS, WIDE), BF16), columns],
+        scratch_shapes=[
+            pltpu.VMEM((2 * PX, LOCAL), BF16),
+            pltpu.VMEM(columns.shape, BF16),
+            pltpu.SemaphoreType.DMA,
+            pltpu.SemaphoreType.DMA((TAPS, 1)),
+            pltpu.SemaphoreType.DMA((TAPS, 1)),
+        ],
+        compiler_params=params(),
+        cost_estimate=spatial_cost(FIRST),
+        name="spatial_send",
+    )(lat, weight)
+    own = pl.pallas_call(
+        spatial_own_kernel,
+        in_specs=[vmem] * 2,
+        out_specs=vmem,
+        out_shape=sums,
+        compiler_params=params(),
+        cost_estimate=spatial_cost(FIRST),
+        name="spatial_own",
+    )(taps, own_weight)
+    return send, own
+
+
+def spatial_second(lat, weight, after):
+    vmem, anywhere = pl.BlockSpec(memory_space=pltpu.VMEM), pl.BlockSpec(memory_space=pl.ANY)
+    columns = part_columns(False)
+    return pl.pallas_call(
+        spatial_rest_kernel,
         in_specs=[anywhere] * 3,
-        out_specs=[vmem] * len(shapes),
-        out_shape=shapes,
+        out_specs=[vmem] * 4,
+        out_shape=part_shapes(False),
         scratch_shapes=[
             pltpu.VMEM((2 * PX, LOCAL), BF16),
             pltpu.VMEM((TAPS, WIDE, columns), BF16),
@@ -206,12 +280,8 @@
             pltpu.SemaphoreType.DMA((TAPS, 2)),
         ],
         compiler_params=params(),
-        cost_estimate=pl.CostEstimate(
-            flops=4 * PX * TAPS * WIDE * columns,
-            bytes_accessed=2 * TAPS * WIDE * columns,
-            transcendentals=2 * PX * LOCAL,
-        ),
-        name="spatial",
+        cost_estimate=spatial_cost(columns),
+        name="spatial_rest",
     )(lat, weight, after)
 
 
@@ -241,7 +311,7 @@
     put(halo(across_ref, pair_ref, seq == 0), (0, 0))
     put(act(hidden_ref[:PX]), (0, 1), (1, 0))
     put(act(hidden_ref[PX:]), (0, 2), (1, 1))
-    for copy in copies[0]:
+    for copy in copies:
         copy.wait()
     put(halo(pair_ref, across_ref, seq == size - 1), (1, 2))
     for frame in range(2):
@@ -445,8 +515,8 @@
     weight_s = pltpu.with_memory_space_constraint(spatial_weight.reshape(TAPS, WIDE, CH), pltpu.HBM)
     weight_t = temporal_weight.reshape(1, WIDE, CH)
     base, half_first, half_rest = reduce_channels(
-        lambda: spatial_call(lat_hbm, weight_s, lat_hbm, True),
-        lambda after: spatial_call(lat_hbm, weight_s, after, False),
+        lambda: spatial_first(lat_hbm, weight_s),
+        lambda after: spatial_second(lat_hbm, weight_s, after),
         lambda own, cores: base_call(lat, own, cores),
     )
     hidden, edges, stats = hidden_call(base, half_first, half_rest, size)

time: 79.9 us -> 78.4 us (0.981)
  waiting for transfers between devices: 15.5 us -> 14 us
    ppermute x8, waiting for transfers between devices: 2.91 us -> 1.37 us  [to_core(): lax.ppermute(array[i * rows:(i + 1) * rows], 'ch', CORE_SWAP)]
    pallas_call x2 -> x3, Pallas kernels: 14.2 us -> 14.5 us  [the longest x1 8.44 us: spatial_second(): pl.pallas_call(spatial_rest_kernel, in_specs=[anywhere] * 3, out_specs=[v...]
  transfers between devices with their start and end apart: 14 -> 14, of which waited for: 8 -> 7; matrix products, arithmetic and copies ran while one was open for 0% -> 0% of each run, Pallas kernels for 16% -> 19%
where the time goes in v6:
time: 78.4 us; the launch traced here: 78.2 us
  Pallas kernels  23.9 us (30%)
  blocking collectives  21.4 us (27%)
  starting transfers between devices  17.8 us (23%)
  waiting for transfers between devices  14 us (18%)
  between operations  0.93 us (1%)
    all_to_all x1, blocking collectives, per_device(): stats = lax.all_to_all(stats, 'seq', 0, 0, tiled=True)  21.4 us
    ppermute x4, waiting for transfers between devices, to_half(): return lax.ppermute(array, 'ch', HALF_SWAP)  12.7 us
    ppermute x8, starting transfers between devices, to_core(): lax.ppermute(array[i * rows:(i + 1) * rows], 'ch', CORE_SWAP)  9.16 us
    pallas_call x1, Pallas kernels, spatial_second(): pl.pallas_call(spatial_rest_kernel, in_specs=[anywhere] * 3, out_specs=[v...  8.44 us
    ppermute x4, starting transfers between devices, to_half(): return lax.ppermute(array, 'ch', HALF_SWAP)  6.32 us
    pallas_call x2, Pallas kernels, temporal_call(): pl.pallas_call(functools.partial(temporal_kernel, other), in_specs=[vmem]...  6.02 us
    pallas_call x1, Pallas kernels, spatial_first(): pl.pallas_call(spatial_send_kernel, in_specs=[anywhere] * 2, out_specs=[v...  4.33 us
    ppermute x2, starting transfers between devices, per_device(): halos.append(lax.ppermute(edge, 'seq', pairs + [(b, a) for a, b in pairs]))  2.3 us
  transfers between devices with their start and end apart: 14, of which 7 were waited for; matrix products, arithmetic and copies ran while one was open for 0% of the time, Pallas kernels for 19%

profile of v6, /device:TPU:1, one launch (start us, length us, event | category | flops | bytes accessed | tf_op | source)
XLA Modules:
  0.0 78.2 jit_solution(11649653255005225440)
XLA Ops:
  0.0 4.3 %spatial_send.1 = (bf16[1024,256]{1,0:T(8,128)(2,1)S(1)}, bf16[2,576,960]{2,1,0:T(8,128)(2,1)S(1)}, bf16[3,960,256]{2,1,0:T(8,128)(2,1)S(1)}) custom-call(bf16[1024,320]{1,0:T(8,128)(2,1)} %bitcast.12, bf16[3,960,1280]{2,1,0:T(8,128)(2,1)} %bitcast.20), custom_call_target="tpu_custom_call" | custom-call | flops 1509949440 | bytes 1474560 | tf_op jit(solution)/shard_map/spatial_send/pallas_call | solution.py:238
  4.3 3.3 %collective-permute-start = (bf16[1024,256]{1,0:T(8,128)(2,1)S(1)}, bf16[1024,256]{1,0:T(8,128)(2,1)S(1)}, u32[]{:S(2)}, u32[]{:S(2)}) collective-permute-start(bf16[1024,256]{1,0:T(8,128)(2,1)S(1)} %get-tuple-element.23), channel_id=1, source_target_pairs={{0,1},{1,0},{2,3},{3,2},{4,5},{5,4},{6,7},{7,6},{8,9},{9,8},{10,11... | collective-permute-start | bytes 1572872 | tf_op jit(solution)/shard_map/ppermute | solution.py:480
  7.7 1.8 %spatial_own.1.own_ref = bf16[1024,256]{1,0:T(8,128)(2,1)S(1)} custom-call(bf16[2,576,960]{2,1,0:T(8,128)(2,1)S(1)} %get-tuple-element.21.taps_ref, bf16[3,960,256]{2,1,0:T(8,128)(2,1)S(1)} %get-tuple-element.22.weight_ref), custom_call_target="tpu_custom_call" | custom-call | flops 1509949440 | bytes 1474560 | tf_op jit(solution)/shard_map/spatial_own/pallas_call | solution.py:254
  9.5 0.1 chip_sum.4.after_ref
  9.6 1.3 %collective-permute-start.3 = (bf16[1024,256]{1,0:T(8,128)(2,1)S(1)}, bf16[1024,256]{1,0:T(8,128)(2,1)S(1)}, u32[]{:S(2)}, u32[]{:S(2)}) collective-permute-start(bf16[1024,256]{1,0:T(8,128)(2,1)S(1)} %chip_sum.4.after_ref), channel_id=1, source_target_pairs={{0,2},{2,0},{1,3},{3,1},{4,6},{6,4},{5,7},{7,5},{8,10},{10,8},{9,1... | collective-permute-start | bytes 1572872 | tf_op jit(solution)/shard_map/ppermute | solution.py:484
  10.9 8.4 %spatial_rest.1 = (bf16[512,128]{1,0:T(8,128)(2,1)S(1)}, bf16[512,128]{1,0:T(8,128)(2,1)S(1)}, bf16[512,640]{1,0:T(8,128)(2,1)S(1)}, bf16[512,640]{1,0:T(8,128)(2,1)S(1)}) custom-call(bf16[1024,320]{1,0:T(8,128)(2,1)} %bitcast.13, bf16[3,960,1280]{2,1,0:T(8,128)(2,1)} %bitcast.21, bf16[1024,256]{1,0:T(8,128)(2,1)S(1)} %chip_sum.4.after_ref), custom_call_target="tpu_custom_call" | custom-call | flops 4529848320 | bytes 4423680 | tf_op jit(solution)/shard_map/spatial_rest/pallas_call | solution.py:269
  19.3 0.5 collective-permute-start.4
  19.8 0.4 collective-permute-start.2
  20.3 0.4 collective-permute-start.1
  20.6 0.1 collective-permute-done.4.got_ref
  20.8 1.9 %collective-permute-start.5 = (bf16[512,128]{1,0:T(8,128)(2,1)S(1)}, bf16[512,128]{1,0:T(8,128)(2,1)S(1)}, u32[]{:S(2)}, u32[]{:S(2)}) collective-permute-start(bf16[512,128]{1,0:T(8,128)(2,1)S(1)} %chip_sum.5), channel_id=1, source_target_pairs={{0,2},{2,0},{1,3},{3,1},{4,6},{6,4},{5,7},{7,5},{8,10},{10,8},{9,1... | collective-permute-start | bytes 393224 | tf_op jit(solution)/shard_map/ppermute | solution.py:484
  22.7 0.4 base.1.after_ref.base_ref
  23.1 1.5 %collective-permute-done.3.in_ref = bf16[1024,256]{1,0:T(8,128)(2,1)S(1)} collective-permute-done((bf16[1024,256]{1,0:T(8,128)(2,1)S(1)}, bf16[1024,256]{1,0:T(8,128)(2,1)S(1)}, u32[]{:S(2)}, u32[]{:S(2)}) %collective-permute-start.3) | collective-permute-done | bytes 524320 | tf_op jit(solution)/shard_map/ppermute | solution.py:484
  24.7 2.5 %collective-permute-done.5.half_rest = bf16[512,128]{1,0:T(8,128)(2,1)S(1)} collective-permute-done((bf16[512,128]{1,0:T(8,128)(2,1)S(1)}, bf16[512,128]{1,0:T(8,128)(2,1)S(1)}, u32[]{:S(2)}, u32[]{:S(2)}) %collective-permute-start.5) | collective-permute-done | bytes 131104 | tf_op jit(solution)/shard_map/ppermute | solution.py:484
  27.2 0.9 %hidden.1 = (f32[1024,320]{1,0:T(8,128)S(1)}, bf16[512,640]{1,0:T(8,128)(2,1)S(1)}, f32[64,128]{1,0:T(8,128)S(1)}) custom-call(f32[1024,320]{1,0:T(8,128)S(1)} %base.1.after_ref.base_ref, bf16[1024,256]{1,0:T(8,128)(2,1)S(1)} %settle.2.half_first, bf16[512,128]{1,0:T(8,128)(2,1)S(1)} %collective-permute-done.5.half_rest), custom_call_target="tpu_custom_call" | custom-call | flops 1638400 | bytes 3276800 | tf_op jit(solution)/shard_map/hidden/pallas_call | solution.py:415
  28.2 1.6 %collective-permute-start.7 = (bf16[256,640]{1,0:T(8,128)(2,1)S(1)}, bf16[256,640]{1,0:T(8,128)(2,1)S(1)}, u32[]{:S(2)}, u32[]{:S(2)}) collective-permute-start(bf16[256,640]{1,0:T(8,128)(2,1)S(1)} %get-tuple-element.39), channel_id=1, source_target_pairs={{0,4},{8,12},{16,20},{24,28},{32,36},{40,44},{48,52},{56,60},{64,6... | collective-permute-start | bytes 983048 | tf_op jit(solution)/shard_map/ppermute | solution.py:527
  29.8 0.7 collective-permute-start.6
  30.5 21.4 %all_to_all.11 = f32[64,1,128]{2,1,0:T(1,128)S(1)} all-to-all(f32[64,1,128]{2,1,0:T(1,128)S(1)} %bitcast.19), channel_id=1, replica_groups=mesh['seq'=64,'ch'=4] {'seq'}, dimensions={0} | all-to-all | bytes 65536 | tf_op jit(solution)/shard_map/all_to_all | solution.py:528
  51.9 2.5 %temporal.2 = (bf16[1024,256]{1,0:T(8,128)(2,1)S(1)}, bf16[1024,256]{1,0:T(8,128)(2,1)S(1)}) custom-call(f32[1024,320]{1,0:T(8,128)S(1)} %get-tuple-element.28.hidden_ref.after_ref, bf16[256,640]{1,0:T(8,128)(2,1)S(1)} %collective-permute-done.6.across_ref, bf16[256,640]{1,0:T(8,128)(2,1)S(1)} %collective-permute-done.7.pair_ref, f32[64,128]{1,0:T(8,128)S(1)} %bitcast.17, ...), custom_call_target="tpu_custom_call" | custom-call | flops 1006632960 | bytes 983040 | tf_op jit(solution)/shard_map/temporal/pallas_call | solution.py:325
  54.4 3.3 %collective-permute-start.8 = (bf16[1024,256]{1,0:T(8,128)(2,1)S(1)}, bf16[1024,256]{1,0:T(8,128)(2,1)S(1)}, u32[]{:S(2)}, u32[]{:S(2)}) collective-permute-start(bf16[1024,256]{1,0:T(8,128)(2,1)S(1)} %get-tuple-element.32), channel_id=1, source_target_pairs={{0,1},{1,0},{2,3},{3,2},{4,5},{5,4},{6,7},{7,6},{8,9},{9,8},{10,11... | collective-permute-start | bytes 1572872 | tf_op jit(solution)/shard_map/ppermute | solution.py:480
  58.3 0.9 %collective-permute-done.8.got_ref = bf16[1024,256]{1,0:T(8,128)(2,1)S(1)} collective-permute-done((bf16[1024,256]{1,0:T(8,128)(2,1)S(1)}, bf16[1024,256]{1,0:T(8,128)(2,1)S(1)}, u32[]{:S(2)}, u32[]{:S(2)}) %collective-permute-start.8) | collective-permute-done | bytes 524320 | tf_op jit(solution)/shard_map/ppermute | solution.py:480
  59.2 0.1 chip_sum.6.after_ref
  59.3 1.9 %collective-permute-start.11 = (bf16[1024,256]{1,0:T(8,128)(2,1)S(1)}, bf16[1024,256]{1,0:T(8,128)(2,1)S(1)}, u32[]{:S(2)}, u32[]{:S(2)}) collective-permute-start(bf16[1024,256]{1,0:T(8,128)(2,1)S(1)} %chip_sum.6.after_ref), channel_id=1, source_target_pairs={{0,2},{2,0},{1,3},{3,1},{4,6},{6,4},{5,7},{7,5},{8,10},{10,8},{9,1... | collective-permute-start | bytes 1572872 | tf_op jit(solution)/shard_map/ppermute | solution.py:484
  61.3 3.5 %temporal.3 = (bf16[512,128]{1,0:T(8,128)(2,1)S(1)}, bf16[512,128]{1,0:T(8,128)(2,1)S(1)}, bf16[512,640]{1,0:T(8,128)(2,1)S(1)}, bf16[512,640]{1,0:T(8,128)(2,1)S(1)}) custom-call(f32[1024,320]{1,0:T(8,128)S(1)} %get-tuple-element.28.hidden_ref.after_ref, bf16[256,640]{1,0:T(8,128)(2,1)S(1)} %collective-permute-done.6.across_ref, ...), custom_call_target="tpu_custom_call" | custom-call | flops 1509949440 | bytes 1474560 | tf_op jit(solution)/shard_map/temporal/pallas_call | solution.py:325
  64.8 0.7 collective-permute-start.12
  65.7 0.5 collective-permute-start.9
  66.2 0.3 collective-permute-done.12.got_ref
  66.6 1.2 %collective-permute-start.13 = (bf16[512,128]{1,0:T(8,128)(2,1)S(1)}, bf16[512,128]{1,0:T(8,128)(2,1)S(1)}, u32[]{:S(2)}, u32[]{:S(2)}) collective-permute-start(bf16[512,128]{1,0:T(8,128)(2,1)S(1)} %chip_sum.7), channel_id=1, source_target_pairs={{0,2},{2,0},{1,3},{3,1},{4,6},{6,4},{5,7},{7,5},{8,10},{10,8},{9,1... | collective-permute-start | bytes 393224 | tf_op jit(solution)/shard_map/ppermute | solution.py:484
  67.8 0.5 mixed.1.after_ref.mixed_ref
  68.3 5.8 %collective-permute-done.11.in_ref = bf16[1024,256]{1,0:T(8,128)(2,1)S(1)} collective-permute-done((bf16[1024,256]{1,0:T(8,128)(2,1)S(1)}, bf16[1024,256]{1,0:T(8,128)(2,1)S(1)}, u32[]{:S(2)}, u32[]{:S(2)}) %collective-permute-start.11) | collective-permute-done | bytes 524320 | tf_op jit(solution)/shard_map/ppermute | solution.py:484
  74.1 2.8 %collective-permute-done.13.half_rest = bf16[512,128]{1,0:T(8,128)(2,1)S(1)} collective-permute-done((bf16[512,128]{1,0:T(8,128)(2,1)S(1)}, bf16[512,128]{1,0:T(8,128)(2,1)S(1)}, u32[]{:S(2)}, u32[]{:S(2)}) %collective-permute-start.13) | collective-permute-done | bytes 131104 | tf_op jit(solution)/shard_map/ppermute | solution.py:484
  76.9 1.2 %blend.1 = bf16[1024,320]{1,0:T(8,128)(2,1)} custom-call(f32[1]{0:T(128)S(6)} %copy.10.mix_ref, f32[1024,320]{1,0:T(8,128)S(1)} %mixed.1.after_ref.mixed_ref, bf16[1024,256]{1,0:T(8,128)(2,1)S(1)} %settle.3.half_first, bf16[512,128]{1,0:T(8,128)(2,1)S(1)} %collective-permute-done.13.half_rest), custom_call_target="tpu_custom_call" | custom-call | flops 1638400 | bytes 3276800 | tf_op jit(solution)/shard_map/blend/pallas_call | solution.py:453
  (19 shorter events, 0.4 us)
Async XLA Ops:
  4.3 5.1 %collective-permute-start = (bf16[1024,256]{1,0:T(8,128)(2,1)S(1)}, bf16[1024,256]{1,0:T(8,128)(2,1)S(1)}, u32[]{:S(2)}, u32[]{:S(2)}) collective-permute-start(bf16[1024,256]{1,0:T(8,128)(2,1)S(1)} %get-tuple-element.23), channel_id=1, source_target_pairs={{0,1},{1,0},{2,3},{3,2},{4,5},{5,4},{6,7},{7,6},{8,9},{9,8},{10,11... | collective-permute-start | bytes 1572872 | tf_op jit(solution)/shard_map/ppermute | solution.py:480
  9.6 15.1 %collective-permute-start.3 = (bf16[1024,256]{1,0:T(8,128)(2,1)S(1)}, bf16[1024,256]{1,0:T(8,128)(2,1)S(1)}, u32[]{:S(2)}, u32[]{:S(2)}) collective-permute-start(bf16[1024,256]{1,0:T(8,128)(2,1)S(1)} %chip_sum.4.after_ref), channel_id=1, source_target_pairs={{0,2},{2,0},{1,3},{3,1},{4,6},{6,4},{5,7},{7,5},{8,10},{10,8},{9,1... | collective-permute-start | bytes 1572872 | tf_op jit(solution)/shard_map/ppermute | solution.py:484
  19.3 1.4 %collective-permute-start.4 = (bf16[512,128]{1,0:T(8,128)(2,1)S(1)}, bf16[512,128]{1,0:T(8,128)(2,1)S(1)}, u32[]{:S(2)}, u32[]{:S(2)}) collective-permute-start(bf16[512,128]{1,0:T(8,128)(2,1)S(1)} %get-tuple-element.27), channel_id=1, source_target_pairs={{0,1},{1,0},{2,3},{3,2},{4,5},{5,4},{6,7},{7,6},{8,9},{9,8},{10,11... | collective-permute-start | bytes 393224 | tf_op jit(solution)/shard_map/ppermute | solution.py:480
  19.8 2.9 %collective-permute-start.2 = (bf16[256,640]{1,0:T(8,128)(2,1)S(1)}, bf16[256,640]{1,0:T(8,128)(2,1)S(1)}, u32[]{:S(2)}, u32[]{:S(2)}) collective-permute-start(bf16[256,640]{1,0:T(8,128)(2,1)S(1)} %get-tuple-element.41), channel_id=1, source_target_pairs={{0,1},{1,0},{2,3},{3,2},{4,5},{5,4},{6,7},{7,6},{8,9},{9,8},{10,11... | collective-permute-start | bytes 983048 | tf_op jit(solution)/shard_map/ppermute | solution.py:480
  20.3 2.4 %collective-permute-start.1 = (bf16[256,640]{1,0:T(8,128)(2,1)S(1)}, bf16[256,640]{1,0:T(8,128)(2,1)S(1)}, u32[]{:S(2)}, u32[]{:S(2)}) collective-permute-start(bf16[256,640]{1,0:T(8,128)(2,1)S(1)} %get-tuple-element.42), channel_id=1, source_target_pairs={{0,1},{1,0},{2,3},{3,2},{4,5},{5,4},{6,7},{7,6},{8,9},{9,8},{10,11... | collective-permute-start | bytes 983048 | tf_op jit(solution)/shard_map/ppermute | solution.py:480
  20.8 1.9 %copy-start = (bf16[2,320,16,32]{1,3,2,0:T(8,128)(2,1)S(1)}, bf16[2,320,16,32]{1,3,2,0:T(8,128)(2,1)}, u32[]{:S(2)}) copy-start(bf16[2,320,16,32]{1,3,2,0:T(8,128)(2,1)} %param.4) | copy-start | bytes 1966084
  20.8 6.4 %collective-permute-start.5 = (bf16[512,128]{1,0:T(8,128)(2,1)S(1)}, bf16[512,128]{1,0:T(8,128)(2,1)S(1)}, u32[]{:S(2)}, u32[]{:S(2)}) collective-permute-start(bf16[512,128]{1,0:T(8,128)(2,1)S(1)} %chip_sum.5), channel_id=1, source_target_pairs={{0,2},{2,0},{1,3},{3,1},{4,6},{6,4},{5,7},{7,5},{8,10},{10,8},{9,1... | collective-permute-start | bytes 393224 | tf_op jit(solution)/shard_map/ppermute | solution.py:484
  24.7 27.3 %copy-start.1 = (bf16[3,320,1280]{2,1,0:T(8,128)(2,1)S(1)}, bf16[3,320,1280]{2,1,0:T(8,128)(2,1)}, u32[]{:S(2)}) copy-start(bf16[3,320,1280]{2,1,0:T(8,128)(2,1)} %param.6) | copy-start | bytes 7372804
  28.2 23.7 %collective-permute-start.7 = (bf16[256,640]{1,0:T(8,128)(2,1)S(1)}, bf16[256,640]{1,0:T(8,128)(2,1)S(1)}, u32[]{:S(2)}, u32[]{:S(2)}) collective-permute-start(bf16[256,640]{1,0:T(8,128)(2,1)S(1)} %get-tuple-element.39), channel_id=1, source_target_pairs={{0,4},{8,12},{16,20},{24,28},{32,36},{40,44},{48,52},{56,60},{64,6... | collective-permute-start | bytes 983048 | tf_op jit(solution)/shard_map/ppermute | solution.py:527
  29.8 22.1 %collective-permute-start.6 = (bf16[256,640]{1,0:T(8,128)(2,1)S(1)}, bf16[256,640]{1,0:T(8,128)(2,1)S(1)}, u32[]{:S(2)}, u32[]{:S(2)}) collective-permute-start(bf16[256,640]{1,0:T(8,128)(2,1)S(1)} %get-tuple-element.40), channel_id=1, source_target_pairs={{4,8},{12,16},{20,24},{28,32},{36,40},{44,48},{52,56},{60,64},{68,... | collective-permute-start | bytes 983048 | tf_op jit(solution)/shard_map/ppermute | solution.py:527
  54.4 4.8 %collective-permute-start.8 = (bf16[1024,256]{1,0:T(8,128)(2,1)S(1)}, bf16[1024,256]{1,0:T(8,128)(2,1)S(1)}, u32[]{:S(2)}, u32[]{:S(2)}) collective-permute-start(bf16[1024,256]{1,0:T(8,128)(2,1)S(1)} %get-tuple-element.32), channel_id=1, source_target_pairs={{0,1},{1,0},{2,3},{3,2},{4,5},{5,4},{6,7},{7,6},{8,9},{9,8},{10,11... | collective-permute-start | bytes 1572872 | tf_op jit(solution)/shard_map/ppermute | solution.py:480
  59.3 14.7 %collective-permute-start.11 = (bf16[1024,256]{1,0:T(8,128)(2,1)S(1)}, bf16[1024,256]{1,0:T(8,128)(2,1)S(1)}, u32[]{:S(2)}, u32[]{:S(2)}) collective-permute-start(bf16[1024,256]{1,0:T(8,128)(2,1)S(1)} %chip_sum.6.after_ref), channel_id=1, source_target_pairs={{0,2},{2,0},{1,3},{3,1},{4,6},{6,4},{5,7},{7,5},{8,10},{10,8},{9,1... | collective-permute-start | bytes 1572872 | tf_op jit(solution)/shard_map/ppermute | solution.py:484
  64.8 1.7 %collective-permute-start.12 = (bf16[512,128]{1,0:T(8,128)(2,1)S(1)}, bf16[512,128]{1,0:T(8,128)(2,1)S(1)}, u32[]{:S(2)}, u32[]{:S(2)}) collective-permute-start(bf16[512,128]{1,0:T(8,128)(2,1)S(1)} %get-tuple-element.36), channel_id=1, source_target_pairs={{0,1},{1,0},{2,3},{3,2},{4,5},{5,4},{6,7},{7,6},{8,9},{9,8},{10,11... | collective-permute-start | bytes 393224 | tf_op jit(solution)/shard_map/ppermute | solution.py:480
  65.6 2.2 %collective-permute-start.10 = (bf16[256,640]{1,0:T(8,128)(2,1)S(1)}, bf16[256,640]{1,0:T(8,128)(2,1)S(1)}, u32[]{:S(2)}, u32[]{:S(2)}) collective-permute-start(bf16[256,640]{1,0:T(8,128)(2,1)S(1)} %get-tuple-element.37), channel_id=1, source_target_pairs={{0,1},{1,0},{2,3},{3,2},{4,5},{5,4},{6,7},{7,6},{8,9},{9,8},{10,11... | collective-permute-start | bytes 983048 | tf_op jit(solution)/shard_map/ppermute | solution.py:480
  65.7 2.1 %collective-permute-start.9 = (bf16[256,640]{1,0:T(8,128)(2,1)S(1)}, bf16[256,640]{1,0:T(8,128)(2,1)S(1)}, u32[]{:S(2)}, u32[]{:S(2)}) collective-permute-start(bf16[256,640]{1,0:T(8,128)(2,1)S(1)} %get-tuple-element.38), channel_id=1, source_target_pairs={{0,1},{1,0},{2,3},{3,2},{4,5},{5,4},{6,7},{7,6},{8,9},{9,8},{10,11... | collective-permute-start | bytes 983048 | tf_op jit(solution)/shard_map/ppermute | solution.py:480
  66.6 10.3 %collective-permute-start.13 = (bf16[512,128]{1,0:T(8,128)(2,1)S(1)}, bf16[512,128]{1,0:T(8,128)(2,1)S(1)}, u32[]{:S(2)}, u32[]{:S(2)}) collective-permute-start(bf16[512,128]{1,0:T(8,128)(2,1)S(1)} %chip_sum.7), channel_id=1, source_target_pairs={{0,2},{2,0},{1,3},{3,1},{4,6},{6,4},{5,7},{7,5},{8,10},{10,8},{9,1... | collective-permute-start | bytes 393224 | tf_op jit(solution)/shard_map/ppermute | solution.py:484

commit v7 on v6

--- a/solution.py
+++ b/solution.py
@@ -285,9 +285,7 @@
     )(lat, weight, after)
 
 
-def temporal_kernel(other, hidden_ref, across_ref, pair_ref, stats_ref, weight_hbm, after_ref, *refs):
-    *outs, weight_ref, taps_ref, total_ref, sems = refs
-    copies = copy_columns(other, weight_hbm, weight_ref, sems)
+def temporal_taps(hidden_ref, pair_ref, across_ref, stats_ref, taps_ref, copies):
     seq, size = lax.axis_index("seq"), lax.axis_size("seq")
     sums = jnp.sum(stats_ref[...], axis=0, keepdims=True) * (1.0 / (GROUP * 2 * PX * size))
     squares = pltpu.roll(jnp.broadcast_to(sums, (8, 128)), 128 - LOCAL_GROUPS, 1)[0:1]
@@ -314,19 +312,83 @@
     for copy in copies:
         copy.wait()
     put(halo(pair_ref, across_ref, seq == size - 1), (1, 2))
-    for frame in range(2):
-        total = jnp.dot(taps_ref[frame], weight_ref[0], preferred_element_type=F32)
-        store_sums(other, frame, total, outs, total_ref)
-
-
-def temporal_call(hidden, halos, stats, weight, after, other):
-    vmem = pl.BlockSpec(memory_space=pltpu.VMEM)
-    shapes, columns = part_shapes(other), part_columns(other)
-    return pl.pallas_call(
-        functools.partial(temporal_kernel, other),
-        in_specs=[vmem] * 4 + [pl.BlockSpec(memory_space=pl.ANY)] * 2,
-        out_specs=[vmem] * len(shapes),
-        out_shape=shapes,
+
+
+def temporal_sums(taps_ref, weight_ref, frame):
+    return jnp.dot(taps_ref[frame], weight_ref[0], preferred_element_type=F32)
+
+
+def temporal_send_kernel(*refs):
+    *inputs, weight_hbm, send_ref, taps_ref, own_weight_ref, weight_ref, sems, own_sems = refs
+    copies = start_copies([(first_columns(False), 0, FIRST)], weight_hbm, weight_ref, sems)
+    own_copies = start_copies([(first_columns(True), 0, FIRST)], weight_hbm, own_weight_ref, own_sems)
+    temporal_taps(*inputs, taps_ref, copies)
+    for frame in range(2):
+        send_ref[frame * PX : (frame + 1) * PX] = temporal_sums(taps_ref, weight_ref, frame).astype(BF16)
+    for copy in own_copies:
+        copy.wait()
+
+
+def temporal_own_kernel(taps_ref, weight_ref, own_ref):
+    for frame in range(2):
+        own_ref[frame * PX : (frame + 1) * PX] = temporal_sums(taps_ref, weight_ref, frame).astype(BF16)
+
+
+def temporal_rest_kernel(*refs):
+    *inputs, weight_hbm, after_ref = refs[:6]
+    *outs, weight_ref, taps_ref, total_ref, sems = refs[6:]
+    copies = copy_columns(False, weight_hbm, weight_ref, sems)
+    temporal_taps(*inputs, taps_ref, copies)
+    for frame in range(2):
+        store_sums(False, frame, temporal_sums(taps_ref, weight_ref, frame), outs, total_ref)
+
+
+def temporal_cost(columns):
+    return pl.CostEstimate(
+        flops=4 * PX * WIDE * columns,
+        bytes_accessed=2 * WIDE * columns,
+        transcendentals=4 * PX * LOCAL,
+    )
+
+
+def temporal_first(hidden, halos, stats, weight):
+    vmem, anywhere = pl.BlockSpec(memory_space=pltpu.VMEM), pl.BlockSpec(memory_space=pl.ANY)
+    sums = jax.ShapeDtypeStruct((2 * PX, FIRST), BF16)
+    columns = jax.ShapeDtypeStruct((1, WIDE, FIRST), BF16)
+    send, taps, own_weight = pl.pallas_call(
+        temporal_send_kernel,
+        in_specs=[vmem] * 4 + [anywhere],
+        out_specs=[vmem] * 3,
+        out_shape=[sums, jax.ShapeDtypeStruct((2, PX, WIDE), BF16), columns],
+        scratch_shapes=[
+            pltpu.VMEM(columns.shape, BF16),
+            pltpu.SemaphoreType.DMA((1, 1)),
+            pltpu.SemaphoreType.DMA((1, 1)),
+        ],
+        compiler_params=params(),
+        cost_estimate=temporal_cost(FIRST),
+        name="temporal_send",
+    )(hidden, *halos, stats, weight)
+    own = pl.pallas_call(
+        temporal_own_kernel,
+        in_specs=[vmem] * 2,
+        out_specs=vmem,
+        out_shape=sums,
+        compiler_params=params(),
+        cost_estimate=temporal_cost(FIRST),
+        name="temporal_own",
+    )(taps, own_weight)
+    return send, own
+
+
+def temporal_second(hidden, halos, stats, weight, after):
+    vmem, anywhere = pl.BlockSpec(memory_space=pltpu.VMEM), pl.BlockSpec(memory_space=pl.ANY)
+    columns = part_columns(False)
+    return pl.pallas_call(
+        temporal_rest_kernel,
+        in_specs=[vmem] * 4 + [anywhere] * 2,
+        out_specs=[vmem] * 4,
+        out_shape=part_shapes(False),
         scratch_shapes=[
             pltpu.VMEM((1, WIDE, columns), BF16),
             pltpu.VMEM((2, PX, WIDE), BF16),
@@ -334,13 +396,9 @@
             pltpu.SemaphoreType.DMA((1, 2)),
         ],
         compiler_params=params(),
-        cost_estimate=pl.CostEstimate(
-            flops=4 * PX * WIDE * columns,
-            bytes_accessed=2 * WIDE * columns,
-            transcendentals=4 * PX * LOCAL,
-        ),
-        name="temporal",
-    )(hidden, *halos[::-1], stats, weight, after)
+        cost_estimate=temporal_cost(columns),
+        name="temporal_rest",
+    )(hidden, *halos, stats, weight, after)
 
 
 def chip_sum_kernel(own_ref, got_ref, out_ref):
@@ -527,8 +585,8 @@
         halos.append(lax.ppermute(edge, "seq", pairs + [(b, a) for a, b in pairs]))
     stats = lax.all_to_all(stats, "seq", 0, 0, tiled=True)
     mixed, half_first, half_rest = reduce_channels(
-        lambda: temporal_call(hidden, halos, stats, weight_t, hidden, True),
-        lambda after: temporal_call(hidden, halos, stats, weight_t, after, False),
+        lambda: temporal_first(hidden, halos, stats, weight_t),
+        lambda after: temporal_second(hidden, halos, stats, weight_t, after),
         lambda own, cores: mix_call(mixed_kernel, mix_factor, F32, "mixed", hidden, own, *cores),
     )
     out = blend_call(mix_factor, mixed, half_first, half_rest)

time: 78.4 us -> 78.3 us (level)
  starting transfers between devices: 17.8 us -> 20.6 us
  blocking collectives: 21.4 us -> 19 us
    ppermute x2, starting transfers between devices: 2.3 us -> 5.17 us  [per_device(): halos.append(lax.ppermute(edge, 'seq', pairs + [(b, a) for a, b in pairs]))]
    all_to_all x1, blocking collectives: 21.4 us -> 19 us  [per_device(): stats = lax.all_to_all(stats, 'seq', 0, 0, tiled=True)]
    pallas_call x2 -> x3, Pallas kernels: 6.02 us -> 6.18 us  [the longest x1 3.54 us: temporal_second(): pl.pallas_call(temporal_rest_kernel, in_specs=[vmem] * 4 + [anywhere] * 2...]
  transfers between devices with their start and end apart: 14 -> 14, of which waited for: 7 -> 7; matrix products, arithmetic and copies ran while one was open for 0% -> 0% of each run, Pallas kernels for 19% -> 20%
where the time goes in v7:
time: 78.3 us; the launch traced here: 78.1 us
  Pallas kernels  24 us (31%)
  starting transfers between devices  20.6 us (26%)
  blocking collectives  19 us (24%)
  waiting for transfers between devices  13.3 us (17%)
  between operations  0.94 us (1%)
    all_to_all x1, blocking collectives, per_device(): stats = lax.all_to_all(stats, 'seq', 0, 0, tiled=True)  19 us
    ppermute x4, waiting for transfers between devices, to_half(): return lax.ppermute(array, 'ch', HALF_SWAP)  12.7 us
    ppermute x8, starting transfers between devices, to_core(): lax.ppermute(array[i * rows:(i + 1) * rows], 'ch', CORE_SWAP)  9.16 us
    pallas_call x1, Pallas kernels, spatial_second(): pl.pallas_call(spatial_rest_kernel, in_specs=[anywhere] * 3, out_specs=[v...  8.44 us
    ppermute x4, starting transfers between devices, to_half(): return lax.ppermute(array, 'ch', HALF_SWAP)  6.32 us
    ppermute x2, starting transfers between devices, per_device(): halos.append(lax.ppermute(edge, 'seq', pairs + [(b, a) for a, b in pairs]))  5.17 us
    pallas_call x1, Pallas kernels, spatial_first(): pl.pallas_call(spatial_send_kernel, in_specs=[anywhere] * 2, out_specs=[v...  4.33 us
    pallas_call x1, Pallas kernels, temporal_second(): pl.pallas_call(temporal_rest_kernel, in_specs=[vmem] * 4 + [anywhere] * 2...  3.54 us
  transfers between devices with their start and end apart: 14, of which 7 were waited for; matrix products, arithmetic and copies ran while one was open for 0% of the time, Pallas kernels for 20%

profile of v7, /device:TPU:1, one launch (start us, length us, event | category | flops | bytes accessed | tf_op | source)
XLA Modules:
  0.0 78.1 jit_solution(11276123664374072096)
XLA Ops:
  0.0 4.3 %spatial_send.1 = (bf16[1024,256]{1,0:T(8,128)(2,1)S(1)}, bf16[2,576,960]{2,1,0:T(8,128)(2,1)S(1)}, bf16[3,960,256]{2,1,0:T(8,128)(2,1)S(1)}) custom-call(bf16[1024,320]{1,0:T(8,128)(2,1)} %bitcast.12, bf16[3,960,1280]{2,1,0:T(8,128)(2,1)} %bitcast.20), custom_call_target="tpu_custom_call" | custom-call | flops 1509949440 | bytes 1474560 | tf_op jit(solution)/shard_map/spatial_send/pallas_call | solution.py:238
  4.3 3.3 %collective-permute-start = (bf16[1024,256]{1,0:T(8,128)(2,1)S(1)}, bf16[1024,256]{1,0:T(8,128)(2,1)S(1)}, u32[]{:S(2)}, u32[]{:S(2)}) collective-permute-start(bf16[1024,256]{1,0:T(8,128)(2,1)S(1)} %get-tuple-element.24), channel_id=1, source_target_pairs={{0,1},{1,0},{2,3},{3,2},{4,5},{5,4},{6,7},{7,6},{8,9},{9,8},{10,11... | collective-permute-start | bytes 1572872 | tf_op jit(solution)/shard_map/ppermute | solution.py:538
  7.7 1.8 %spatial_own.1.own_ref = bf16[1024,256]{1,0:T(8,128)(2,1)S(1)} custom-call(bf16[2,576,960]{2,1,0:T(8,128)(2,1)S(1)} %get-tuple-element.22.taps_ref, bf16[3,960,256]{2,1,0:T(8,128)(2,1)S(1)} %get-tuple-element.23.weight_ref), custom_call_target="tpu_custom_call" | custom-call | flops 1509949440 | bytes 1474560 | tf_op jit(solution)/shard_map/spatial_own/pallas_call | solution.py:254
  9.5 0.1 chip_sum.4.after_ref
  9.6 1.3 %collective-permute-start.3 = (bf16[1024,256]{1,0:T(8,128)(2,1)S(1)}, bf16[1024,256]{1,0:T(8,128)(2,1)S(1)}, u32[]{:S(2)}, u32[]{:S(2)}) collective-permute-start(bf16[1024,256]{1,0:T(8,128)(2,1)S(1)} %chip_sum.4.after_ref), channel_id=1, source_target_pairs={{0,2},{2,0},{1,3},{3,1},{4,6},{6,4},{5,7},{7,5},{8,10},{10,8},{9,1... | collective-permute-start | bytes 1572872 | tf_op jit(solution)/shard_map/ppermute | solution.py:542
  10.9 8.4 %spatial_rest.1 = (bf16[512,128]{1,0:T(8,128)(2,1)S(1)}, bf16[512,128]{1,0:T(8,128)(2,1)S(1)}, bf16[512,640]{1,0:T(8,128)(2,1)S(1)}, bf16[512,640]{1,0:T(8,128)(2,1)S(1)}) custom-call(bf16[1024,320]{1,0:T(8,128)(2,1)} %bitcast.13, bf16[3,960,1280]{2,1,0:T(8,128)(2,1)} %bitcast.21, bf16[1024,256]{1,0:T(8,128)(2,1)S(1)} %chip_sum.4.after_ref), custom_call_target="tpu_custom_call" | custom-call | flops 4529848320 | bytes 4423680 | tf_op jit(solution)/shard_map/spatial_rest/pallas_call | solution.py:269
  19.3 0.5 collective-permute-start.4
  19.8 0.4 collective-permute-start.2
  20.3 0.4 collective-permute-start.1
  20.6 0.1 collective-permute-done.4.got_ref
  20.8 1.9 %collective-permute-start.5 = (bf16[512,128]{1,0:T(8,128)(2,1)S(1)}, bf16[512,128]{1,0:T(8,128)(2,1)S(1)}, u32[]{:S(2)}, u32[]{:S(2)}) collective-permute-start(bf16[512,128]{1,0:T(8,128)(2,1)S(1)} %chip_sum.5), channel_id=1, source_target_pairs={{0,2},{2,0},{1,3},{3,1},{4,6},{6,4},{5,7},{7,5},{8,10},{10,8},{9,1... | collective-permute-start | bytes 393224 | tf_op jit(solution)/shard_map/ppermute | solution.py:542
  22.7 0.4 base.1.after_ref.base_ref
  23.1 1.5 %collective-permute-done.3.in_ref = bf16[1024,256]{1,0:T(8,128)(2,1)S(1)} collective-permute-done((bf16[1024,256]{1,0:T(8,128)(2,1)S(1)}, bf16[1024,256]{1,0:T(8,128)(2,1)S(1)}, u32[]{:S(2)}, u32[]{:S(2)}) %collective-permute-start.3) | collective-permute-done | bytes 524320 | tf_op jit(solution)/shard_map/ppermute | solution.py:542
  24.7 2.5 %collective-permute-done.5.half_rest = bf16[512,128]{1,0:T(8,128)(2,1)S(1)} collective-permute-done((bf16[512,128]{1,0:T(8,128)(2,1)S(1)}, bf16[512,128]{1,0:T(8,128)(2,1)S(1)}, u32[]{:S(2)}, u32[]{:S(2)}) %collective-permute-start.5) | collective-permute-done | bytes 131104 | tf_op jit(solution)/shard_map/ppermute | solution.py:542
  27.2 0.9 %hidden.1 = (f32[1024,320]{1,0:T(8,128)S(1)}, bf16[512,640]{1,0:T(8,128)(2,1)S(1)}, f32[64,128]{1,0:T(8,128)S(1)}) custom-call(f32[1024,320]{1,0:T(8,128)S(1)} %base.1.after_ref.base_ref, bf16[1024,256]{1,0:T(8,128)(2,1)S(1)} %settle.2.half_first, bf16[512,128]{1,0:T(8,128)(2,1)S(1)} %collective-permute-done.5.half_rest), custom_call_target="tpu_custom_call" | custom-call | flops 1638400 | bytes 3276800 | tf_op jit(solution)/shard_map/hidden/pallas_call | solution.py:473
  28.2 0.7 collective-permute-start.7
  28.9 4.5 %collective-permute-start.6 = (bf16[256,640]{1,0:T(8,128)(2,1)S(1)}, bf16[256,640]{1,0:T(8,128)(2,1)S(1)}, u32[]{:S(2)}, u32[]{:S(2)}) collective-permute-start(bf16[256,640]{1,0:T(8,128)(2,1)S(1)} %get-tuple-element.42), channel_id=1, source_target_pairs={{0,4},{8,12},{16,20},{24,28},{32,36},{40,44},{48,52},{56,60},{64,6... | collective-permute-start | bytes 983048 | tf_op jit(solution)/shard_map/ppermute | solution.py:585
  33.4 19.0 %all_to_all.11 = f32[64,1,128]{2,1,0:T(1,128)S(1)} all-to-all(f32[64,1,128]{2,1,0:T(1,128)S(1)} %bitcast.19), channel_id=1, replica_groups=mesh['seq'=64,'ch'=4] {'seq'}, dimensions={0} | all-to-all | bytes 65536 | tf_op jit(solution)/shard_map/all_to_all | solution.py:586
  52.4 1.9 %temporal_send.1 = (bf16[1024,256]{1,0:T(8,128)(2,1)S(1)}, bf16[2,512,960]{2,1,0:T(8,128)(2,1)S(1)}, bf16[1,960,256]{2,1,0:T(8,128)(2,1)S(1)}) custom-call(f32[1024,320]{1,0:T(8,128)S(1)} %get-tuple-element.29.refs_0_.hidden_ref, bf16[256,640]{1,0:T(8,128)(2,1)S(1)} %collective-permute-done.6.refs_1_, bf16[256,640]{1,0:T(8,128)(2,1)S(1)} %collective-permute-done.7.refs_2_, ...), custom_call_target="tpu_custom_call" | custom-call | flops 503316480 | bytes 491520 | tf_op jit(solution)/shard_map/temporal_send/pallas_call | solution.py:358
  54.3 3.3 %collective-permute-start.8 = (bf16[1024,256]{1,0:T(8,128)(2,1)S(1)}, bf16[1024,256]{1,0:T(8,128)(2,1)S(1)}, u32[]{:S(2)}, u32[]{:S(2)}) collective-permute-start(bf16[1024,256]{1,0:T(8,128)(2,1)S(1)} %get-tuple-element.34), channel_id=1, source_target_pairs={{0,1},{1,0},{2,3},{3,2},{4,5},{5,4},{6,7},{7,6},{8,9},{9,8},{10,11... | collective-permute-start | bytes 1572872 | tf_op jit(solution)/shard_map/ppermute | solution.py:538
  58.2 0.7 temporal_own.1.own_ref
  59.0 0.2 collective-permute-done.8.got_ref
  59.3 1.9 %collective-permute-start.11 = (bf16[1024,256]{1,0:T(8,128)(2,1)S(1)}, bf16[1024,256]{1,0:T(8,128)(2,1)S(1)}, u32[]{:S(2)}, u32[]{:S(2)}) collective-permute-start(bf16[1024,256]{1,0:T(8,128)(2,1)S(1)} %chip_sum.6.refs_5_), channel_id=1, source_target_pairs={{0,2},{2,0},{1,3},{3,1},{4,6},{6,4},{5,7},{7,5},{8,10},{10,8},{9,1... | collective-permute-start | bytes 1572872 | tf_op jit(solution)/shard_map/ppermute | solution.py:542
  61.2 3.5 %temporal_rest.1 = (bf16[512,128]{1,0:T(8,128)(2,1)S(1)}, bf16[512,128]{1,0:T(8,128)(2,1)S(1)}, bf16[512,640]{1,0:T(8,128)(2,1)S(1)}, bf16[512,640]{1,0:T(8,128)(2,1)S(1)}) custom-call(f32[1024,320]{1,0:T(8,128)S(1)} %get-tuple-element.29.refs_0_.hidden_ref, bf16[256,640]{1,0:T(8,128)(2,1)S(1)} %collective-permute-done.6.refs_1_, ...), custom_call_target="tpu_custom_call" | custom-call | flops 1509949440 | bytes 1474560 | tf_op jit(solution)/shard_map/temporal_rest/pallas_call | solution.py:387
  64.7 0.7 collective-permute-start.12
  65.6 0.5 collective-permute-start.9
  66.1 0.3 collective-permute-done.12.got_ref
  66.5 1.2 %collective-permute-start.13 = (bf16[512,128]{1,0:T(8,128)(2,1)S(1)}, bf16[512,128]{1,0:T(8,128)(2,1)S(1)}, u32[]{:S(2)}, u32[]{:S(2)}) collective-permute-start(bf16[512,128]{1,0:T(8,128)(2,1)S(1)} %chip_sum.7), channel_id=1, source_target_pairs={{0,2},{2,0},{1,3},{3,1},{4,6},{6,4},{5,7},{7,5},{8,10},{10,8},{9,1... | collective-permute-start | bytes 393224 | tf_op jit(solution)/shard_map/ppermute | solution.py:542
  67.7 0.5 mixed.1.after_ref.mixed_ref
  68.2 5.8 %collective-permute-done.11.in_ref = bf16[1024,256]{1,0:T(8,128)(2,1)S(1)} collective-permute-done((bf16[1024,256]{1,0:T(8,128)(2,1)S(1)}, bf16[1024,256]{1,0:T(8,128)(2,1)S(1)}, u32[]{:S(2)}, u32[]{:S(2)}) %collective-permute-start.11) | collective-permute-done | bytes 524320 | tf_op jit(solution)/shard_map/ppermute | solution.py:542
  74.0 2.8 %collective-permute-done.13.half_rest = bf16[512,128]{1,0:T(8,128)(2,1)S(1)} collective-permute-done((bf16[512,128]{1,0:T(8,128)(2,1)S(1)}, bf16[512,128]{1,0:T(8,128)(2,1)S(1)}, u32[]{:S(2)}, u32[]{:S(2)}) %collective-permute-start.13) | collective-permute-done | bytes 131104 | tf_op jit(solution)/shard_map/ppermute | solution.py:542
  76.8 1.2 %blend.1 = bf16[1024,320]{1,0:T(8,128)(2,1)} custom-call(f32[1]{0:T(128)S(6)} %copy.10.mix_ref, f32[1024,320]{1,0:T(8,128)S(1)} %mixed.1.after_ref.mixed_ref, bf16[1024,256]{1,0:T(8,128)(2,1)S(1)} %settle.3.half_first, bf16[512,128]{1,0:T(8,128)(2,1)S(1)} %collective-permute-done.13.half_rest), custom_call_target="tpu_custom_call" | custom-call | flops 1638400 | bytes 3276800 | tf_op jit(solution)/shard_map/blend/pallas_call | solution.py:511
  (20 shorter events, 0.5 us)
Async XLA Ops:
  4.3 5.1 %collective-permute-start = (bf16[1024,256]{1,0:T(8,128)(2,1)S(1)}, bf16[1024,256]{1,0:T(8,128)(2,1)S(1)}, u32[]{:S(2)}, u32[]{:S(2)}) collective-permute-start(bf16[1024,256]{1,0:T(8,128)(2,1)S(1)} %get-tuple-element.24), channel_id=1, source_target_pairs={{0,1},{1,0},{2,3},{3,2},{4,5},{5,4},{6,7},{7,6},{8,9},{9,8},{10,11... | collective-permute-start | bytes 1572872 | tf_op jit(solution)/shard_map/ppermute | solution.py:538
  9.6 15.1 %collective-permute-start.3 = (bf16[1024,256]{1,0:T(8,128)(2,1)S(1)}, bf16[1024,256]{1,0:T(8,128)(2,1)S(1)}, u32[]{:S(2)}, u32[]{:S(2)}) collective-permute-start(bf16[1024,256]{1,0:T(8,128)(2,1)S(1)} %chip_sum.4.after_ref), channel_id=1, source_target_pairs={{0,2},{2,0},{1,3},{3,1},{4,6},{6,4},{5,7},{7,5},{8,10},{10,8},{9,1... | collective-permute-start | bytes 1572872 | tf_op jit(solution)/shard_map/ppermute | solution.py:542
  19.3 1.4 %collective-permute-start.4 = (bf16[512,128]{1,0:T(8,128)(2,1)S(1)}, bf16[512,128]{1,0:T(8,128)(2,1)S(1)}, u32[]{:S(2)}, u32[]{:S(2)}) collective-permute-start(bf16[512,128]{1,0:T(8,128)(2,1)S(1)} %get-tuple-element.28), channel_id=1, source_target_pairs={{0,1},{1,0},{2,3},{3,2},{4,5},{5,4},{6,7},{7,6},{8,9},{9,8},{10,11... | collective-permute-start | bytes 393224 | tf_op jit(solution)/shard_map/ppermute | solution.py:538
  19.8 2.9 %collective-permute-start.2 = (bf16[256,640]{1,0:T(8,128)(2,1)S(1)}, bf16[256,640]{1,0:T(8,128)(2,1)S(1)}, u32[]{:S(2)}, u32[]{:S(2)}) collective-permute-start(bf16[256,640]{1,0:T(8,128)(2,1)S(1)} %get-tuple-element.43), channel_id=1, source_target_pairs={{0,1},{1,0},{2,3},{3,2},{4,5},{5,4},{6,7},{7,6},{8,9},{9,8},{10,11... | collective-permute-start | bytes 983048 | tf_op jit(solution)/shard_map/ppermute | solution.py:538
  20.3 2.4 %collective-permute-start.1 = (bf16[256,640]{1,0:T(8,128)(2,1)S(1)}, bf16[256,640]{1,0:T(8,128)(2,1)S(1)}, u32[]{:S(2)}, u32[]{:S(2)}) collective-permute-start(bf16[256,640]{1,0:T(8,128)(2,1)S(1)} %get-tuple-element.44), channel_id=1, source_target_pairs={{0,1},{1,0},{2,3},{3,2},{4,5},{5,4},{6,7},{7,6},{8,9},{9,8},{10,11... | collective-permute-start | bytes 983048 | tf_op jit(solution)/shard_map/ppermute | solution.py:538
  20.8 1.9 %copy-start = (bf16[2,320,16,32]{1,3,2,0:T(8,128)(2,1)S(1)}, bf16[2,320,16,32]{1,3,2,0:T(8,128)(2,1)}, u32[]{:S(2)}) copy-start(bf16[2,320,16,32]{1,3,2,0:T(8,128)(2,1)} %param.4) | copy-start | bytes 1966084
  20.8 6.4 %collective-permute-start.5 = (bf16[512,128]{1,0:T(8,128)(2,1)S(1)}, bf16[512,128]{1,0:T(8,128)(2,1)S(1)}, u32[]{:S(2)}, u32[]{:S(2)}) collective-permute-start(bf16[512,128]{1,0:T(8,128)(2,1)S(1)} %chip_sum.5), channel_id=1, source_target_pairs={{0,2},{2,0},{1,3},{3,1},{4,6},{6,4},{5,7},{7,5},{8,10},{10,8},{9,1... | collective-permute-start | bytes 393224 | tf_op jit(solution)/shard_map/ppermute | solution.py:542
  24.7 27.7 %copy-start.1 = (bf16[3,320,1280]{2,1,0:T(8,128)(2,1)S(1)}, bf16[3,320,1280]{2,1,0:T(8,128)(2,1)}, u32[]{:S(2)}) copy-start(bf16[3,320,1280]{2,1,0:T(8,128)(2,1)} %param.6) | copy-start | bytes 7372804
  28.2 24.2 %collective-permute-start.7 = (bf16[256,640]{1,0:T(8,128)(2,1)S(1)}, bf16[256,640]{1,0:T(8,128)(2,1)S(1)}, u32[]{:S(2)}, u32[]{:S(2)}) collective-permute-start(bf16[256,640]{1,0:T(8,128)(2,1)S(1)} %get-tuple-element.41), channel_id=1, source_target_pairs={{4,8},{12,16},{20,24},{28,32},{36,40},{44,48},{52,56},{60,64},{68,... | collective-permute-start | bytes 983048 | tf_op jit(solution)/shard_map/ppermute | solution.py:585
  28.9 23.5 %collective-permute-start.6 = (bf16[256,640]{1,0:T(8,128)(2,1)S(1)}, bf16[256,640]{1,0:T(8,128)(2,1)S(1)}, u32[]{:S(2)}, u32[]{:S(2)}) collective-permute-start(bf16[256,640]{1,0:T(8,128)(2,1)S(1)} %get-tuple-element.42), channel_id=1, source_target_pairs={{0,4},{8,12},{16,20},{24,28},{32,36},{40,44},{48,52},{56,60},{64,6... | collective-permute-start | bytes 983048 | tf_op jit(solution)/shard_map/ppermute | solution.py:585
  54.3 4.8 %collective-permute-start.8 = (bf16[1024,256]{1,0:T(8,128)(2,1)S(1)}, bf16[1024,256]{1,0:T(8,128)(2,1)S(1)}, u32[]{:S(2)}, u32[]{:S(2)}) collective-permute-start(bf16[1024,256]{1,0:T(8,128)(2,1)S(1)} %get-tuple-element.34), channel_id=1, source_target_pairs={{0,1},{1,0},{2,3},{3,2},{4,5},{5,4},{6,7},{7,6},{8,9},{9,8},{10,11... | collective-permute-start | bytes 1572872 | tf_op jit(solution)/shard_map/ppermute | solution.py:538
  59.3 14.7 %collective-permute-start.11 = (bf16[1024,256]{1,0:T(8,128)(2,1)S(1)}, bf16[1024,256]{1,0:T(8,128)(2,1)S(1)}, u32[]{:S(2)}, u32[]{:S(2)}) collective-permute-start(bf16[1024,256]{1,0:T(8,128)(2,1)S(1)} %chip_sum.6.refs_5_), channel_id=1, source_target_pairs={{0,2},{2,0},{1,3},{3,1},{4,6},{6,4},{5,7},{7,5},{8,10},{10,8},{9,1... | collective-permute-start | bytes 1572872 | tf_op jit(solution)/shard_map/ppermute | solution.py:542
  64.7 1.7 %collective-permute-start.12 = (bf16[512,128]{1,0:T(8,128)(2,1)S(1)}, bf16[512,128]{1,0:T(8,128)(2,1)S(1)}, u32[]{:S(2)}, u32[]{:S(2)}) collective-permute-start(bf16[512,128]{1,0:T(8,128)(2,1)S(1)} %get-tuple-element.38), channel_id=1, source_target_pairs={{0,1},{1,0},{2,3},{3,2},{4,5},{5,4},{6,7},{7,6},{8,9},{9,8},{10,11... | collective-permute-start | bytes 393224 | tf_op jit(solution)/shard_map/ppermute | solution.py:538
  65.5 2.2 %collective-permute-start.10 = (bf16[256,640]{1,0:T(8,128)(2,1)S(1)}, bf16[256,640]{1,0:T(8,128)(2,1)S(1)}, u32[]{:S(2)}, u32[]{:S(2)}) collective-permute-start(bf16[256,640]{1,0:T(8,128)(2,1)S(1)} %get-tuple-element.39), channel_id=1, source_target_pairs={{0,1},{1,0},{2,3},{3,2},{4,5},{5,4},{6,7},{7,6},{8,9},{9,8},{10,11... | collective-permute-start | bytes 983048 | tf_op jit(solution)/shard_map/ppermute | solution.py:538
  65.6 2.1 %collective-permute-start.9 = (bf16[256,640]{1,0:T(8,128)(2,1)S(1)}, bf16[256,640]{1,0:T(8,128)(2,1)S(1)}, u32[]{:S(2)}, u32[]{:S(2)}) collective-permute-start(bf16[256,640]{1,0:T(8,128)(2,1)S(1)} %get-tuple-element.40), channel_id=1, source_target_pairs={{0,1},{1,0},{2,3},{3,2},{4,5},{5,4},{6,7},{7,6},{8,9},{9,8},{10,11... | collective-permute-start | bytes 983048 | tf_op jit(solution)/shard_map/ppermute | solution.py:538
  66.5 10.3 %collective-permute-start.13 = (bf16[512,128]{1,0:T(8,128)(2,1)S(1)}, bf16[512,128]{1,0:T(8,128)(2,1)S(1)}, u32[]{:S(2)}, u32[]{:S(2)}) collective-permute-start(bf16[512,128]{1,0:T(8,128)(2,1)S(1)} %chip_sum.7), channel_id=1, source_target_pairs={{0,2},{2,0},{1,3},{3,1},{4,6},{6,4},{5,7},{7,5},{8,10},{10,8},{9,1... | collective-permute-start | bytes 393224 | tf_op jit(solution)/shard_map/ppermute | solution.py:542
